TPU v7x, 256 devices: a whole 4x4x8 slice. The times are simulated.
256 devices in a mesh: rot: 8 (over x, z_lo), rows: 32 (over z_hi, y, core).
Axes of the slice: x: 4, y: 4, z: 8 (z_hi: 4, z_lo: 2; z = z_hi * 2 + z_lo), core: 2. Of those that a mesh axis runs over, the one named last changes fastest.
Arguments:
- inputs: bfloat16 [512, 256, 128], P('rot', 'rows'), may hold values from -6 to 6
- cotangent: bfloat16 [512, 256, 128], P('rot', 'rows'), may hold values from -6 to 6
- filters: bfloat16 [16, 9, 32, 32], replicated, may hold values from -0.09375 to 0.09375
- bias: float32 [32], replicated, may hold values from -1 to 1
Outputs:
- input_grad: bfloat16 [512, 256, 128], P('rot', 'rows')
- filter_grad: float32 [16, 9, 32, 32], P('rot')
All inputs are finite; a program needn't handle non-finite values.
Results may differ from a plain program's by a relative error of at most 0.0049.
Values may be sent and summed in bfloat16 or wider, within the bound.
No kernel may reach another device: no remote copies, remote signals or barrier semaphores. Data moves between devices by JAX's collectives and lax.ppermute only.
A program may use at most 64 MiB of HBM per device.

v0:
```python
import jax
import jax.numpy as jnp
from jax import lax
from jax.sharding import PartitionSpec as P

CH = 32


def with_halo(shard, sides, width):
    for axis, dim in sides:
        peers, length = (lax.axis_size(axis), shard.shape[dim])
        up = [(i, (i + 1) % peers) for i in range(peers - 1)]
        down = [(j, i) for i, j in up]
        last = lax.slice_in_dim(shard, length - width, length, axis=dim)
        first = lax.slice_in_dim(shard, 0, width, axis=dim)
        before = lax.ppermute(last, axis, up)
        after = lax.ppermute(first, axis, down)
        shard = jnp.concatenate([before, shard, after], axis=dim)
    return shard


def pad_columns(block):
    return jnp.pad(block, ((0, 0), (0, 0), (1, 1)))


def forward_weights(filters, rot_out, rot_in):
    relative = (rot_in[None, :] - rot_out[:, None]) % filters.shape[0]
    taken = jnp.transpose(filters[relative], (2, 0, 3, 1, 4))
    return taken.reshape(9, rot_out.shape[0] * CH, rot_in.shape[0] * CH)


def backward_weights(filters, rot_in, rot_out):
    relative = (rot_in[:, None] - rot_out[None, :]) % filters.shape[0]
    taken = jnp.transpose(filters[relative], (2, 0, 4, 1, 3))
    return taken.reshape(9, rot_in.shape[0] * CH, rot_out.shape[0] * CH)


def one_hot(relative, rotations):
    return (relative.reshape(-1)[None, :] == jnp.arange(rotations)[:, None]).astype(jnp.float32)


def spread_taps(stacked, relative, rotations):
    table = one_hot(relative, rotations)
    return jnp.einsum("sk,tkm->stm", table, stacked, precision=lax.Precision.HIGHEST)


def shards(inputs, cotangent, filters, bias):
    local_ch, band, width = inputs.shape
    rotations = filters.shape[0]
    rot_local = local_ch // CH
    rot_mine = lax.axis_index("rot") * rot_local + jnp.arange(rot_local)
    in_halo = with_halo(inputs, (("rows", 1),), 1)
    empty = jnp.zeros((local_ch, band * width), jnp.float32)
    total = empty
    piece = lax.all_gather(in_halo, "rot", axis=0, tiled=True)
    count = piece.shape[0] // CH
    rot_in = jnp.arange(count)
    mats = forward_weights(filters, rot_mine, rot_in)
    padded = pad_columns(piece)
    for forward_tap_row in range(3):
        for forward_tap_col in range(3):
            window = padded[
                :,
                forward_tap_row : forward_tap_row + band,
                forward_tap_col : forward_tap_col + width,
            ].reshape(piece.shape[0], -1)
            total = total + jnp.dot(
                mats[3 * forward_tap_row + forward_tap_col],
                window,
                preferred_element_type=jnp.float32,
            )
    pre = total.reshape(local_ch, band, width) + jnp.tile(bias, rot_local)[:, None, None]
    sigma = jax.nn.sigmoid(pre)
    grad_pre = (cotangent.astype(jnp.float32) * sigma * (1.0 + pre * (1.0 - sigma))).astype(
        jnp.bfloat16
    )
    grad_halo = with_halo(grad_pre, (("rows", 1),), 1)
    filter_empty = jnp.zeros((rotations, 9, CH, CH), jnp.float32)
    grad_padded = pad_columns(grad_halo)
    grad_windows = [
        grad_padded[:, 2 - tap_row : 2 - tap_row + band, 2 - tap_col : 2 - tap_col + width].reshape(
            local_ch, -1
        )
        for tap_row in range(3)
        for tap_col in range(3)
    ]
    count = local_ch * lax.axis_size("rot")
    rot_in = jnp.arange(count // CH)
    mats = backward_weights(filters, rot_in, rot_mine)
    term = jnp.zeros((count, band * width), jnp.float32)
    for tap in range(9):
        term = term + jnp.dot(mats[tap], grad_windows[tap], preferred_element_type=jnp.float32)
    input_sum = lax.psum_scatter(
        term.reshape(count, band, width), "rot", scatter_dimension=0, tiled=True
    )
    grad_flat = grad_pre.reshape(local_ch, -1)
    piece = lax.all_gather(in_halo, "rot", axis=0, tiled=True)
    count = piece.shape[0] // CH
    rot_in = jnp.arange(count)
    relative = (rot_in[None, :] - rot_mine[:, None]) % rotations
    padded = pad_columns(piece)
    stacked = []
    for tap_row in range(3):
        for tap_col in range(3):
            window = padded[:, tap_row : tap_row + band, tap_col : tap_col + width].reshape(
                piece.shape[0], -1
            )
            product = lax.dot_general(
                grad_flat, window, (((1,), (1,)), ((), ())), preferred_element_type=jnp.float32
            )
            product = product.reshape(rot_local, CH, count, CH).transpose(0, 2, 1, 3)
            stacked.append(product.reshape(rot_local * count, CH * CH))
    added = spread_taps(jnp.stack(stacked), relative, rotations)
    filter_partial = added.reshape(filter_empty.shape)
    summed = lax.psum(filter_partial, "rows")
    share = lax.psum_scatter(summed, "rot", scatter_dimension=0, tiled=True)
    scale = float(rotations * band * lax.axis_size("rows") * width) ** (-0.5)
    return (input_sum.astype(jnp.bfloat16), share * scale)


def solution(mesh):
    return jax.shard_map(
        shards,
        mesh=mesh,
        in_specs=(P("rot", "rows", None), P("rot", "rows", None), P(), P()),
        out_specs=(P("rot", "rows", None), P("rot", None, None, None)),
        check_vma=False,
    )
```

profile of v0, /device:TPU:1, one launch (start us, length us, event | category | flops | bytes accessed | tf_op | source)
XLA Modules:
  0.0 538.6 jit_solution(5030257668946540419)
XLA Ops:
  8.3 4.6 collective-permute-start
  12.9 1.9 collective-permute-start.1
  14.8 3.1 collective-permute-done.1
  31.1 1.5 copy.95
  40.8 23.3 %all-gather.2.cloned.1.call-done = bf16[512,10,128]{2,0,1:T(8,128)(2,1)} async-done(((bf16[64,10,128]{2,0,1:T(8,128)(2,1)}), bf16[512,10,128]{2,0,1:T(8,128)(2,1)}) %all-gather.2.cloned.1.call-update) | async-done | bytes 1310736 | tf_op jit(solution)/shard_map/all_gather | solution.py:55
  64.1 1.6 copy.30
  65.7 3.8 pad_slice_fusion
  74.9 1.5 copy.42
  76.5 2.5 copy.36
  79.0 2.4 copy.37
  81.4 1.5 copy.39
  82.9 2.5 copy.40
  85.4 2.4 copy.41
  87.9 1.5 copy.38
  90.8 6.9 %collective-permute-start.3 = (bf16[64,1,128]{2,1,0:T(2,128)(2,1)}, bf16[64,1,128]{2,1,0:T(2,128)(2,1)}, u32[]{:S(2)}, u32[]{:S(2)}) collective-permute-start(bf16[64,1,128]{2,1,0:T(2,128)(2,1)} %get-tuple-element.37), channel_id=1, source_target_pairs={{1,0},{2,1},{3,2},{4,3},{5,4},{6,5},{7,6},{8,7},{9,8},{10,9},{11,1... | collective-permute-start | bytes 49160 | tf_op jit(solution)/shard_map/ppermute | solution.py:17
  97.7 3.1 collective-permute-start.2
  100.8 1.7 reshape.386
  102.5 1.8 convolution_bitcast_fusion
  105.6 2.4 reshape.380
  107.9 3.0 convolution_bitcast_fusion.6
  110.9 1.3 stack_reshape.29
  112.2 1.3 reshape.381
  113.5 2.3 convolution_bitcast_fusion.5
  116.7 2.4 reshape.383
  119.1 3.1 convolution_bitcast_fusion.3
  122.2 1.9 stack_reshape.32
  125.4 2.3 convolution_bitcast_fusion.2
  128.5 2.4 reshape.385
  130.9 3.1 convolution_bitcast_fusion.1
  134.0 1.9 stack_reshape.34
  137.2 2.3 convolution_bitcast_fusion.4
  140.9 1.9 convolution_bitcast_fusion.7
  146.4 1.6 copy.43
  149.3 1.3 fusion.6
  150.9 1.8 fusion.12
  153.6 1.8 fusion.9
  155.5 1.9 fusion.27
  157.3 1.8 fusion.15
  159.1 1.9 fusion.21
  161.0 1.8 fusion.24
  162.7 1.8 fusion.30
  164.5 41.5 %reduce-scatter.5.cloned.1.call-done = f32[2,9,32,32]{3,2,1,0:T(8,128)} async-done(((f32[16,9,32,32]{3,2,1,0:T(8,128)}), f32[2,9,32,32]{3,2,1,0:T(8,128)}) %reduce-scatter.5.cloned.1.call-update) | async-done | bytes 73744 | tf_op jit(solution)/shard_map/reduce_scatter | solution.py:116
  206.1 6.2 %add_bitcast_fusion = f32[64,8,8,128]{3,1,2,0:T(8,128)S(1)} fusion(f32[512,1024]{1,0:T(8,128)} %fusion.9, f32[512,1024]{1,0:T(8,128)} %fusion.12, f32[512,1024]{1,0:T(8,128)} %fusion.15, f32[512,1024]{1,0:T(8,128)S(1)} %fusion.18, f32[512,1024]{1,0:T(8,128)} %fusion.21, f32[512,1024]{1,0:T(8,128)} %fusion.24, f32[512,1024]{1,0:T(8,128)} %fusion.30, ...), kind=kOutput, calls=%fused_computation.4 | convolution fusion | flops 71303168 | bytes 19070976 | tf_op jit(solution)/shard_map/dot_general | solution.py:92
  212.2 1.8 copy.55
  214.1 259.9 %all-reduce.4.cloned.1.call-done = f32[2,9,32,32]{3,2,1,0:T(8,128)} async-done(((f32[2,9,32,32]{3,2,1,0:T(8,128)}), f32[2,9,32,32]{3,2,1,0:T(8,128)}) %all-reduce.4.cloned.1.call-update) | async-done | bytes 73744 | tf_op jit(solution)/shard_map/psum | solution.py:115
  473.9 1.7 broadcast_multiply_fusion
  475.6 54.8 %reduce-scatter.3.cloned.1.call-done = f32[64,8,128]{2,1,0:T(8,128)} async-done(((f32[512,8,128]{2,1,0:T(8,128)}), f32[64,8,128]{2,1,0:T(8,128)}) %reduce-scatter.3.cloned.1.call-update) | async-done | bytes 262160 | tf_op jit(solution)/shard_map/reduce_scatter | solution.py:93
  530.4 1.6 convert_element_type.17
  (170 shorter events, 41.9 us)
Async XLA Ops:
  7.2 12.7 %copy-start = (bf16[16,9,32,32]{3,2,1,0:T(8,128)(2,1)S(1)}, bf16[16,9,32,32]{3,2,1,0:T(8,128)(2,1)}, u32[]{:S(2)}) copy-start(bf16[16,9,32,32]{3,2,1,0:T(8,128)(2,1)} %param.6) | copy-start | bytes 884740
  7.2 56.9 %all-gather.2.cloned.1.call-start = ((), (), s32[]{:S(2)}) async-start(), calls=%async_computation.2 | async-start | bytes 1474560 | tf_op jit(solution)/shard_map/all_gather | solution.py:55
  8.3 6.5 %collective-permute-start = (bf16[64,1,128]{2,0,1:T(8,128)(2,1)S(1)}, bf16[64,1,128]{2,0,1:T(8,128)(2,1)S(1)}, u32[]{:S(2)}, u32[]{:S(2)}) collective-permute-start(bf16[64,1,128]{2,0,1:T(8,128)(2,1)S(1)} %get-tuple-element.39), channel_id=1, source_target_pairs={{0,1},{1,2},{2,3},{3,4},{4,5},{5,6},{6,7},{7,8},{8,9},{9,10},{10,1... | collective-permute-start | bytes 49160 | tf_op jit(solution)/shard_map/ppermute | solution.py:16
  12.9 5.1 collective-permute-start.1
  18.6 187.4 %reduce-scatter.5.cloned.1.call-start = ((), (), s32[]{:S(2)}) async-start(), calls=%async_computation.4 | async-start | bytes 2654208 | tf_op jit(solution)/shard_map/reduce_scatter | solution.py:116
  65.7 3.9 copy-start.37
  65.7 4.3 copy-start.36
  69.5 1.9 copy-start.2
  69.5 2.4 copy-start.6
  69.5 2.8 copy-start.5
  69.5 3.3 copy-start.4
  69.5 3.7 copy-start.8
  69.5 3.7 copy-start.9
  69.5 3.7 copy-start.10
  69.5 0.9 copy-start.35
  69.5 1.4 copy-start.34
  70.0 1.4 copy-start.33
  70.5 1.4 copy-start.32
  70.9 1.4 copy-start.31
  71.4 1.4 copy-start.30
  71.9 1.4 copy-start.29
  72.8 1.0 copy-start.38
  73.7 1.2 copy-start.11
  74.9 33.0 %copy-start.39 = (bf16[2,32,1024,1]{2,1,0,3:T(8,128)(2,1)}, bf16[2,32,1024,1]{2,1,0,3:T(8,128)(2,1)S(1)}, u32[]{:S(2)}) copy-start(bf16[2,32,1024,1]{2,1,0,3:T(8,128)(2,1)S(1)} %reshape.377) | copy-start | bytes 393220
  76.5 5.0 copy-start.7
  82.9 5.0 copy-start.3
  90.8 58.4 %collective-permute-start.3 = (bf16[64,1,128]{2,1,0:T(2,128)(2,1)}, bf16[64,1,128]{2,1,0:T(2,128)(2,1)}, u32[]{:S(2)}, u32[]{:S(2)}) collective-permute-start(bf16[64,1,128]{2,1,0:T(2,128)(2,1)} %get-tuple-element.37), channel_id=1, source_target_pairs={{1,0},{2,1},{3,2},{4,3},{5,4},{6,5},{7,6},{8,7},{9,8},{10,9},{11,1... | collective-permute-start | bytes 49160 | tf_op jit(solution)/shard_map/ppermute | solution.py:17
  97.7 51.6 %collective-permute-start.2 = (bf16[64,1,128]{2,1,0:T(2,128)(2,1)}, bf16[64,1,128]{2,1,0:T(2,128)(2,1)}, u32[]{:S(2)}, u32[]{:S(2)}) collective-permute-start(bf16[64,1,128]{2,1,0:T(2,128)(2,1)} %get-tuple-element.38), channel_id=1, source_target_pairs={{0,1},{1,2},{2,3},{3,4},{4,5},{5,6},{6,7},{7,8},{8,9},{9,10},{10,1... | collective-permute-start | bytes 49160 | tf_op jit(solution)/shard_map/ppermute | solution.py:16
  105.5 6.7 %copy-start.14 = (bf16[512,8,128]{2,1,0:T(8,128)(2,1)S(1)}, bf16[512,8,128]{2,1,0:T(8,128)(2,1)}, u32[]{:S(2)}) copy-start(bf16[512,8,128]{2,1,0:T(8,128)(2,1)} %copy.37) | copy-start | bytes 3145732
  116.7 7.4 %copy-start.13 = (bf16[512,8,128]{2,1,0:T(8,128)(2,1)S(1)}, bf16[512,8,128]{2,1,0:T(8,128)(2,1)}, u32[]{:S(2)}) copy-start(bf16[512,8,128]{2,1,0:T(8,128)(2,1)} %copy.40) | copy-start | bytes 3145732
  128.5 7.4 %copy-start.12 = (bf16[512,8,128]{2,1,0:T(8,128)(2,1)S(1)}, bf16[512,8,128]{2,1,0:T(8,128)(2,1)}, u32[]{:S(2)}) copy-start(bf16[512,8,128]{2,1,0:T(8,128)(2,1)} %copy.38) | copy-start | bytes 3145732
  140.8 2.7 copy-start.40
  143.6 1.3 copy-start.15
  143.6 1.4 copy-start.19
  143.6 1.4 copy-start.16
  143.6 1.4 copy-start.17
  143.6 1.4 copy-start.18
  148.0 325.9 %all-reduce.4.cloned.1.call-start = ((), (), s32[]{:S(2)}) async-start(), calls=%async_computation.5 | async-start | bytes 589824 | tf_op jit(solution)/shard_map/psum | solution.py:115
  148.8 2.1 copy-start.27
  150.6 3.0 copy-start.25
  150.9 4.5 copy-start.26
  153.6 3.7 copy-start.21
  155.5 3.6 copy-start.23
  157.3 3.7 copy-start.22
  159.1 3.6 copy-start.24
  161.0 45.1 %copy-start.20 = (bf16[512,64]{0,1:T(8,128)(2,1)S(1)}, bf16[512,64]{0,1:T(8,128)(2,1)}, u32[]{:S(2)}) copy-start(bf16[512,64]{0,1:T(8,128)(2,1)} %squeeze.71) | copy-start | bytes 196612
  206.0 324.4 %reduce-scatter.3.cloned.1.call-start = ((), (), s32[]{:S(2)}) async-start(), calls=%async_computation.3 | async-start | bytes 2359296 | tf_op jit(solution)/shard_map/reduce_scatter | solution.py:93
  212.2 319.8 %copy-start.1 = (bf16[16,9,32,32]{3,2,1,0:T(8,128)(2,1)S(1)}, bf16[16,9,32,32]{3,2,1,0:T(8,128)(2,1)}, u32[]{:S(2)}) copy-start(bf16[16,9,32,32]{3,2,1,0:T(8,128)(2,1)} %param.6) | copy-start | bytes 884740
  (1 other events, 0.8 us)
Sparse Core Ops, SparseCore 0:
  18.7 45.2 all-gather.1
  148.1 57.8 reduce-scatter.4
  208.6 265.2 all-reduce.3
  476.5 53.8 reduce-scatter.2
where the time goes:
time: 540 us; the launch traced here: 539 us
  waiting for transfers between devices  383 us (71%)
  local copies, waits for them, and re-layouts  73.6 us (14%)
  matrix products  44.4 us (8%)
  starting transfers between devices  16.8 us (3%)
  between operations  14.6 us (3%)
  other arithmetic  6.58 us (1%)
    psum x1, waiting for transfers between devices, shards(): summed = lax.psum(filter_partial, 'rows')  260 us
    reduce_scatter x1, waiting for transfers between devices, shards(): lax.psum_scatter(term.reshape(count, band, width), 'rot', scatter_dimensi...  54.8 us
    reduce_scatter x1, waiting for transfers between devices, shards(): share = lax.psum_scatter(summed, 'rot', scatter_dimension=0, tiled=True)  41.5 us
    all_gather x1, waiting for transfers between devices, shards(): piece = lax.all_gather(in_halo, 'rot', axis=0, tiled=True)  23.3 us
    dot_general x9, matrix products, shards(): lax.dot_general(grad_flat, window, (((1,), (1,)), ((), ())), preferred_el...  20.7 us
    slice x10, local copies, waits for them, and re-layouts, shards(): padded[:, forward_tap_row:forward_tap_row + band, forward_tap_col:forward...  19.6 us
    dot_general x9, matrix products, shards(): jnp.dot(mats[tap], grad_windows[tap], preferred_element_type=jnp.float32)  19.2 us
    dot_general x10, local copies, waits for them, and re-layouts, shards(): lax.dot_general(grad_flat, window, (((1,), (1,)), ((), ())), preferred_el...  13.7 us
  transfers between devices with their start and end apart: 8, of which 5 were waited for; matrix products, arithmetic and copies ran while one was open for 17% of the time, Pallas kernels for 0%

commit v1 on v0

v1 whole, which is shorter than its diff:
```python
import jax
import jax.numpy as jnp
from jax import lax
from jax.experimental import pallas as pl
from jax.experimental.pallas import tpu as pltpu
from jax.sharding import PartitionSpec as P

CH = 32
F32 = jnp.float32
BF16 = jnp.bfloat16


def weight_kernel(fwd_ref, bwd_ref, w_ref, wt_ref):
    for src, dst in ((fwd_ref, w_ref), (bwd_ref, wt_ref)):
        for a in range(3):
            for b in range(3):
                v = src[3 * a + b]
                n = v.shape[1]
                for fine in range(4):
                    t = v
                    if fine:
                        cut = n - CH * fine
                        t = jnp.concatenate([v[:, cut:], v[:, :cut]], axis=1)
                    for coarse in range(n // 128):
                        u = t
                        if coarse:
                            cut = n - 128 * coarse
                            u = jnp.concatenate([t[:, cut:], t[:, :cut]], axis=1)
                        row = b * n + CH * (4 * coarse + fine)
                        dst[row : row + CH, a * n : (a + 1) * n] = u


def shift_right(v):
    lane = lax.broadcasted_iota(jnp.int32, v.shape, 1)
    return jnp.where(lane == 0, 0.0, pltpu.roll(v, 1, 1))


def shift_left(v):
    lane = lax.broadcasted_iota(jnp.int32, v.shape, 1)
    n = v.shape[1]
    return jnp.where(lane == n - 1, 0.0, pltpu.roll(v, n - 1, 1))


def grad_kernel(recv_ref, above_ref, below_ref, w_ref, bias_ref, g_ref, fg_ref, x2_ref):
    groups, two, width = recv_ref.shape
    half = two // 2
    n = groups * half
    rot = n // CH
    x0 = recv_ref[:, :half, :].reshape(n, width)
    cot = recv_ref[:, half:, :].reshape(n, width)
    rows = (above_ref[...], x0, below_ref[...])
    x3 = jnp.concatenate(rows, axis=0)
    for a in range(3):
        x = rows[a]
        turned = jnp.concatenate([x[CH:], x[:CH]], axis=0)
        for rep in range(2):
            x2_ref[a, rep * n : (rep + 1) * n, :width] = x
            x2_ref[a, rep * n : (rep + 1) * n, width:] = turned
    parts = [
        jnp.dot(w_ref[b * n : (b + 1) * n, :], x3, preferred_element_type=F32) for b in range(3)
    ]
    bias = jnp.concatenate([bias_ref[...]] * rot, axis=0)
    pre = parts[1] + shift_right(parts[0]) + shift_left(parts[2]) + bias
    sigma = jax.nn.sigmoid(pre)
    grad = cot.astype(F32) * sigma * (1.0 + pre * (1.0 - sigma))
    own = grad.astype(BF16)
    g_ref[...] = own
    taps = (shift_left(grad).astype(BF16), own, shift_right(grad).astype(BF16))
    blank = jnp.zeros((CH, width), BF16)
    total = [None] * 3
    for p in range(rot // 2):
        sides = []
        for r in (2 * p, 2 * p + 1):
            sides.append(jnp.concatenate([t[CH * r : CH * (r + 1)] for t in taps] + [blank], axis=0))
        g2 = jnp.concatenate(sides, axis=1)
        for a in range(3):
            x = x2_ref[a, 2 * CH * p : 2 * CH * p + n, :]
            d = lax.dot_general(x, g2, (((1,), (1,)), ((), ())), preferred_element_type=F32)
            total[a] = d if total[a] is None else total[a] + d
    for a in range(3):
        fg_ref[:, a] = total[a].reshape(groups, half, 4 * CH)


def input_kernel(above_ref, own_ref, below_ref, wt_ref, out_ref):
    n = own_ref.shape[0]
    g3 = jnp.concatenate([below_ref[...], own_ref[...], above_ref[...]], axis=0)
    parts = [
        jnp.dot(wt_ref[b * n : (b + 1) * n, :], g3, preferred_element_type=F32) for b in range(3)
    ]
    out = parts[1] + shift_left(parts[0]) + shift_right(parts[2])
    out_ref[...] = out.astype(BF16)


LIMIT = pltpu.CompilerParams(vmem_limit_bytes=48 * 1024 * 1024)


def call(kernel, outs, flops, scratch=()):
    return pl.pallas_call(
        kernel,
        out_shape=outs,
        scratch_shapes=list(scratch),
        compiler_params=LIMIT,
        cost_estimate=pl.CostEstimate(flops=flops, bytes_accessed=6_000_000, transcendentals=0),
    )


def shaped(shape, dtype):
    return jax.ShapeDtypeStruct(shape, dtype)


def shards(inputs, cotangent, filters, bias):
    local_ch, band, width = inputs.shape
    rotations, taps = filters.shape[:2]
    n = rotations * CH
    groups = lax.axis_size("rot")
    bands = lax.axis_size("rows")
    total = groups * bands

    with jax.named_scope("to_rows"):
        packed = jnp.concatenate(
            [jnp.transpose(inputs, (1, 0, 2)), jnp.transpose(cotangent, (1, 0, 2))], axis=1
        )
        recv = lax.all_to_all(packed, "rot", 0, 0, tiled=True)
    with jax.named_scope("weights"):
        fwd = jnp.transpose(filters, (1, 2, 0, 3)).reshape(taps, CH, n)
        back = filters[(-jnp.arange(rotations)) % rotations]
        bwd = jnp.transpose(back, (1, 3, 0, 2)).reshape(taps, CH, n)
        w, wt = call(weight_kernel, (shaped((3 * n, 3 * n), BF16),) * 2, 1000)(fwd, bwd)
        bias2 = jnp.broadcast_to(bias[:, None], (CH, width))

    order = ("rot", "rows")

    def place(row):
        return (row % groups) * bands + row // groups

    up = [(place(i), place(i + 1)) for i in range(total - 1)]
    down = [(j, i) for i, j in up]
    with jax.named_scope("input_rows"):
        own = recv[:, :local_ch].reshape(n, width)
        above = lax.ppermute(own, order, up)
        below = lax.ppermute(own, order, down)
    with jax.named_scope("grad"):
        g, part = call(
            grad_kernel,
            (shaped((n, width), BF16), shaped((groups, 3, local_ch, 4 * CH), F32)),
            2 * 18 * n * n * width,
            [pltpu.VMEM((3, 2 * n, 2 * width), BF16)],
        )(recv, above, below, w, bias2)
    with jax.named_scope("filter_rot"):
        got = lax.all_to_all(part.reshape(groups, 3 * local_ch, 4 * CH), "rot", 0, 0, tiled=True)
        mine = jnp.sum(got, axis=0).reshape(3, 2, CH, 4 * CH)
    with jax.named_scope("grad_rows"):
        g_above = lax.ppermute(g, order, up)
        g_below = lax.ppermute(g, order, down)
    with jax.named_scope("input_grad"):
        dx = call(input_kernel, shaped((n, width), BF16), 2 * 9 * n * n * width)(
            g_above, g, g_below, wt
        )
        dx = lax.all_to_all(dx.reshape(groups, local_ch, width), "rot", 0, 0, tiled=True)
        input_grad = jnp.transpose(dx, (1, 0, 2))

    core = lax.axis_index("rows") % 2
    swap = [(i, i ^ 1) for i in range(bands)]

    def turns(step, count):
        perms = []
        for s in range(1, count):
            perms.append([(i, i + ((i // step + s) % count - i // step % count) * step) for i in range(bands)])
        return perms

    def add_four(v, step):
        p1, p2, p3 = [lax.ppermute(v, "rows", perm) for perm in turns(step, 4)]
        return (v + p2) + (p1 + p3)

    with jax.named_scope("filter_core"):
        keep = lax.dynamic_index_in_dim(mine, core, 1, keepdims=False)
        give = lax.dynamic_index_in_dim(mine, 1 - core, 1, keepdims=False)
        v = keep + lax.ppermute(give, "rows", swap)
    with jax.named_scope("filter_y"):
        v = add_four(v, 2)
    with jax.named_scope("filter_z"):
        v = add_four(v, 8)
    with jax.named_scope("filter_out"):
        scale = float(rotations * band * bands * width) ** (-0.5)
        v = v * scale
        other = lax.ppermute(v, "rows", swap)
        both = jnp.where(core == 0, jnp.stack([v, other]), jnp.stack([other, v]))
        both = both[..., : 3 * CH].reshape(2, 3, CH, 3, CH)
        filter_grad = jnp.transpose(both, (0, 1, 3, 4, 2)).reshape(2, taps, CH, CH)
    return input_grad, filter_grad


def solution(mesh):
    return jax.shard_map(
        shards,
        mesh=mesh,
        in_specs=(P("rot", "rows", None), P("rot", "rows", None), P(), P()),
        out_specs=(P("rot", "rows", None), P("rot", None, None, None)),
        check_vma=False,
    )
```

time: 540 us -> 95 us (0.18)
  the two profiles are of different devices: /device:TPU:1 before, /device:TPU:2 now
where the time goes in v1:
time: 95 us; the launch traced here: 94.6 us
  starting transfers between devices  43.2 us (45%)
  waiting for transfers between devices  18.2 us (19%)
  blocking collectives  11.7 us (12%)
  local copies, waits for them, and re-layouts  10.4 us (11%)
  Pallas kernels  9.97 us (10%)
    ppermute x6, starting transfers between devices, add_four(): p1, p2, p3 = [lax.ppermute(v, 'rows', perm) for perm in turns(step, 4)]  15.9 us
    all_to_all x1, waiting for transfers between devices, shards(): lax.all_to_all(part.reshape(groups, 3 * local_ch, 4 * CH), 'rot', 0, 0, t...  12.1 us
    all_to_all x1, blocking collectives, shards(): recv = lax.all_to_all(packed, 'rot', 0, 0, tiled=True)  11.7 us
    all_to_all x1, starting transfers between devices, shards(): lax.all_to_all(dx.reshape(groups, local_ch, width), 'rot', 0, 0, tiled=True)  9.69 us
    pallas_call x1, Pallas kernels, shards(): call(grad_kernel, (shaped((n, width), BF16), shaped((groups, 3, local_ch,...  5.14 us
    all_to_all x1, waiting for transfers between devices, shards(): lax.all_to_all(dx.reshape(groups, local_ch, width), 'rot', 0, 0, tiled=True)  4.95 us
    all_to_all x1, starting transfers between devices, shards(): lax.all_to_all(part.reshape(groups, 3 * local_ch, 4 * CH), 'rot', 0, 0, t...  3.91 us
    ppermute x1, starting transfers between devices, shards(): below = lax.ppermute(own, order, down)  3.91 us
  transfers between devices with their start and end apart: 14, of which 3 were waited for; matrix products, arithmetic and copies ran while one was open for 6% of the time, Pallas kernels for 5%

profile of v1, /device:TPU:2, one launch (start us, length us, event | category | flops | bytes accessed | tf_op | source)
XLA Modules:
  0.0 94.6 jit_solution(16728944001805902561)
XLA Ops:
  0.6 0.0 copy-start.1
  0.6 1.1 %copy_bitcast_fusion = (bf16[8,64,128]{2,1,0:T(8,128)(2,1)S(1)}, bf16[8,64,128]{2,1,0:T(8,128)(2,1)S(1)}) fusion(bf16[64,8,128]{2,1,0:T(8,128)(2,1)} %param.5, bf16[64,8,128]{2,1,0:T(8,128)(2,1)} %param.4), kind=kLoop, calls=%fused_computation.2 | loop fusion | bytes 524288 | tf_op jit(solution)/shard_map/to_rows/transpose | solution.py:121
  1.8 11.7 %all_to_all.15.recv_ref = bf16[8,128,128]{2,1,0:T(8,128)(2,1)S(1)} all-to-all(bf16[8,128,128]{2,1,0:T(8,128)(2,1)S(1)} %pad_maximum_fusion), channel_id=1, replica_groups=mesh['rot'=8,'rows'=32] {'rot'}, dimensions={0} | all-to-all | bytes 524288 | tf_op jit(solution)/shard_map/to_rows/all_to_all | solution.py:123
  13.5 0.7 slice.10
  14.2 2.8 %collective-permute-start = (bf16[512,128]{1,0:T(8,128)(2,1)}, bf16[512,128]{1,0:T(8,128)(2,1)S(1)}, u32[]{:S(2)}, u32[]{:S(2)}) collective-permute-start(bf16[512,128]{1,0:T(8,128)(2,1)} %bitcast.2), channel_id=1, source_target_pairs={{0,32},{32,64},{64,96},{96,128},{128,160},{160,192},{192,224},{224... | collective-permute-start | bytes 393224 | tf_op jit(solution)/shard_map/input_rows/ppermute | solution.py:140
  17.0 3.9 %collective-permute-start.1 = (bf16[512,128]{1,0:T(8,128)(2,1)}, bf16[512,128]{1,0:T(8,128)(2,1)S(1)}, u32[]{:S(2)}, u32[]{:S(2)}) collective-permute-start(bf16[512,128]{1,0:T(8,128)(2,1)} %bitcast.2), channel_id=1, source_target_pairs={{32,0},{64,32},{96,64},{128,96},{160,128},{192,160},{224,192},{1,2... | collective-permute-start | bytes 393224 | tf_op jit(solution)/shard_map/input_rows/ppermute | solution.py:141
  20.9 0.0 copy-done.1
  21.0 0.5 copy.29
  21.4 1.1 %reshape.79.fwd_ref = bf16[9,32,512]{2,1,0:T(8,128)(2,1)S(1)} reshape(bf16[9,32,16,32]{3,2,1,0:T(8,128)(2,1)S(1)} %copy.29) | data formatting | bytes 589824 | tf_op jit(solution)/shard_map/weights/reshape | solution.py:125
  22.6 0.8 gather_fusion
  23.4 0.9 copy.30
  24.3 0.0 copy-start.2
  24.3 1.1 %reshape.80.bwd_ref = bf16[9,32,512]{2,1,0:T(8,128)(2,1)S(1)} reshape(bf16[9,32,16,32]{3,2,1,0:T(8,128)(2,1)S(1)} %copy.30) | data formatting | bytes 589824 | tf_op jit(solution)/shard_map/weights/reshape | solution.py:127
  25.4 2.8 %weights.1 = (bf16[1536,1536]{1,0:T(8,128)(2,1)S(1)}, bf16[1536,1536]{1,0:T(8,128)(2,1)}) custom-call(bf16[9,32,512]{2,1,0:T(8,128)(2,1)S(1)} %reshape.79.fwd_ref, bf16[9,32,512]{2,1,0:T(8,128)(2,1)S(1)} %reshape.80.bwd_ref), custom_call_target="tpu_custom_call" | custom-call | flops 1000 | bytes 6000000 | tf_op jit(solution)/shard_map/weights/pallas_call | solution.py:128
  28.2 0.0 collective-permute-done.above_ref
  28.2 0.0 collective-permute-done.1.below_ref
  28.2 0.0 copy-done.2
  28.2 0.1 broadcast_in_dim.2.bias_ref
  28.3 5.1 %grad.1 = (bf16[512,128]{1,0:T(8,128)(2,1)S(1)}, f32[8,3,64,128]{3,2,1,0:T(8,128)}) custom-call(bf16[8,128,128]{2,1,0:T(8,128)(2,1)S(1)} %all_to_all.15.recv_ref, bf16[512,128]{1,0:T(8,128)(2,1)S(1)} %collective-permute-done.above_ref, bf16[512,128]{1,0:T(8,128)(2,1)S(1)} %collective-permute-done.1.below_ref, bf16[1536,1536]{1,0:T(8,128)(2,1)S(1)} %get-tuple-element.6.w_ref, ...), custom_call_target="tpu_custom_call" | custom-call | flops 1207959552 | bytes 6000000 | tf_op jit(solution)/shard_map/grad/pallas_call | solution.py:143
  33.5 3.9 %all-to-all-start.2 = ((f32[8,192,128]{2,1,0:T(8,128)}), f32[8,192,128]{2,1,0:T(8,128)S(1)}, u32[]{:S(2)}, u32[]{:S(2)}) async-start(f32[8,192,128]{2,1,0:T(8,128)} %bitcast.8), calls=%async_computation.2 | async-start | bytes 1572864 | tf_op jit(solution)/shard_map/filter_rot/all_to_all | solution.py:150
  37.4 12.1 %all-to-all-done.2 = f32[8,192,128]{2,1,0:T(8,128)S(1)} async-done(((f32[8,192,128]{2,1,0:T(8,128)}), f32[8,192,128]{2,1,0:T(8,128)S(1)}, u32[]{:S(2)}, u32[]{:S(2)}) %all-to-all-start.2) | async-done | bytes 786464 | tf_op jit(solution)/shard_map/filter_rot/all_to_all | solution.py:150
  49.6 0.2 collective-permute-start.4
  49.8 1.1 %collective-permute-done.4 = f32[3,32,128]{2,1,0:T(8,128)S(1)} collective-permute-done((f32[3,32,128]{2,1,0:T(8,128)S(1)}, f32[3,32,128]{2,1,0:T(8,128)S(1)}, u32[]{:S(2)}, u32[]{:S(2)}) %collective-permute-start.4) | collective-permute-done | bytes 49184 | tf_op jit(solution)/shard_map/filter_core/ppermute | solution.py:178
  50.9 2.0 %collective-permute-start.6 = (f32[3,32,128]{2,1,0:T(8,128)S(1)}, f32[3,32,128]{2,1,0:T(8,128)S(1)}, u32[]{:S(2)}, u32[]{:S(2)}) collective-permute-start(f32[3,32,128]{2,1,0:T(8,128)S(1)} %bitcast_add_fusion), channel_id=1, source_target_pairs={{0,2},{1,3},{2,4},{3,5},{4,6},{5,7},{6,0},{7,1},{8,10},{9,11},{10,... | collective-permute-start | bytes 147464 | tf_op jit(solution)/shard_map/filter_y/ppermute | solution.py:172
  52.9 3.2 %collective-permute-start.7 = (f32[3,32,128]{2,1,0:T(8,128)S(1)}, f32[3,32,128]{2,1,0:T(8,128)S(1)}, u32[]{:S(2)}, u32[]{:S(2)}) collective-permute-start(f32[3,32,128]{2,1,0:T(8,128)S(1)} %bitcast_add_fusion), channel_id=1, source_target_pairs={{0,6},{1,7},{2,0},{3,1},{4,2},{5,3},{6,4},{7,5},{8,14},{9,15},{10,... | collective-permute-start | bytes 147464 | tf_op jit(solution)/shard_map/filter_y/ppermute | solution.py:172
  56.1 1.4 %collective-permute-start.5 = (f32[3,32,128]{2,1,0:T(8,128)S(1)}, f32[3,32,128]{2,1,0:T(8,128)S(1)}, u32[]{:S(2)}, u32[]{:S(2)}) collective-permute-start(f32[3,32,128]{2,1,0:T(8,128)S(1)} %bitcast_add_fusion), channel_id=1, source_target_pairs={{0,4},{1,5},{2,6},{3,7},{4,0},{5,1},{6,2},{7,3},{8,12},{9,13},{10,... | collective-permute-start | bytes 147464 | tf_op jit(solution)/shard_map/filter_y/ppermute | solution.py:172
  57.5 3.4 %collective-permute-start.2 = (bf16[512,128]{1,0:T(8,128)(2,1)S(1)}, bf16[512,128]{1,0:T(8,128)(2,1)S(1)}, u32[]{:S(2)}, u32[]{:S(2)}) collective-permute-start(bf16[512,128]{1,0:T(8,128)(2,1)S(1)} %get-tuple-element.7.own_ref), channel_id=1, source_target_pairs={{0,32},{32,64},{64,96},{96,128},{128,160},{160,192},{192,224},{224... | collective-permute-start | bytes 393224 | tf_op jit(solution)/shard_map/grad_rows/ppermute | solution.py:153
  60.9 3.4 %collective-permute-start.3 = (bf16[512,128]{1,0:T(8,128)(2,1)S(1)}, bf16[512,128]{1,0:T(8,128)(2,1)S(1)}, u32[]{:S(2)}, u32[]{:S(2)}) collective-permute-start(bf16[512,128]{1,0:T(8,128)(2,1)S(1)} %get-tuple-element.7.own_ref), channel_id=1, source_target_pairs={{32,0},{64,32},{96,64},{128,96},{160,128},{192,160},{224,192},{1,2... | collective-permute-start | bytes 393224 | tf_op jit(solution)/shard_map/grad_rows/ppermute | solution.py:154
  64.2 0.0 collective-permute-done.6
  64.2 0.0 collective-permute-done.7
  64.3 0.0 collective-permute-done.5
  64.3 3.9 %collective-permute-start.9 = (f32[3,32,128]{2,1,0:T(8,128)S(1)}, f32[3,32,128]{2,1,0:T(8,128)S(1)}, u32[]{:S(2)}, u32[]{:S(2)}) collective-permute-start(f32[3,32,128]{2,1,0:T(8,128)S(1)} %add_add_fusion), channel_id=1, source_target_pairs={{0,8},{1,9},{2,10},{3,11},{4,12},{5,13},{6,14},{7,15},{8,16},{9,17... | collective-permute-start | bytes 147464 | tf_op jit(solution)/shard_map/filter_z/ppermute | solution.py:172
  68.2 0.4 collective-permute-start.10
  68.6 4.9 %collective-permute-start.8 = (f32[3,32,128]{2,1,0:T(8,128)S(1)}, f32[3,32,128]{2,1,0:T(8,128)S(1)}, u32[]{:S(2)}, u32[]{:S(2)}) collective-permute-start(f32[3,32,128]{2,1,0:T(8,128)S(1)} %add_add_fusion), channel_id=1, source_target_pairs={{0,16},{1,17},{2,18},{3,19},{4,20},{5,21},{6,22},{7,23},{8,24},{9,... | collective-permute-start | bytes 147464 | tf_op jit(solution)/shard_map/filter_z/ppermute | solution.py:172
  73.6 0.0 collective-permute-done.2.above_ref
  73.6 0.0 collective-permute-done.3.below_ref
  73.6 2.3 %copy-done = bf16[1536,1536]{1,0:T(8,128)(2,1)S(1)} copy-done((bf16[1536,1536]{1,0:T(8,128)(2,1)S(1)}, bf16[1536,1536]{1,0:T(8,128)(2,1)}, u32[]{:S(2)}) %copy-start) | copy-done | bytes 4718616
  75.9 2.0 %input_grad.1 = bf16[512,128]{1,0:T(8,128)(2,1)} custom-call(bf16[512,128]{1,0:T(8,128)(2,1)S(1)} %collective-permute-done.2.above_ref, bf16[512,128]{1,0:T(8,128)(2,1)S(1)} %get-tuple-element.7.own_ref, bf16[512,128]{1,0:T(8,128)(2,1)S(1)} %collective-permute-done.3.below_ref, bf16[1536,1536]{1,0:T(8,128)(2,1)S(1)} %copy-done), custom_call_target="tpu_custom_call" | custom-call | flops 603979776 | bytes 6000000 | tf_op jit(solution)/shard_map/input_grad/pallas_call | solution.py:156
  78.0 9.7 %all-to-all-start.1 = ((bf16[8,64,128]{2,1,0:T(8,128)(2,1)}), bf16[8,64,128]{2,1,0:T(8,128)(2,1)S(1)}, u32[]{:S(2)}, u32[]{:S(2)}) async-start(bf16[8,64,128]{2,1,0:T(8,128)(2,1)} %bitcast.6), calls=%async_computation.1 | async-start | bytes 262144 | tf_op jit(solution)/shard_map/input_grad/all_to_all | solution.py:159
  87.7 0.0 collective-permute-done.9
  87.7 0.0 collective-permute-done.10
  87.7 0.0 collective-permute-done.8
  87.7 0.1 collective-permute-start.11
  87.8 4.9 %all-to-all-done.1 = bf16[8,64,128]{2,1,0:T(8,128)(2,1)S(1)} async-done(((bf16[8,64,128]{2,1,0:T(8,128)(2,1)}), bf16[8,64,128]{2,1,0:T(8,128)(2,1)S(1)}, u32[]{:S(2)}, u32[]{:S(2)}) %all-to-all-start.1) | async-done | bytes 131104 | tf_op jit(solution)/shard_map/input_grad/all_to_all | solution.py:159
  92.7 0.7 copy.32
  93.5 0.0 collective-permute-done.11
  93.5 0.2 reshape.84
  93.7 0.9 copy.31
  (10 shorter events, 0.1 us)
Async XLA Ops:
  0.6 20.3 %copy-start.1 = (bf16[16,9,32,32]{3,2,1,0:T(8,128)(2,1)S(1)}, bf16[16,9,32,32]{3,2,1,0:T(8,128)(2,1)}, u32[]{:S(2)}) copy-start(bf16[16,9,32,32]{3,2,1,0:T(8,128)(2,1)} %param.6) | copy-start | bytes 884740
  14.2 14.0 %collective-permute-start = (bf16[512,128]{1,0:T(8,128)(2,1)}, bf16[512,128]{1,0:T(8,128)(2,1)S(1)}, u32[]{:S(2)}, u32[]{:S(2)}) collective-permute-start(bf16[512,128]{1,0:T(8,128)(2,1)} %bitcast.2), channel_id=1, source_target_pairs={{0,32},{32,64},{64,96},{96,128},{128,160},{160,192},{192,224},{224... | collective-permute-start | bytes 393224 | tf_op jit(solution)/shard_map/input_rows/ppermute | solution.py:140
  17.0 11.2 %collective-permute-start.1 = (bf16[512,128]{1,0:T(8,128)(2,1)}, bf16[512,128]{1,0:T(8,128)(2,1)S(1)}, u32[]{:S(2)}, u32[]{:S(2)}) collective-permute-start(bf16[512,128]{1,0:T(8,128)(2,1)} %bitcast.2), channel_id=1, source_target_pairs={{32,0},{64,32},{96,64},{128,96},{160,128},{192,160},{224,192},{1,2... | collective-permute-start | bytes 393224 | tf_op jit(solution)/shard_map/input_rows/ppermute | solution.py:141
  24.3 3.9 %copy-start.2 = (f32[32]{0:T(128)S(1)}, f32[32]{0:T(128)}, u32[]{:S(2)}) copy-start(f32[32]{0:T(128)} %param.7) | copy-start | bytes 388
  33.5 16.1 %all-to-all-start.2 = ((f32[8,192,128]{2,1,0:T(8,128)}), f32[8,192,128]{2,1,0:T(8,128)S(1)}, u32[]{:S(2)}, u32[]{:S(2)}) async-start(f32[8,192,128]{2,1,0:T(8,128)} %bitcast.8), calls=%async_computation.2 | async-start | bytes 1572864 | tf_op jit(solution)/shard_map/filter_rot/all_to_all | solution.py:150
  49.6 1.3 %collective-permute-start.4 = (f32[3,32,128]{2,1,0:T(8,128)S(1)}, f32[3,32,128]{2,1,0:T(8,128)S(1)}, u32[]{:S(2)}, u32[]{:S(2)}) collective-permute-start(f32[3,32,128]{2,1,0:T(8,128)S(1)} %dynamic-slice_bitcast_fusion), channel_id=1, source_target_pairs={{0,1},{1,0},{2,3},{3,2},{4,5},{5,4},{6,7},{7,6},{8,9},{9,8},{10,11... | collective-permute-start | bytes 147464 | tf_op jit(solution)/shard_map/filter_core/ppermute | solution.py:178
  50.9 13.3 %collective-permute-start.6 = (f32[3,32,128]{2,1,0:T(8,128)S(1)}, f32[3,32,128]{2,1,0:T(8,128)S(1)}, u32[]{:S(2)}, u32[]{:S(2)}) collective-permute-start(f32[3,32,128]{2,1,0:T(8,128)S(1)} %bitcast_add_fusion), channel_id=1, source_target_pairs={{0,2},{1,3},{2,4},{3,5},{4,6},{5,7},{6,0},{7,1},{8,10},{9,11},{10,... | collective-permute-start | bytes 147464 | tf_op jit(solution)/shard_map/filter_y/ppermute | solution.py:172
  52.9 11.3 %collective-permute-start.7 = (f32[3,32,128]{2,1,0:T(8,128)S(1)}, f32[3,32,128]{2,1,0:T(8,128)S(1)}, u32[]{:S(2)}, u32[]{:S(2)}) collective-permute-start(f32[3,32,128]{2,1,0:T(8,128)S(1)} %bitcast_add_fusion), channel_id=1, source_target_pairs={{0,6},{1,7},{2,0},{3,1},{4,2},{5,3},{6,4},{7,5},{8,14},{9,15},{10,... | collective-permute-start | bytes 147464 | tf_op jit(solution)/shard_map/filter_y/ppermute | solution.py:172
  56.1 8.1 %collective-permute-start.5 = (f32[3,32,128]{2,1,0:T(8,128)S(1)}, f32[3,32,128]{2,1,0:T(8,128)S(1)}, u32[]{:S(2)}, u32[]{:S(2)}) collective-permute-start(f32[3,32,128]{2,1,0:T(8,128)S(1)} %bitcast_add_fusion), channel_id=1, source_target_pairs={{0,4},{1,5},{2,6},{3,7},{4,0},{5,1},{6,2},{7,3},{8,12},{9,13},{10,... | collective-permute-start | bytes 147464 | tf_op jit(solution)/shard_map/filter_y/ppermute | solution.py:172
  57.5 16.1 %collective-permute-start.2 = (bf16[512,128]{1,0:T(8,128)(2,1)S(1)}, bf16[512,128]{1,0:T(8,128)(2,1)S(1)}, u32[]{:S(2)}, u32[]{:S(2)}) collective-permute-start(bf16[512,128]{1,0:T(8,128)(2,1)S(1)} %get-tuple-element.7.own_ref), channel_id=1, source_target_pairs={{0,32},{32,64},{64,96},{96,128},{128,160},{160,192},{192,224},{224... | collective-permute-start | bytes 393224 | tf_op jit(solution)/shard_map/grad_rows/ppermute | solution.py:153
  60.9 12.7 %collective-permute-start.3 = (bf16[512,128]{1,0:T(8,128)(2,1)S(1)}, bf16[512,128]{1,0:T(8,128)(2,1)S(1)}, u32[]{:S(2)}, u32[]{:S(2)}) collective-permute-start(bf16[512,128]{1,0:T(8,128)(2,1)S(1)} %get-tuple-element.7.own_ref), channel_id=1, source_target_pairs={{32,0},{64,32},{96,64},{128,96},{160,128},{192,160},{224,192},{1,2... | collective-permute-start | bytes 393224 | tf_op jit(solution)/shard_map/grad_rows/ppermute | solution.py:154
  64.3 23.4 %collective-permute-start.9 = (f32[3,32,128]{2,1,0:T(8,128)S(1)}, f32[3,32,128]{2,1,0:T(8,128)S(1)}, u32[]{:S(2)}, u32[]{:S(2)}) collective-permute-start(f32[3,32,128]{2,1,0:T(8,128)S(1)} %add_add_fusion), channel_id=1, source_target_pairs={{0,8},{1,9},{2,10},{3,11},{4,12},{5,13},{6,14},{7,15},{8,16},{9,17... | collective-permute-start | bytes 147464 | tf_op jit(solution)/shard_map/filter_z/ppermute | solution.py:172
  68.2 19.5 %collective-permute-start.10 = (f32[3,32,128]{2,1,0:T(8,128)S(1)}, f32[3,32,128]{2,1,0:T(8,128)S(1)}, u32[]{:S(2)}, u32[]{:S(2)}) collective-permute-start(f32[3,32,128]{2,1,0:T(8,128)S(1)} %add_add_fusion), channel_id=1, source_target_pairs={{0,24},{1,25},{2,26},{3,27},{4,28},{5,29},{6,30},{7,31},{8,0},{9,1... | collective-permute-start | bytes 147464 | tf_op jit(solution)/shard_map/filter_z/ppermute | solution.py:172
  68.6 19.0 %collective-permute-start.8 = (f32[3,32,128]{2,1,0:T(8,128)S(1)}, f32[3,32,128]{2,1,0:T(8,128)S(1)}, u32[]{:S(2)}, u32[]{:S(2)}) collective-permute-start(f32[3,32,128]{2,1,0:T(8,128)S(1)} %add_add_fusion), channel_id=1, source_target_pairs={{0,16},{1,17},{2,18},{3,19},{4,20},{5,21},{6,22},{7,23},{8,24},{9,... | collective-permute-start | bytes 147464 | tf_op jit(solution)/shard_map/filter_z/ppermute | solution.py:172
  73.6 2.3 %copy-start = (bf16[1536,1536]{1,0:T(8,128)(2,1)S(1)}, bf16[1536,1536]{1,0:T(8,128)(2,1)}, u32[]{:S(2)}) copy-start(bf16[1536,1536]{1,0:T(8,128)(2,1)} %get-tuple-element.8.wt_ref) | copy-start | bytes 14155780
  78.0 14.8 %all-to-all-start.1 = ((bf16[8,64,128]{2,1,0:T(8,128)(2,1)}), bf16[8,64,128]{2,1,0:T(8,128)(2,1)S(1)}, u32[]{:S(2)}, u32[]{:S(2)}) async-start(bf16[8,64,128]{2,1,0:T(8,128)(2,1)} %bitcast.6), calls=%async_computation.1 | async-start | bytes 262144 | tf_op jit(solution)/shard_map/input_grad/all_to_all | solution.py:159
  87.7 5.8 %collective-permute-start.11 = (f32[3,32,128]{2,1,0:T(8,128)S(1)}, f32[3,32,128]{2,1,0:T(8,128)S(1)}, u32[]{:S(2)}, u32[]{:S(2)}) collective-permute-start(f32[3,32,128]{2,1,0:T(8,128)S(1)} %add_multiply_fusion), channel_id=1, source_target_pairs={{0,1},{1,0},{2,3},{3,2},{4,5},{5,4},{6,7},{7,6},{8,9},{9,8},{10,11... | collective-permute-start | bytes 147464 | tf_op jit(solution)/shard_map/filter_out/ppermute | solution.py:186

commit v2 on v1

v2 whole, which is shorter than its diff:
```python
import functools

import jax
import jax.numpy as jnp
from jax import lax
from jax.experimental import pallas as pl
from jax.experimental.pallas import tpu as pltpu
from jax.sharding import PartitionSpec as P

CH = 32
F32 = jnp.float32
BF16 = jnp.bfloat16


def spread(src, dst):
    n = src.shape[2]
    for a in range(3):
        for b in range(3):
            v = src[3 * a + b]
            for fine in range(4):
                t = v
                if fine:
                    cut = n - CH * fine
                    t = jnp.concatenate([v[:, cut:], v[:, :cut]], axis=1)
                for coarse in range(n // 128):
                    u = t
                    if coarse:
                        cut = n - 128 * coarse
                        u = jnp.concatenate([t[:, cut:], t[:, :cut]], axis=1)
                    row = b * n + CH * (4 * coarse + fine)
                    dst[row : row + CH, a * n : (a + 1) * n] = u


def row_of(j, groups):
    return jnp.where(j % 2 == 0, j // 2, groups - 1 - j // 2)


def place_of(k, groups):
    return 2 * k if 2 * k < groups else 2 * (groups - 1 - k) + 1


def turned_rows(v, groups, forth):
    n = v.shape[0]
    local = n // groups
    i = lax.broadcasted_iota(jnp.int32, (n, n), 0)
    j = lax.broadcasted_iota(jnp.int32, (n, n), 1)
    if forth:
        i, j = j, i
    one = (i // groups == j % local) & (i % groups == row_of(j // local, groups))
    return jnp.dot(one.astype(BF16), v, preferred_element_type=F32).astype(BF16)


def pack_kernel(x_ref, c_ref, out_ref):
    groups, two, width = out_ref.shape
    out_ref[:, : two // 2] = turned_rows(x_ref[...], groups, True).reshape(groups, two // 2, width)
    out_ref[:, two // 2 :] = turned_rows(c_ref[...], groups, True).reshape(groups, two // 2, width)


def unpack_kernel(groups, dx_ref, out_ref):
    out_ref[...] = turned_rows(dx_ref[...], groups, False)


def shift_right(v):
    lane = lax.broadcasted_iota(jnp.int32, v.shape, 1)
    return jnp.where(lane == 0, 0.0, pltpu.roll(v, 1, 1))


def shift_left(v):
    lane = lax.broadcasted_iota(jnp.int32, v.shape, 1)
    n = v.shape[1]
    return jnp.where(lane == n - 1, 0.0, pltpu.roll(v, n - 1, 1))


def grad_kernel(recv_ref, above_ref, below_ref, f_ref, bias_ref, g_ref, keep_ref, give_ref, x2_ref, w_ref):
    groups, two, width = recv_ref.shape
    half = two // 2
    n = groups * half
    rot = n // CH
    x0 = recv_ref[:, :half, :].reshape(n, width)
    cot = recv_ref[:, half:, :].reshape(n, width)
    rows = (above_ref[...], x0, below_ref[...])
    x3 = jnp.concatenate(rows, axis=0)
    spread(f_ref, w_ref)
    for a in range(3):
        x = rows[a]
        turned = jnp.concatenate([x[CH:], x[:CH]], axis=0)
        for rep in range(2):
            x2_ref[a, rep * n : (rep + 1) * n, :width] = x
            x2_ref[a, rep * n : (rep + 1) * n, width:] = turned
    parts = [
        jnp.dot(w_ref[b * n : (b + 1) * n, :], x3, preferred_element_type=F32) for b in range(3)
    ]
    bias = jnp.concatenate([bias_ref[...]] * rot, axis=0)
    pre = parts[1] + shift_right(parts[0]) + shift_left(parts[2]) + bias
    sigma = jax.nn.sigmoid(pre)
    grad = cot.astype(F32) * sigma * (1.0 + pre * (1.0 - sigma))
    own = grad.astype(BF16)
    g_ref[...] = own
    taps = (shift_left(grad).astype(BF16), own, shift_right(grad).astype(BF16))
    blank = jnp.zeros((CH, width), BF16)
    total = [None] * 3
    for p in range(rot // 2):
        sides = []
        for r in (2 * p, 2 * p + 1):
            sides.append(jnp.concatenate([t[CH * r : CH * (r + 1)] for t in taps] + [blank], axis=0))
        g2 = jnp.concatenate(sides, axis=1)
        for a in range(3):
            x = x2_ref[a, 2 * CH * p : 2 * CH * p + n, :]
            d = lax.dot_general(x, g2, (((1,), (1,)), ((), ())), preferred_element_type=F32)
            total[a] = d if total[a] is None else total[a] + d
    lane = lax.broadcasted_iota(jnp.int32, (n, 4 * CH), 1)
    first = jnp.where(lane < 3 * CH, total[0], pltpu.roll(total[2], 3 * CH, 1))
    second = jnp.where(lane < 3 * CH, total[1], pltpu.roll(total[2], 2 * CH, 1))
    first = first.reshape(groups, 2, CH, 4 * CH)
    second = second.reshape(groups, 2, CH, 4 * CH)
    third = total[2].reshape(groups, 2, 4, 8, 4 * CH)
    spots = lax.broadcasted_iota(jnp.int32, (groups, 2, 8, 4 * CH), 3) // CH
    last = jnp.zeros((groups, 2, 8, 4 * CH), F32)
    for j in range(4):
        moved = pltpu.roll(third[:, :, j].reshape(-1, 4 * CH), (2 * CH + CH * j) % (4 * CH), 1)
        last = jnp.where(spots == j, moved.reshape(last.shape), last)
    core = lax.axis_index("rows") % 2
    for c in range(2):

        @pl.when(core == c)
        def _():
            for ref, part in ((keep_ref, c), (give_ref, 1 - c)):
                ref[:, :CH] = first[:, part]
                ref[:, CH : 2 * CH] = second[:, part]
                ref[:, 2 * CH :] = last[:, part]


def out_kernel(scale, own_ref, other_ref, out_ref):
    core = lax.axis_index("rows") % 2
    for c in range(2):

        @pl.when(core == c)
        def _():
            for ref, part in ((own_ref, c), (other_ref, 1 - c)):
                v = ref[...] * scale
                for row in range(2):
                    t = v[CH * row : CH * (row + 1)].T
                    for b in range(3):
                        out_ref[part, 3 * row + b] = t[CH * b : CH * (b + 1)]
                    out_ref[part, 6 + row] = t[3 * CH :]
                e = v[2 * CH :]
                e = jnp.concatenate([e[:, CH * j : CH * (j + 1)] for j in range(4)], axis=0)
                out_ref[part, 8] = e.T


def input_kernel(above_ref, own_ref, below_ref, f_ref, out_ref, wt_ref):
    n = own_ref.shape[0]
    spread(f_ref, wt_ref)
    g3 = jnp.concatenate([below_ref[...], own_ref[...], above_ref[...]], axis=0)
    parts = [
        jnp.dot(wt_ref[b * n : (b + 1) * n, :], g3, preferred_element_type=F32) for b in range(3)
    ]
    out = parts[1] + shift_left(parts[0]) + shift_right(parts[2])
    out_ref[...] = out.astype(BF16)


LIMIT = pltpu.CompilerParams(vmem_limit_bytes=20 * 1024 * 1024)


def call(kernel, outs, flops, scratch=()):
    return pl.pallas_call(
        kernel,
        out_shape=outs,
        scratch_shapes=list(scratch),
        compiler_params=LIMIT,
        cost_estimate=pl.CostEstimate(flops=flops, bytes_accessed=6_000_000, transcendentals=0),
    )


def shaped(shape, dtype):
    return jax.ShapeDtypeStruct(shape, dtype)


def shards(inputs, cotangent, filters, bias):
    local_ch, band, width = inputs.shape
    rotations, taps = filters.shape[:2]
    n = rotations * CH
    groups = lax.axis_size("rot")
    bands = lax.axis_size("rows")
    total = groups * bands

    with jax.named_scope("to_rows"):
        packed = call(pack_kernel, shaped((groups, 2 * local_ch, width), BF16), 4 * n * n * width)(
            inputs.reshape(n, width), cotangent.reshape(n, width)
        )
        recv = lax.all_to_all(packed, "rot", 0, 0, tiled=True)
    with jax.named_scope("weights"):
        fwd = jnp.transpose(filters, (1, 2, 0, 3)).reshape(taps, CH, n)
        back = jnp.concatenate([filters[:1], filters[:0:-1]], axis=0)
        bwd = jnp.transpose(back, (1, 3, 0, 2)).reshape(taps, CH, n)
        bias2 = jnp.broadcast_to(bias[:, None], (CH, width))

    order = ("rot", "rows")

    def place(row):
        return place_of(row % groups, groups) * bands + row // groups

    up = [(place(i), place(i + 1)) for i in range(total - 1)]
    down = [(j, i) for i, j in up]
    with jax.named_scope("input_rows"):
        recv, fwd, bwd, bias2 = lax.optimization_barrier((recv, fwd, bwd, bias2))
        own = recv[:, :local_ch].reshape(n, width)
        above = lax.ppermute(own, order, up)
        below = lax.ppermute(own, order, down)
    with jax.named_scope("grad"):
        square = pltpu.VMEM((3 * n, 3 * n), BF16)
        half = shaped((groups, 9 * 8, 4 * CH), F32)
        g, keep, give = call(
            grad_kernel,
            (shaped((n, width), BF16), half, half),
            2 * 18 * n * n * width,
            [pltpu.VMEM((3, 2 * n, 2 * width), BF16), square],
        )(recv, above, below, fwd, bias2)
    swap = [(i, i ^ 1) for i in range(bands)]
    with jax.named_scope("filter_core"):
        part = keep + lax.ppermute(give, "rows", swap)
    with jax.named_scope("filter_rot"):
        got = lax.all_to_all(part, "rot", 0, 0, tiled=True)
    with jax.named_scope("grad_rows"):
        g_above = lax.ppermute(g, order, up)
        g_below = lax.ppermute(g, order, down)
    with jax.named_scope("input_grad"):
        dx = call(input_kernel, shaped((n, width), BF16), 2 * 9 * n * n * width, [square])(
            g_above, g, g_below, bwd
        )
    with jax.named_scope("filter_rot"):
        got, dx = lax.optimization_barrier((got, dx))
        v = jnp.sum(got, axis=0)
    with jax.named_scope("input_grad"):
        dx = lax.all_to_all(dx.reshape(groups, local_ch, width), "rot", 0, 0, tiled=True)
        input_grad = call(
            functools.partial(unpack_kernel, groups), shaped((n, width), BF16), 2 * n * n * width
        )(dx.reshape(n, width)).reshape(inputs.shape)

    def turn(i, step, s):
        now = i // step % 4
        return i + ((now + s) % 4 - now) * step

    def add_four(v, step):
        p1, p2, p3 = [
            lax.ppermute(v, "rows", [(i, turn(i, step, s)) for i in range(bands)]) for s in (1, 2, 3)
        ]
        return (v + p2) + (p1 + p3)

    with jax.named_scope("filter_y"):
        v = add_four(v, 2)
    with jax.named_scope("filter_z"):
        v = add_four(v, 8)
    with jax.named_scope("filter_out"):
        scale = float(rotations * band * bands * width) ** (-0.5)
        other = lax.ppermute(v, "rows", swap)
        filter_grad = call(
            functools.partial(out_kernel, scale), shaped((2, taps, CH, CH), F32), 1000
        )(v, other)
    return input_grad, filter_grad


def solution(mesh):
    return jax.shard_map(
        shards,
        mesh=mesh,
        in_specs=(P("rot", "rows", None), P("rot", "rows", None), P(), P()),
        out_specs=(P("rot", "rows", None), P("rot", None, None, None)),
        check_vma=False,
    )
```

time: 95 us -> 80.2 us (0.84)
  the two profiles are of different devices: /device:TPU:2 before, /device:TPU:24 now
where the time goes in v2:
time: 80.2 us; the launch traced here: 79.7 us
  starting transfers between devices  40.2 us (50%)
  waiting for transfers between devices  21 us (26%)
  Pallas kernels  9.46 us (12%)
  local copies, waits for them, and re-layouts  7.1 us (9%)
  other arithmetic  1.02 us (1%)
  between operations  0.81 us (1%)
    ppermute x6, starting transfers between devices, add_four(): lax.ppermute(v, 'rows', [(i, turn(i, step, s)) for i in range(bands)])  11.7 us
    all_to_all x1, starting transfers between devices, shards(): recv = lax.all_to_all(packed, 'rot', 0, 0, tiled=True)  5.66 us
    all_to_all x1, starting transfers between devices, shards(): got = lax.all_to_all(part, 'rot', 0, 0, tiled=True)  5.57 us
    ppermute x6, waiting for transfers between devices, add_four(): lax.ppermute(v, 'rows', [(i, turn(i, step, s)) for i in range(bands)])  5.1 us
    pallas_call x1, Pallas kernels, shards(): call(grad_kernel, (shaped((n, width), BF16), half, half), 2 * 18 * n * n...  4.38 us
    all_to_all x1, waiting for transfers between devices, shards(): lax.all_to_all(dx.reshape(groups, local_ch, width), 'rot', 0, 0, tiled=True)  4.29 us
    all_to_all x1, starting transfers between devices, shards(): lax.all_to_all(dx.reshape(groups, local_ch, width), 'rot', 0, 0, tiled=True)  4.24 us
    ppermute x1, starting transfers between devices, shards(): below = lax.ppermute(own, order, down)  4.06 us
  transfers between devices with their start and end apart: 15, of which 11 were waited for; matrix products, arithmetic and copies ran while one was open for 5% of the time, Pallas kernels for 4%

profile of v2, /device:TPU:24, one launch (start us, length us, event | category | flops | bytes accessed | tf_op | source)
XLA Modules:
  0.0 79.7 jit_solution(1996107428427700227)
XLA Ops:
  0.6 0.9 %copy-done = bf16[64,8,128]{2,1,0:T(8,128)(2,1)S(1)} copy-done((bf16[64,8,128]{2,1,0:T(8,128)(2,1)S(1)}, bf16[64,8,128]{2,1,0:T(8,128)(2,1)}, u32[]{:S(2)}) %copy-start) | copy-done | bytes 131096
  1.5 0.9 %copy-done.1 = bf16[64,8,128]{2,1,0:T(8,128)(2,1)S(1)} copy-done((bf16[64,8,128]{2,1,0:T(8,128)(2,1)S(1)}, bf16[64,8,128]{2,1,0:T(8,128)(2,1)}, u32[]{:S(2)}) %copy-start.1) | copy-done | bytes 131096
  2.4 1.1 %to_rows.1 = bf16[8,128,128]{2,1,0:T(8,128)(2,1)} custom-call(bf16[512,128]{1,0:T(8,128)(2,1)S(1)} %bitcast.14, bf16[512,128]{1,0:T(8,128)(2,1)S(1)} %bitcast.15), custom_call_target="tpu_custom_call" | custom-call | flops 134217728 | bytes 6000000 | tf_op jit(solution)/shard_map/to_rows/pallas_call | solution.py:188
  3.6 5.7 %all-to-all-start = ((bf16[8,128,128]{2,1,0:T(8,128)(2,1)}), bf16[8,128,128]{2,1,0:T(8,128)(2,1)S(1)}, u32[]{:S(2)}, u32[]{:S(2)}) async-start(bf16[8,128,128]{2,1,0:T(8,128)(2,1)} %to_rows.1), calls=%async_computation | async-start | bytes 524288 | tf_op jit(solution)/shard_map/to_rows/all_to_all | solution.py:191
  9.2 0.0 slice-start.1
  9.3 1.2 %slice-done = bf16[15,9,32,32]{3,2,1,0:T(8,128)(2,1)S(1)} async-done(((bf16[16,9,32,32]{3,2,1,0:T(8,128)(2,1)}), bf16[15,9,32,32]{3,2,1,0:T(8,128)(2,1)S(1)}, s32[]{:S(2)}) %slice-start) | async-done | bytes 276504 | tf_op jit(solution)/shard_map/weights/slice | solution.py:194
  10.5 0.2 rev.3
  10.7 0.2 maximum_bitcast_fusion
  10.9 0.9 %copy.7 = bf16[9,32,16,32]{3,2,1,0:T(8,128)(2,1)S(1)} copy(bf16[9,32,16,32]{1,3,0,2:T(8,128)(2,1)S(1)} %maximum_bitcast_fusion) | data formatting | bytes 589824 | tf_op jit(solution)/shard_map/weights/transpose | solution.py:195
  11.9 0.0 copy-start.2
  11.9 1.1 %reshape.32.f_ref = bf16[9,32,512]{2,1,0:T(8,128)(2,1)S(1)} reshape(bf16[9,32,16,32]{3,2,1,0:T(8,128)(2,1)S(1)} %copy.7) | data formatting | bytes 589824 | tf_op jit(solution)/shard_map/weights/reshape | solution.py:195
  13.0 0.1 copy-done.2
  13.1 0.5 copy.6
  13.6 0.0 copy-start.3
  13.6 1.1 %reshape.31.f_ref = bf16[9,32,512]{2,1,0:T(8,128)(2,1)S(1)} reshape(bf16[9,32,16,32]{3,2,1,0:T(8,128)(2,1)S(1)} %copy.6) | data formatting | bytes 589824 | tf_op jit(solution)/shard_map/weights/reshape | solution.py:193
  14.8 1.8 %all-to-all-done.recv_ref = bf16[8,128,128]{2,1,0:T(8,128)(2,1)S(1)} async-done(((bf16[8,128,128]{2,1,0:T(8,128)(2,1)}), bf16[8,128,128]{2,1,0:T(8,128)(2,1)S(1)}, u32[]{:S(2)}, u32[]{:S(2)}) %all-to-all-start) | async-done | bytes 262176 | tf_op jit(solution)/shard_map/to_rows/all_to_all | solution.py:191
  16.5 0.1 broadcast_in_dim.2.bias_ref
  16.6 2.4 %collective-permute-start = (bf16[512,128]{1,0:T(8,128)(2,1)S(1)}, bf16[512,128]{1,0:T(8,128)(2,1)S(1)}, u32[]{:S(2)}, u32[]{:S(2)}) collective-permute-start(bf16[512,128]{1,0:T(8,128)(2,1)S(1)} %bitcast.17), channel_id=1, source_target_pairs={{0,64},{64,128},{128,192},{192,224},{224,160},{160,96},{96,32},{32... | collective-permute-start | bytes 393224 | tf_op jit(solution)/shard_map/input_rows/ppermute | solution.py:208
  19.0 4.1 %collective-permute-start.1 = (bf16[512,128]{1,0:T(8,128)(2,1)S(1)}, bf16[512,128]{1,0:T(8,128)(2,1)S(1)}, u32[]{:S(2)}, u32[]{:S(2)}) collective-permute-start(bf16[512,128]{1,0:T(8,128)(2,1)S(1)} %bitcast.18), channel_id=1, source_target_pairs={{64,0},{128,64},{192,128},{224,192},{160,224},{96,160},{32,96},{1,... | collective-permute-start | bytes 393224 | tf_op jit(solution)/shard_map/input_rows/ppermute | solution.py:209
  23.1 0.8 %collective-permute-done.above_ref = bf16[512,128]{1,0:T(8,128)(2,1)S(1)} collective-permute-done((bf16[512,128]{1,0:T(8,128)(2,1)S(1)}, bf16[512,128]{1,0:T(8,128)(2,1)S(1)}, u32[]{:S(2)}, u32[]{:S(2)}) %collective-permute-start) | collective-permute-done | bytes 131104 | tf_op jit(solution)/shard_map/input_rows/ppermute | solution.py:208
  23.9 2.0 %collective-permute-done.1.below_ref = bf16[512,128]{1,0:T(8,128)(2,1)S(1)} collective-permute-done((bf16[512,128]{1,0:T(8,128)(2,1)S(1)}, bf16[512,128]{1,0:T(8,128)(2,1)S(1)}, u32[]{:S(2)}, u32[]{:S(2)}) %collective-permute-start.1) | collective-permute-done | bytes 131104 | tf_op jit(solution)/shard_map/input_rows/ppermute | solution.py:209
  25.9 4.4 %grad.1 = (bf16[512,128]{1,0:T(8,128)(2,1)S(1)}, f32[8,72,128]{2,1,0:T(8,128)S(1)}, f32[8,72,128]{2,1,0:T(8,128)S(1)}) custom-call(bf16[8,128,128]{2,1,0:T(8,128)(2,1)S(1)} %all-to-all-done.recv_ref, bf16[512,128]{1,0:T(8,128)(2,1)S(1)} %collective-permute-done.above_ref, bf16[512,128]{1,0:T(8,128)(2,1)S(1)} %collective-permute-done.1.below_ref, ...), custom_call_target="tpu_custom_call" | custom-call | flops 1207959552 | bytes 6000000 | tf_op jit(solution)/shard_map/grad/pallas_call | solution.py:213
  30.3 0.1 collective-permute-start.2
  30.4 1.6 %collective-permute-done.2 = f32[8,72,128]{2,1,0:T(8,128)S(1)} collective-permute-done((f32[8,72,128]{2,1,0:T(8,128)S(1)}, f32[8,72,128]{2,1,0:T(8,128)S(1)}, u32[]{:S(2)}, u32[]{:S(2)}) %collective-permute-start.2) | collective-permute-done | bytes 294944 | tf_op jit(solution)/shard_map/filter_core/ppermute | solution.py:221
  31.9 0.7 add.21
  32.7 5.6 %all-to-all-start.1 = ((f32[8,72,128]{2,1,0:T(8,128)}), f32[8,72,128]{2,1,0:T(8,128)S(1)}, u32[]{:S(2)}, u32[]{:S(2)}) async-start(f32[8,72,128]{2,1,0:T(8,128)} %add.21), calls=%async_computation.1 | async-start | bytes 589824 | tf_op jit(solution)/shard_map/filter_rot/all_to_all | solution.py:223
  38.3 3.9 %collective-permute-start.3 = (bf16[512,128]{1,0:T(8,128)(2,1)S(1)}, bf16[512,128]{1,0:T(8,128)(2,1)S(1)}, u32[]{:S(2)}, u32[]{:S(2)}) collective-permute-start(bf16[512,128]{1,0:T(8,128)(2,1)S(1)} %get-tuple-element.16.own_ref), channel_id=1, source_target_pairs={{0,64},{64,128},{128,192},{192,224},{224,160},{160,96},{96,32},{32... | collective-permute-start | bytes 393224 | tf_op jit(solution)/shard_map/grad_rows/ppermute | solution.py:225
  42.2 2.5 %collective-permute-start.4 = (bf16[512,128]{1,0:T(8,128)(2,1)S(1)}, bf16[512,128]{1,0:T(8,128)(2,1)S(1)}, u32[]{:S(2)}, u32[]{:S(2)}) collective-permute-start(bf16[512,128]{1,0:T(8,128)(2,1)S(1)} %get-tuple-element.16.own_ref), channel_id=1, source_target_pairs={{64,0},{128,64},{192,128},{224,192},{160,224},{96,160},{32,96},{1,... | collective-permute-start | bytes 393224 | tf_op jit(solution)/shard_map/grad_rows/ppermute | solution.py:226
  44.7 1.2 %collective-permute-done.3.above_ref = bf16[512,128]{1,0:T(8,128)(2,1)S(1)} collective-permute-done((bf16[512,128]{1,0:T(8,128)(2,1)S(1)}, bf16[512,128]{1,0:T(8,128)(2,1)S(1)}, u32[]{:S(2)}, u32[]{:S(2)}) %collective-permute-start.3) | collective-permute-done | bytes 131104 | tf_op jit(solution)/shard_map/grad_rows/ppermute | solution.py:225
  45.9 3.1 %collective-permute-done.4.below_ref = bf16[512,128]{1,0:T(8,128)(2,1)S(1)} collective-permute-done((bf16[512,128]{1,0:T(8,128)(2,1)S(1)}, bf16[512,128]{1,0:T(8,128)(2,1)S(1)}, u32[]{:S(2)}, u32[]{:S(2)}) %collective-permute-start.4) | collective-permute-done | bytes 131104 | tf_op jit(solution)/shard_map/grad_rows/ppermute | solution.py:226
  49.1 2.1 %input_grad.2 = bf16[512,128]{1,0:T(8,128)(2,1)} custom-call(bf16[512,128]{1,0:T(8,128)(2,1)S(1)} %collective-permute-done.3.above_ref, bf16[512,128]{1,0:T(8,128)(2,1)S(1)} %get-tuple-element.16.own_ref, bf16[512,128]{1,0:T(8,128)(2,1)S(1)} %collective-permute-done.4.below_ref, bf16[9,32,512]{2,1,0:T(8,128)(2,1)S(1)} %reshape.32.f_ref), custom_call_target="tpu_custom_call" | custom-call | flops 603979776 | bytes 6000000 | tf_op jit(solution)/shard_map/input_grad/pallas_call | solution.py:228
  51.1 0.0 all-to-all-done.1
  51.2 0.1 collective-permute-start.5
  51.3 1.8 %collective-permute-start.6 = (f32[72,128]{1,0:T(8,128)S(1)}, f32[72,128]{1,0:T(8,128)S(1)}, u32[]{:S(2)}, u32[]{:S(2)}) collective-permute-start(f32[72,128]{1,0:T(8,128)S(1)} %reduce_sum.9), channel_id=1, source_target_pairs={{0,2},{1,3},{2,4},{3,5},{4,6},{5,7},{6,0},{7,1},{8,10},{9,11},{10,... | collective-permute-start | bytes 110600 | tf_op jit(solution)/shard_map/filter_y/ppermute | solution.py:246
  53.1 0.3 collective-permute-start.7
  53.4 3.3 %collective-permute-done.5 = f32[72,128]{1,0:T(8,128)S(1)} collective-permute-done((f32[72,128]{1,0:T(8,128)S(1)}, f32[72,128]{1,0:T(8,128)S(1)}, u32[]{:S(2)}, u32[]{:S(2)}) %collective-permute-start.5) | collective-permute-done | bytes 36896 | tf_op jit(solution)/shard_map/filter_y/ppermute | solution.py:246
  56.7 0.0 collective-permute-done.6
  56.7 1.6 %collective-permute-done.7 = f32[72,128]{1,0:T(8,128)S(1)} collective-permute-done((f32[72,128]{1,0:T(8,128)S(1)}, f32[72,128]{1,0:T(8,128)S(1)}, u32[]{:S(2)}, u32[]{:S(2)}) %collective-permute-start.7) | collective-permute-done | bytes 36896 | tf_op jit(solution)/shard_map/filter_y/ppermute | solution.py:246
  58.3 5.7 %collective-permute-start.10 = (f32[72,128]{1,0:T(8,128)S(1)}, f32[72,128]{1,0:T(8,128)S(1)}, u32[]{:S(2)}, u32[]{:S(2)}) collective-permute-start(f32[72,128]{1,0:T(8,128)S(1)} %add_add_fusion.1), channel_id=1, source_target_pairs={{0,24},{1,25},{2,26},{3,27},{4,28},{5,29},{6,30},{7,31},{8,0},{9,1... | collective-permute-start | bytes 110600 | tf_op jit(solution)/shard_map/filter_z/ppermute | solution.py:246
  64.0 2.0 %collective-permute-start.8 = (f32[72,128]{1,0:T(8,128)S(1)}, f32[72,128]{1,0:T(8,128)S(1)}, u32[]{:S(2)}, u32[]{:S(2)}) collective-permute-start(f32[72,128]{1,0:T(8,128)S(1)} %add_add_fusion.1), channel_id=1, source_target_pairs={{0,16},{1,17},{2,18},{3,19},{4,20},{5,21},{6,22},{7,23},{8,24},{9,... | collective-permute-start | bytes 110600 | tf_op jit(solution)/shard_map/filter_z/ppermute | solution.py:246
  65.9 1.9 %collective-permute-start.9 = (f32[72,128]{1,0:T(8,128)S(1)}, f32[72,128]{1,0:T(8,128)S(1)}, u32[]{:S(2)}, u32[]{:S(2)}) collective-permute-start(f32[72,128]{1,0:T(8,128)S(1)} %add_add_fusion.1), channel_id=1, source_target_pairs={{0,8},{1,9},{2,10},{3,11},{4,12},{5,13},{6,14},{7,15},{8,16},{9,17... | collective-permute-start | bytes 110600 | tf_op jit(solution)/shard_map/filter_z/ppermute | solution.py:246
  67.8 4.2 %all-to-all-start.2 = ((bf16[8,64,128]{2,1,0:T(8,128)(2,1)}), bf16[8,64,128]{2,1,0:T(8,128)(2,1)S(1)}, u32[]{:S(2)}, u32[]{:S(2)}) async-start(bf16[8,64,128]{2,1,0:T(8,128)(2,1)} %bitcast.5), calls=%async_computation.2 | async-start | bytes 262144 | tf_op jit(solution)/shard_map/input_grad/all_to_all | solution.py:235
  72.0 0.2 collective-permute-done.9
  72.2 0.1 collective-permute-start.11
  72.3 1.2 %collective-permute-done.11.other_ref = f32[72,128]{1,0:T(8,128)S(1)} collective-permute-done((f32[72,128]{1,0:T(8,128)S(1)}, f32[72,128]{1,0:T(8,128)S(1)}, u32[]{:S(2)}, u32[]{:S(2)}) %collective-permute-start.11) | collective-permute-done | bytes 36896 | tf_op jit(solution)/shard_map/filter_out/ppermute | solution.py:256
  73.5 0.9 %filter_out.1 = f32[2,9,32,32]{3,2,1,0:T(8,128)} custom-call(f32[72,128]{1,0:T(8,128)S(1)} %add_add_fusion.own_ref, f32[72,128]{1,0:T(8,128)S(1)} %collective-permute-done.11.other_ref), custom_call_target="tpu_custom_call" | custom-call | flops 1000 | bytes 6000000 | tf_op jit(solution)/shard_map/filter_out/pallas_call | solution.py:257
  74.4 4.3 %all-to-all-done.2 = bf16[8,64,128]{2,1,0:T(8,128)(2,1)S(1)} async-done(((bf16[8,64,128]{2,1,0:T(8,128)(2,1)}), bf16[8,64,128]{2,1,0:T(8,128)(2,1)S(1)}, u32[]{:S(2)}, u32[]{:S(2)}) %all-to-all-start.2) | async-done | bytes 131104 | tf_op jit(solution)/shard_map/input_grad/all_to_all | solution.py:235
  78.7 1.0 %input_grad.3 = bf16[512,128]{1,0:T(8,128)(2,1)} custom-call(bf16[512,128]{1,0:T(8,128)(2,1)S(1)} %bitcast.13), custom_call_target="tpu_custom_call" | custom-call | flops 67108864 | bytes 6000000 | tf_op jit(solution)/shard_map/input_grad/pallas_call | solution.py:236
  (11 shorter events, 0.1 us)
Async XLA Ops:
  0.6 0.9 %copy-start = (bf16[64,8,128]{2,1,0:T(8,128)(2,1)S(1)}, bf16[64,8,128]{2,1,0:T(8,128)(2,1)}, u32[]{:S(2)}) copy-start(bf16[64,8,128]{2,1,0:T(8,128)(2,1)} %param.4) | copy-start | bytes 393220
  1.5 0.9 %copy-start.1 = (bf16[64,8,128]{2,1,0:T(8,128)(2,1)S(1)}, bf16[64,8,128]{2,1,0:T(8,128)(2,1)}, u32[]{:S(2)}) copy-start(bf16[64,8,128]{2,1,0:T(8,128)(2,1)} %param.5) | copy-start | bytes 393220
  3.6 12.9 %all-to-all-start = ((bf16[8,128,128]{2,1,0:T(8,128)(2,1)}), bf16[8,128,128]{2,1,0:T(8,128)(2,1)S(1)}, u32[]{:S(2)}, u32[]{:S(2)}) async-start(bf16[8,128,128]{2,1,0:T(8,128)(2,1)} %to_rows.1), calls=%async_computation | async-start | bytes 524288 | tf_op jit(solution)/shard_map/to_rows/all_to_all | solution.py:191
  9.2 1.2 %slice-start = ((bf16[16,9,32,32]{3,2,1,0:T(8,128)(2,1)}), bf16[15,9,32,32]{3,2,1,0:T(8,128)(2,1)S(1)}, s32[]{:S(2)}) async-start(bf16[16,9,32,32]{3,2,1,0:T(8,128)(2,1)} %param.6), calls=%async_computation.3 | async-start | bytes 2211840 | tf_op jit(solution)/shard_map/weights/slice | solution.py:194
  9.2 1.4 %slice-start.1 = ((bf16[16,9,32,32]{3,2,1,0:T(8,128)(2,1)}), bf16[1,9,32,32]{3,2,1,0:T(8,128)(2,1)S(1)}, s32[]{:S(2)}) async-start(bf16[16,9,32,32]{3,2,1,0:T(8,128)(2,1)} %param.6), calls=%async_computation.4 | async-start | bytes 147456 | tf_op jit(solution)/shard_map/weights/slice | solution.py:194
  11.9 1.3 %copy-start.2 = (bf16[16,9,32,32]{3,2,1,0:T(8,128)(2,1)S(1)}, bf16[16,9,32,32]{3,2,1,0:T(8,128)(2,1)}, u32[]{:S(2)}) copy-start(bf16[16,9,32,32]{3,2,1,0:T(8,128)(2,1)} %param.6) | copy-start | bytes 884740
  13.6 2.9 %copy-start.3 = (f32[32]{0:T(128)S(1)}, f32[32]{0:T(128)}, u32[]{:S(2)}) copy-start(f32[32]{0:T(128)} %param.7) | copy-start | bytes 388
  16.6 7.3 %collective-permute-start = (bf16[512,128]{1,0:T(8,128)(2,1)S(1)}, bf16[512,128]{1,0:T(8,128)(2,1)S(1)}, u32[]{:S(2)}, u32[]{:S(2)}) collective-permute-start(bf16[512,128]{1,0:T(8,128)(2,1)S(1)} %bitcast.17), channel_id=1, source_target_pairs={{0,64},{64,128},{128,192},{192,224},{224,160},{160,96},{96,32},{32... | collective-permute-start | bytes 393224 | tf_op jit(solution)/shard_map/input_rows/ppermute | solution.py:208
  19.0 6.9 %collective-permute-start.1 = (bf16[512,128]{1,0:T(8,128)(2,1)S(1)}, bf16[512,128]{1,0:T(8,128)(2,1)S(1)}, u32[]{:S(2)}, u32[]{:S(2)}) collective-permute-start(bf16[512,128]{1,0:T(8,128)(2,1)S(1)} %bitcast.18), channel_id=1, source_target_pairs={{64,0},{128,64},{192,128},{224,192},{160,224},{96,160},{32,96},{1,... | collective-permute-start | bytes 393224 | tf_op jit(solution)/shard_map/input_rows/ppermute | solution.py:209
  30.3 1.7 %collective-permute-start.2 = (f32[8,72,128]{2,1,0:T(8,128)S(1)}, f32[8,72,128]{2,1,0:T(8,128)S(1)}, u32[]{:S(2)}, u32[]{:S(2)}) collective-permute-start(f32[8,72,128]{2,1,0:T(8,128)S(1)} %get-tuple-element.15), channel_id=1, source_target_pairs={{0,1},{1,0},{2,3},{3,2},{4,5},{5,4},{6,7},{7,6},{8,9},{9,8},{10,11... | collective-permute-start | bytes 884744 | tf_op jit(solution)/shard_map/filter_core/ppermute | solution.py:221
  32.7 18.4 %all-to-all-start.1 = ((f32[8,72,128]{2,1,0:T(8,128)}), f32[8,72,128]{2,1,0:T(8,128)S(1)}, u32[]{:S(2)}, u32[]{:S(2)}) async-start(f32[8,72,128]{2,1,0:T(8,128)} %add.21), calls=%async_computation.1 | async-start | bytes 589824 | tf_op jit(solution)/shard_map/filter_rot/all_to_all | solution.py:223
  38.3 7.7 %collective-permute-start.3 = (bf16[512,128]{1,0:T(8,128)(2,1)S(1)}, bf16[512,128]{1,0:T(8,128)(2,1)S(1)}, u32[]{:S(2)}, u32[]{:S(2)}) collective-permute-start(bf16[512,128]{1,0:T(8,128)(2,1)S(1)} %get-tuple-element.16.own_ref), channel_id=1, source_target_pairs={{0,64},{64,128},{128,192},{192,224},{224,160},{160,96},{96,32},{32... | collective-permute-start | bytes 393224 | tf_op jit(solution)/shard_map/grad_rows/ppermute | solution.py:225
  42.2 6.9 %collective-permute-start.4 = (bf16[512,128]{1,0:T(8,128)(2,1)S(1)}, bf16[512,128]{1,0:T(8,128)(2,1)S(1)}, u32[]{:S(2)}, u32[]{:S(2)}) collective-permute-start(bf16[512,128]{1,0:T(8,128)(2,1)S(1)} %get-tuple-element.16.own_ref), channel_id=1, source_target_pairs={{64,0},{128,64},{192,128},{224,192},{160,224},{96,160},{32,96},{1,... | collective-permute-start | bytes 393224 | tf_op jit(solution)/shard_map/grad_rows/ppermute | solution.py:226
  51.2 5.5 %collective-permute-start.5 = (f32[72,128]{1,0:T(8,128)S(1)}, f32[72,128]{1,0:T(8,128)S(1)}, u32[]{:S(2)}, u32[]{:S(2)}) collective-permute-start(f32[72,128]{1,0:T(8,128)S(1)} %reduce_sum.9), channel_id=1, source_target_pairs={{0,4},{1,5},{2,6},{3,7},{4,0},{5,1},{6,2},{7,3},{8,12},{9,13},{10,... | collective-permute-start | bytes 110600 | tf_op jit(solution)/shard_map/filter_y/ppermute | solution.py:246
  51.3 5.5 %collective-permute-start.6 = (f32[72,128]{1,0:T(8,128)S(1)}, f32[72,128]{1,0:T(8,128)S(1)}, u32[]{:S(2)}, u32[]{:S(2)}) collective-permute-start(f32[72,128]{1,0:T(8,128)S(1)} %reduce_sum.9), channel_id=1, source_target_pairs={{0,2},{1,3},{2,4},{3,5},{4,6},{5,7},{6,0},{7,1},{8,10},{9,11},{10,... | collective-permute-start | bytes 110600 | tf_op jit(solution)/shard_map/filter_y/ppermute | solution.py:246
  53.1 5.2 %collective-permute-start.7 = (f32[72,128]{1,0:T(8,128)S(1)}, f32[72,128]{1,0:T(8,128)S(1)}, u32[]{:S(2)}, u32[]{:S(2)}) collective-permute-start(f32[72,128]{1,0:T(8,128)S(1)} %reduce_sum.9), channel_id=1, source_target_pairs={{0,6},{1,7},{2,0},{3,1},{4,2},{5,3},{6,4},{7,5},{8,14},{9,15},{10,... | collective-permute-start | bytes 110600 | tf_op jit(solution)/shard_map/filter_y/ppermute | solution.py:246
  58.3 13.7 %collective-permute-start.10 = (f32[72,128]{1,0:T(8,128)S(1)}, f32[72,128]{1,0:T(8,128)S(1)}, u32[]{:S(2)}, u32[]{:S(2)}) collective-permute-start(f32[72,128]{1,0:T(8,128)S(1)} %add_add_fusion.1), channel_id=1, source_target_pairs={{0,24},{1,25},{2,26},{3,27},{4,28},{5,29},{6,30},{7,31},{8,0},{9,1... | collective-permute-start | bytes 110600 | tf_op jit(solution)/shard_map/filter_z/ppermute | solution.py:246
  64.0 8.1 %collective-permute-start.8 = (f32[72,128]{1,0:T(8,128)S(1)}, f32[72,128]{1,0:T(8,128)S(1)}, u32[]{:S(2)}, u32[]{:S(2)}) collective-permute-start(f32[72,128]{1,0:T(8,128)S(1)} %add_add_fusion.1), channel_id=1, source_target_pairs={{0,16},{1,17},{2,18},{3,19},{4,20},{5,21},{6,22},{7,23},{8,24},{9,... | collective-permute-start | bytes 110600 | tf_op jit(solution)/shard_map/filter_z/ppermute | solution.py:246
  65.9 6.3 %collective-permute-start.9 = (f32[72,128]{1,0:T(8,128)S(1)}, f32[72,128]{1,0:T(8,128)S(1)}, u32[]{:S(2)}, u32[]{:S(2)}) collective-permute-start(f32[72,128]{1,0:T(8,128)S(1)} %add_add_fusion.1), channel_id=1, source_target_pairs={{0,8},{1,9},{2,10},{3,11},{4,12},{5,13},{6,14},{7,15},{8,16},{9,17... | collective-permute-start | bytes 110600 | tf_op jit(solution)/shard_map/filter_z/ppermute | solution.py:246
  67.8 10.9 %all-to-all-start.2 = ((bf16[8,64,128]{2,1,0:T(8,128)(2,1)}), bf16[8,64,128]{2,1,0:T(8,128)(2,1)S(1)}, u32[]{:S(2)}, u32[]{:S(2)}) async-start(bf16[8,64,128]{2,1,0:T(8,128)(2,1)} %bitcast.5), calls=%async_computation.2 | async-start | bytes 262144 | tf_op jit(solution)/shard_map/input_grad/all_to_all | solution.py:235
  72.2 1.3 %collective-permute-start.11 = (f32[72,128]{1,0:T(8,128)S(1)}, f32[72,128]{1,0:T(8,128)S(1)}, u32[]{:S(2)}, u32[]{:S(2)}) collective-permute-start(f32[72,128]{1,0:T(8,128)S(1)} %add_add_fusion.own_ref), channel_id=1, source_target_pairs={{0,1},{1,0},{2,3},{3,2},{4,5},{5,4},{6,7},{7,6},{8,9},{9,8},{10,11... | collective-permute-start | bytes 110600 | tf_op jit(solution)/shard_map/filter_out/ppermute | solution.py:256

commit v3 on v2

v3 whole, which is shorter than its diff:
```python
import functools

import jax
import jax.numpy as jnp
from jax import lax
from jax.experimental import pallas as pl
from jax.experimental.pallas import tpu as pltpu
from jax.sharding import PartitionSpec as P

CH = 32
HALO = 2
F32 = jnp.float32
BF16 = jnp.bfloat16


def lanes(shape):
    return lax.broadcasted_iota(jnp.int32, shape, len(shape) - 1)


def spread(src, dst):
    n = src.shape[2]
    for a in range(3):
        for b in range(3):
            v = src[3 * a + b]
            for fine in range(4):
                t = v
                if fine:
                    cut = n - CH * fine
                    t = jnp.concatenate([v[:, cut:], v[:, :cut]], axis=1)
                for coarse in range(n // 128):
                    u = t
                    if coarse:
                        cut = n - 128 * coarse
                        u = jnp.concatenate([t[:, cut:], t[:, :cut]], axis=1)
                    row = b * n + CH * (4 * coarse + fine)
                    dst[row : row + CH, a * n : (a + 1) * n] = u


def exchanged(v, band, forth):
    n = v.shape[0]
    i = lax.broadcasted_iota(jnp.int32, (n, n), 0)
    j = lax.broadcasted_iota(jnp.int32, (n, n), 1)
    if forth:
        i, j = j, i
    one = (i // band == j % (n // band)) & (i % band == j // (n // band))
    return jnp.dot(one.astype(BF16), v, preferred_element_type=F32).astype(BF16)


def turn_kernel(band, x_hbm, c_hbm, tile_ref, far_ref, near_ref, held, sems):
    width = tile_ref.shape[2]
    half = tile_ref.shape[1] // 2
    copies = [pltpu.make_async_copy(src, held.at[i], sems.at[i]) for i, src in enumerate((x_hbm, c_hbm))]
    for copy in copies:
        copy.start()
    upper = lax.axis_index("rows") % 2 == 1
    for part, copy in enumerate(copies):
        copy.wait()
        t = exchanged(held[part], band, True).reshape(band, half, width)
        spot = slice(part * half, (part + 1) * half)
        tile_ref[:, spot] = t
        first, last = t[:HALO], t[band - HALO :]
        for ref, end in ((far_ref, upper), (near_ref, ~upper)):

            @pl.when(end)
            def _():
                ref[:, spot] = last

            @pl.when(~end)
            def _():
                ref[:, spot] = first


def pack_kernel(cols, tile_ref, far_ref, near_ref, out_ref, edge_ref):
    groups = out_ref.shape[0]
    band, both, width = tile_ref.shape
    pitch = cols + 2 * HALO
    lane = lanes((both, width))
    upper = lax.axis_index("rows") % 2
    for c in range(2):

        @pl.when(upper == c)
        def _():
            edge_ref[:HALO] = (near_ref if c else far_ref)[...]
            edge_ref[HALO:] = (far_ref if c else near_ref)[...]

    for j in range(groups):
        parts = [jnp.zeros((both, width), BF16) for _ in range(2)]
        for r in range(band + 2 * HALO):
            if r < HALO:
                v = edge_ref[r]
            elif r < HALO + band:
                v = tile_ref[r - HALO]
            else:
                v = edge_ref[r - band]
            low = pitch * r + max(HALO - cols * j, 0)
            high = pitch * r + min(pitch, width + HALO - cols * j)
            moved = pltpu.roll(v, (pitch * r - cols * j + HALO) % width, 1)
            for h in range(2):
                if low < width * (h + 1) and high > width * h:
                    ok = (lane >= low - width * h) & (lane < high - width * h)
                    parts[h] = jnp.where(ok, moved, parts[h])
        for h in range(2):
            out_ref[j, :, width * h : width * (h + 1)] = parts[h]


def inside(size, band, cols, ring):
    pitch = cols + 2 * HALO
    lane = lanes((1, size))
    row, col = lane // pitch, lane % pitch
    edge = HALO - ring
    return (row >= edge) & (row < band + 2 * HALO - edge) & (col >= edge) & (col < pitch - edge)


def rows_turned(v, by):
    by = by % v.shape[0]
    return jnp.concatenate([v[by:], v[:by]], axis=0) if by else v


def grad_kernel(band, cols, recv_ref, f_ref, bias_ref, g_ref, keep_ref, give_ref, x2_ref, w_ref):
    groups, both, size = recv_ref.shape
    half = both // 2
    n = groups * half
    rot = n // CH
    pitch = cols + 2 * HALO
    x = recv_ref[:, :half, :].reshape(n, size)
    cot = recv_ref[:, half:, :].reshape(n, size)
    x2_ref[:n] = x
    x2_ref[n:] = x
    spread(f_ref, w_ref)
    x3 = jnp.concatenate([pltpu.roll(x, pitch, 1), x, pltpu.roll(x, size - pitch, 1)], axis=0)
    parts = [
        jnp.dot(w_ref[b * n : (b + 1) * n, :], x3, preferred_element_type=F32) for b in range(3)
    ]
    bias = jnp.concatenate([bias_ref[...]] * rot, axis=0)
    pre = parts[1] + pltpu.roll(parts[0], 1, 1) + pltpu.roll(parts[2], size - 1, 1) + bias
    sigma = jax.nn.sigmoid(pre)
    grad = cot.astype(F32) * sigma * (1.0 + pre * (1.0 - sigma))
    grad = jnp.where(inside(size, band, cols, 1), grad, 0.0)
    g_ref[...] = grad.astype(BF16)
    own = jnp.where(inside(size, band, cols, 0), grad, 0.0).astype(BF16)
    moved = [
        pltpu.roll(own, (pitch * (a - 1) + b - 1) % size, 1) if (a, b) != (1, 1) else own
        for a in range(3)
        for b in range(3)
    ]
    nt = (((1,), (1,)), ((), ()))
    total = None
    for r in range(rot):
        g8 = jnp.concatenate([t[CH * r : CH * (r + 1)] for t in moved[:8]], axis=0)
        d = lax.dot_general(x2_ref[CH * r : CH * r + n, :], g8, nt, preferred_element_type=F32)
        total = d if total is None else total + d
    lined = [None] * 4
    for m in range(rot // 8):
        d = lax.dot_general(
            x, moved[8][8 * CH * m : 8 * CH * (m + 1)], nt, preferred_element_type=F32
        )
        for v in range(2):
            for t in range(4):
                e = rows_turned(d[:, 128 * v : 128 * (v + 1)], CH * (8 * m + 4 * v + t))
                lined[t] = e if lined[t] is None else lined[t] + e
    last = lined[0]
    for t in range(1, 4):
        last = last + pltpu.roll(lined[t], 128 - CH * t, 1)
    split = last.reshape(groups, 2, 4, 8, 128)
    spots = lanes((groups * 2 * 8, 128)) // CH
    last = split[:, :, 0].reshape(-1, 128)
    for j in range(1, 4):
        last = jnp.where(spots == j, pltpu.roll(split[:, :, j].reshape(-1, 128), CH * j, 1), last)
    last = last.reshape(groups, 2, 8, 128)
    one = total[:, :128].reshape(groups, 2, CH, 128)
    two = total[:, 128:].reshape(groups, 2, CH, 128)
    core = lax.axis_index("rows") % 2
    for c in range(2):

        @pl.when(core == c)
        def _():
            for ref, part in ((keep_ref, c), (give_ref, 1 - c)):
                ref[:, :CH] = one[:, part]
                ref[:, CH : 2 * CH] = two[:, part]
                ref[:, 2 * CH :] = last[:, part]


def input_kernel(band, cols, g_ref, f_ref, out_ref, w_ref):
    n, size = g_ref.shape
    pitch = cols + 2 * HALO
    spread(f_ref, w_ref)
    g = g_ref[...]
    g3 = jnp.concatenate([pltpu.roll(g, size - pitch, 1), g, pltpu.roll(g, pitch, 1)], axis=0)
    parts = [
        jnp.dot(w_ref[b * n : (b + 1) * n, :], g3, preferred_element_type=F32) for b in range(3)
    ]
    grad = parts[1] + pltpu.roll(parts[0], size - 1, 1) + pltpu.roll(parts[2], 1, 1)
    grad = grad.astype(BF16)
    width = out_ref.shape[1]
    lane = lanes((n, width))
    out = jnp.zeros((n, width), BF16)
    for r in range(band):
        at = pitch * (r + HALO) + HALO
        for h in range(size // width):
            low, high = max(at, width * h), min(at + cols, width * (h + 1))
            if low < high:
                piece = pltpu.roll(grad[:, width * h : width * (h + 1)], (cols * r - at) % width, 1)
                low, high = low - at + cols * r, high - at + cols * r
                out = jnp.where((lane >= low) & (lane < high), piece, out)
    out_ref[...] = out


def join_kernel(keep_ref, other_ref, dx_ref, out_ref):
    groups, terms, width = keep_ref.shape
    local = dx_ref.shape[1]
    out_ref[:, :local] = dx_ref[...]
    sums = keep_ref[...] + other_ref[...]
    pad = jnp.zeros((groups, out_ref.shape[1] - local - terms, width), F32)
    out_ref[:, local:] = jnp.concatenate([sums, pad], axis=1).astype(BF16)


def unpack_kernel(band, cols, dx_ref, out_ref):
    groups, local, width = dx_ref.shape
    lane = lanes((local, width))
    rows = []
    for r in range(band):
        out = jnp.zeros((local, width), BF16)
        for j in range(groups):
            piece = pltpu.roll(dx_ref[j], (cols * (j - r)) % width, 1)
            out = jnp.where((lane >= cols * j) & (lane < cols * (j + 1)), piece, out)
        rows.append(out)
    out_ref[...] = exchanged(jnp.concatenate(rows, axis=0), band, False)


def out_kernel(scale, own_ref, other_ref, out_ref):
    core = lax.axis_index("rows") % 2
    for c in range(2):

        @pl.when(core == c)
        def _():
            for ref, part in ((own_ref, c), (other_ref, 1 - c)):
                v = ref[...] * scale
                for row in range(2):
                    t = v[CH * row : CH * (row + 1)].T
                    for b in range(4):
                        out_ref[part, 4 * row + b] = t[CH * b : CH * (b + 1)]
                e = v[2 * CH :]
                e = jnp.concatenate([e[:, CH * j : CH * (j + 1)] for j in range(4)], axis=0)
                out_ref[part, 8] = e.T


def shaped(shape, dtype):
    return jax.ShapeDtypeStruct(shape, dtype)


def call(kernel, outs, flops, scratch=(), limit=24, **specs):
    return pl.pallas_call(
        kernel,
        out_shape=outs,
        scratch_shapes=list(scratch),
        **specs,
        compiler_params=pltpu.CompilerParams(vmem_limit_bytes=limit * 1024 * 1024),
        cost_estimate=pl.CostEstimate(flops=flops, bytes_accessed=2_000_000, transcendentals=0),
    )


def shards(inputs, cotangent, filters, bias):
    local, band, width = inputs.shape
    rotations, taps = filters.shape[:2]
    n = rotations * CH
    groups = lax.axis_size("rot")
    bands = lax.axis_size("rows")
    cols = width // groups
    size = 2 * width
    across = [(i, j) for i in range(1, bands - 1, 2) for i, j in ((i, i + 1), (i + 1, i))]
    swap = [(i, i ^ 1) for i in range(bands)]
    square = pltpu.VMEM((3 * n, 3 * n), BF16)

    with jax.named_scope("edge_rows"):
        edge = shaped((HALO, 2 * local, width), BF16)
        tile, far, near = call(
            functools.partial(turn_kernel, band),
            (shaped((band, 2 * local, width), BF16), edge, edge),
            4 * n * n * width,
            [pltpu.VMEM((2, n, width), BF16), pltpu.SemaphoreType.DMA((2,))],
            in_specs=[pl.BlockSpec(memory_space=pltpu.HBM)] * 2,
            limit=60,
        )(inputs.reshape(n, width), cotangent.reshape(n, width))
        far = lax.ppermute(far, "rows", across)
        near = lax.ppermute(near, "rows", swap)
    with jax.named_scope("to_tiles"):
        packed = call(
            functools.partial(pack_kernel, cols),
            shaped((groups, 2 * local, size), BF16),
            1000,
            [pltpu.VMEM((2 * HALO, 2 * local, width), BF16)],
            limit=60,
        )(tile, far, near)
        recv = lax.all_to_all(packed, "rot", 0, 0, tiled=True)
    with jax.named_scope("weights"):
        fwd = jnp.transpose(filters, (1, 2, 0, 3)).reshape(taps, CH, n)
        back = jnp.concatenate([filters[:1], filters[:0:-1]], axis=0)
        bwd = jnp.transpose(back, (1, 3, 0, 2)).reshape(taps, CH, n)
        bias2 = jnp.broadcast_to(bias[:, None], (CH, size))
        recv, fwd, bwd, bias2 = lax.optimization_barrier((recv, fwd, bwd, bias2))
    with jax.named_scope("grad"):
        half = shaped((groups, 9 * 8, 4 * CH), F32)
        g, keep, give = call(
            functools.partial(grad_kernel, band, cols),
            (shaped((n, size), BF16), half, half),
            2 * 18 * n * n * size,
            [pltpu.VMEM((2 * n, size), BF16), square],
        )(recv, fwd, bias2)
    def turn(i, step, s):
        now = i // step % 4
        return i + ((now + s) % 4 - now) * step

    def add_four(v, step):
        p1, p2, p3 = [
            lax.ppermute(v, "rows", [(i, turn(i, step, s)) for i in range(bands)]) for s in (1, 2, 3)
        ]
        return (v + p2) + (p1 + p3)

    with jax.named_scope("filter_core"):
        other = lax.ppermute(give, "rows", swap)
    with jax.named_scope("input_grad"):
        dx = call(
            functools.partial(input_kernel, band, cols),
            shaped((n, width), BF16),
            2 * 9 * n * n * size,
            [square],
        )(g, bwd)
    with jax.named_scope("to_channels"):
        terms = keep.shape[1]
        block = local + -(-terms // 16) * 16
        sent = call(join_kernel, shaped((groups, block, width), BF16), 1000)(
            keep, other, dx.reshape(groups, local, width)
        )
        got = lax.all_to_all(sent, "rot", 0, 0, tiled=True)
    with jax.named_scope("filter_rot"):
        v = jnp.sum(got[:, local : local + terms].astype(F32), axis=0)
    with jax.named_scope("input_grad"):
        input_grad = call(
            functools.partial(unpack_kernel, band, cols), shaped((n, width), BF16), 2 * n * n * width
        )(got[:, :local]).reshape(inputs.shape)
    with jax.named_scope("filter_y"):
        v = add_four(v, 2)
    with jax.named_scope("filter_z"):
        v = add_four(v, 8)
    with jax.named_scope("filter_out"):
        scale = float(rotations * band * bands * width) ** (-0.5)
        other = lax.ppermute(v, "rows", swap)
        filter_grad = call(
            functools.partial(out_kernel, scale), shaped((2, taps, CH, CH), F32), 1000
        )(v, other)
    return input_grad, filter_grad


def solution(mesh):
    return jax.shard_map(
        shards,
        mesh=mesh,
        in_specs=(P("rot", "rows", None), P("rot", "rows", None), P(), P()),
        out_specs=(P("rot", "rows", None), P("rot", None, None, None)),
        check_vma=False,
    )
```

time: 80.2 us -> 72.2 us (0.900)
  the two profiles are of different devices: /device:TPU:24 before, /device:TPU:1 now
where the time goes in v3:
time: 72.2 us; the launch traced here: 71.8 us
  starting transfers between devices  31.3 us (43%)
  Pallas kernels  14 us (19%)
  waiting for transfers between devices  9.82 us (14%)
  blocking collectives  9.74 us (13%)
  local copies, waits for them, and re-layouts  5.93 us (8%)
  between operations  0.78 us (1%)
    ppermute x6, starting transfers between devices, add_four(): lax.ppermute(v, 'rows', [(i, turn(i, step, s)) for i in range(bands)])  16.6 us
    all_to_all x1, blocking collectives, shards(): got = lax.all_to_all(sent, 'rot', 0, 0, tiled=True)  9.74 us
    all_to_all x1, starting transfers between devices, shards(): recv = lax.all_to_all(packed, 'rot', 0, 0, tiled=True)  5.37 us
    all_to_all x1, waiting for transfers between devices, shards(): recv = lax.all_to_all(packed, 'rot', 0, 0, tiled=True)  4.89 us
    pallas_call x1, Pallas kernels, shards(): call(functools.partial(grad_kernel, band, cols), (shaped((n, size), BF16)...  4.84 us
    ppermute x1, starting transfers between devices, shards(): far = lax.ppermute(far, 'rows', across)  4.6 us
    ppermute x1, starting transfers between devices, shards(): other = lax.ppermute(v, 'rows', swap)  3.92 us
    ppermute x6, waiting for transfers between devices, add_four(): lax.ppermute(v, 'rows', [(i, turn(i, step, s)) for i in range(bands)])  2.88 us
  transfers between devices with their start and end apart: 11, of which 4 were waited for; matrix products, arithmetic and copies ran while one was open for 6% of the time, Pallas kernels for 4%

profile of v3, /device:TPU:1, one launch (start us, length us, event | category | flops | bytes accessed | tf_op | source)
XLA Modules:
  0.0 71.8 jit_solution(1257678188256301428)
XLA Ops:
  0.6 2.5 %edge_rows.1 = (bf16[8,128,128]{2,1,0:T(8,128)(2,1)}, bf16[2,128,128]{2,1,0:T(8,128)(2,1)}, bf16[2,128,128]{2,1,0:T(8,128)(2,1)}) custom-call(bf16[512,128]{1,0:T(8,128)(2,1)} %bitcast.14, bf16[512,128]{1,0:T(8,128)(2,1)} %bitcast.15), custom_call_target="tpu_custom_call" | custom-call | flops 134217728 | bytes 2000000 | tf_op jit(solution)/shard_map/edge_rows/pallas_call | solution.py:276
  3.1 4.6 %collective-permute-start = (bf16[2,128,128]{2,1,0:T(8,128)(2,1)}, bf16[2,128,128]{2,1,0:T(8,128)(2,1)S(1)}, u32[]{:S(2)}, u32[]{:S(2)}) collective-permute-start(bf16[2,128,128]{2,1,0:T(8,128)(2,1)} %get-tuple-element.13), channel_id=1, source_target_pairs={{1,2},{2,1},{3,4},{4,3},{5,6},{6,5},{7,8},{8,7},{9,10},{10,9},{11,... | collective-permute-start | bytes 196616 | tf_op jit(solution)/shard_map/edge_rows/ppermute | solution.py:284
  7.7 0.1 collective-permute-start.1
  7.8 2.0 %collective-permute-done.far_ref = bf16[2,128,128]{2,1,0:T(8,128)(2,1)S(1)} collective-permute-done((bf16[2,128,128]{2,1,0:T(8,128)(2,1)}, bf16[2,128,128]{2,1,0:T(8,128)(2,1)S(1)}, u32[]{:S(2)}, u32[]{:S(2)}) %collective-permute-start) | collective-permute-done | bytes 65568 | tf_op jit(solution)/shard_map/edge_rows/ppermute | solution.py:284
  9.9 0.0 copy-start.1
  9.9 0.0 collective-permute-done.1.near_ref
  9.9 0.0 copy-start.2
  9.9 0.6 copy-done.1
  10.5 0.0 copy-done.2
  10.5 2.7 %to_tiles.1 = bf16[8,128,256]{2,1,0:T(8,128)(2,1)} custom-call(bf16[8,128,128]{2,1,0:T(8,128)(2,1)} %get-tuple-element.12.tile_ref, bf16[2,128,128]{2,1,0:T(8,128)(2,1)} %copy-done.1, bf16[2,128,128]{2,1,0:T(8,128)(2,1)} %copy-done.2), custom_call_target="tpu_custom_call" | custom-call | flops 1000 | bytes 2000000 | tf_op jit(solution)/shard_map/to_tiles/pallas_call | solution.py:287
  13.2 5.4 %all-to-all-start = ((bf16[8,128,256]{2,1,0:T(8,128)(2,1)}), bf16[8,128,256]{2,1,0:T(8,128)(2,1)S(1)}, u32[]{:S(2)}, u32[]{:S(2)}) async-start(bf16[8,128,256]{2,1,0:T(8,128)(2,1)} %to_tiles.1), calls=%async_computation | async-start | bytes 1048576 | tf_op jit(solution)/shard_map/to_tiles/all_to_all | solution.py:294
  18.6 0.0 slice-start
  18.6 0.0 slice-start.1
  18.6 1.2 %slice-done = bf16[15,9,32,32]{3,2,1,0:T(8,128)(2,1)S(1)} async-done(((bf16[16,9,32,32]{3,2,1,0:T(8,128)(2,1)}), bf16[15,9,32,32]{3,2,1,0:T(8,128)(2,1)S(1)}, s32[]{:S(2)}) %slice-start) | async-done | bytes 276504 | tf_op jit(solution)/shard_map/weights/slice | solution.py:297
  19.8 0.2 rev.3
  20.0 0.0 slice-done.1
  20.0 0.2 maximum_bitcast_fusion
  20.3 0.9 %copy.7 = bf16[9,32,16,32]{3,2,1,0:T(8,128)(2,1)S(1)} copy(bf16[9,32,16,32]{1,3,0,2:T(8,128)(2,1)S(1)} %maximum_bitcast_fusion) | data formatting | bytes 589824 | tf_op jit(solution)/shard_map/weights/transpose | solution.py:298
  21.2 0.0 copy-start
  21.2 1.1 %reshape.26.f_ref = bf16[9,32,512]{2,1,0:T(8,128)(2,1)S(1)} reshape(bf16[9,32,16,32]{3,2,1,0:T(8,128)(2,1)S(1)} %copy.7) | data formatting | bytes 589824 | tf_op jit(solution)/shard_map/weights/reshape | solution.py:298
  22.4 0.1 copy-done
  22.5 0.5 copy.6
  23.0 0.0 copy-start.3
  23.0 1.1 %reshape.25.f_ref = bf16[9,32,512]{2,1,0:T(8,128)(2,1)S(1)} reshape(bf16[9,32,16,32]{3,2,1,0:T(8,128)(2,1)S(1)} %copy.6) | data formatting | bytes 589824 | tf_op jit(solution)/shard_map/weights/reshape | solution.py:296
  24.1 4.9 %all-to-all-done.recv_ref = bf16[8,128,256]{2,1,0:T(8,128)(2,1)S(1)} async-done(((bf16[8,128,256]{2,1,0:T(8,128)(2,1)}), bf16[8,128,256]{2,1,0:T(8,128)(2,1)S(1)}, u32[]{:S(2)}, u32[]{:S(2)}) %all-to-all-start) | async-done | bytes 524320 | tf_op jit(solution)/shard_map/to_tiles/all_to_all | solution.py:294
  29.0 0.0 copy-done.3
  29.0 0.1 broadcast_in_dim.2.bias_ref
  29.1 4.8 %grad.1 = (bf16[512,256]{1,0:T(8,128)(2,1)S(1)}, f32[8,72,128]{2,1,0:T(8,128)S(1)}, f32[8,72,128]{2,1,0:T(8,128)S(1)}) custom-call(bf16[8,128,256]{2,1,0:T(8,128)(2,1)S(1)} %all-to-all-done.recv_ref, bf16[9,32,512]{2,1,0:T(8,128)(2,1)S(1)} %reshape.25.f_ref, f32[32,256]{1,0:T(8,128)S(1)} %broadcast_in_dim.2.bias_ref), custom_call_target="tpu_custom_call" | custom-call | flops 2415919104 | bytes 2000000 | tf_op jit(solution)/shard_map/grad/pallas_call | solution.py:303
  33.9 0.7 %collective-permute-start.2 = (f32[8,72,128]{2,1,0:T(8,128)S(1)}, f32[8,72,128]{2,1,0:T(8,128)S(1)}, u32[]{:S(2)}, u32[]{:S(2)}) collective-permute-start(f32[8,72,128]{2,1,0:T(8,128)S(1)} %get-tuple-element.19), channel_id=1, source_target_pairs={{0,1},{1,0},{2,3},{3,2},{4,5},{5,4},{6,7},{7,6},{8,9},{9,8},{10,11... | collective-permute-start | bytes 884744 | tf_op jit(solution)/shard_map/filter_core/ppermute | solution.py:320
  34.7 1.8 %input_grad.2 = bf16[512,128]{1,0:T(8,128)(2,1)S(1)} custom-call(bf16[512,256]{1,0:T(8,128)(2,1)S(1)} %get-tuple-element.20.g_ref, bf16[9,32,512]{2,1,0:T(8,128)(2,1)S(1)} %reshape.26.f_ref), custom_call_target="tpu_custom_call" | custom-call | flops 1207959552 | bytes 2000000 | tf_op jit(solution)/shard_map/input_grad/pallas_call | solution.py:322
  36.5 0.0 collective-permute-done.2.other_ref
  36.5 9.7 %all_to_all.10 = bf16[8,144,128]{2,1,0:T(8,128)(2,1)S(1)} all-to-all(bf16[8,144,128]{2,1,0:T(8,128)(2,1)S(1)} %to_channels.1), channel_id=1, replica_groups=mesh['rot'=8,'rows'=32] {'rot'}, dimensions={0} | all-to-all | bytes 589824 | tf_op jit(solution)/shard_map/to_channels/all_to_all | solution.py:334
  46.3 3.4 %collective-permute-start.3 = (f32[72,128]{1,0:T(8,128)S(1)}, f32[72,128]{1,0:T(8,128)S(1)}, u32[]{:S(2)}, u32[]{:S(2)}) collective-permute-start(f32[72,128]{1,0:T(8,128)S(1)} %convert_reduce_fusion), channel_id=1, source_target_pairs={{0,4},{1,5},{2,6},{3,7},{4,0},{5,1},{6,2},{7,3},{8,12},{9,13},{10,... | collective-permute-start | bytes 110600 | tf_op jit(solution)/shard_map/filter_y/ppermute | solution.py:315
  49.7 0.8 %collective-permute-start.4 = (f32[72,128]{1,0:T(8,128)S(1)}, f32[72,128]{1,0:T(8,128)S(1)}, u32[]{:S(2)}, u32[]{:S(2)}) collective-permute-start(f32[72,128]{1,0:T(8,128)S(1)} %convert_reduce_fusion), channel_id=1, source_target_pairs={{0,2},{1,3},{2,4},{3,5},{4,6},{5,7},{6,0},{7,1},{8,10},{9,11},{10,... | collective-permute-start | bytes 110600 | tf_op jit(solution)/shard_map/filter_y/ppermute | solution.py:315
  50.5 1.9 %collective-permute-start.5 = (f32[72,128]{1,0:T(8,128)S(1)}, f32[72,128]{1,0:T(8,128)S(1)}, u32[]{:S(2)}, u32[]{:S(2)}) collective-permute-start(f32[72,128]{1,0:T(8,128)S(1)} %convert_reduce_fusion), channel_id=1, source_target_pairs={{0,6},{1,7},{2,0},{3,1},{4,2},{5,3},{6,4},{7,5},{8,14},{9,15},{10,... | collective-permute-start | bytes 110600 | tf_op jit(solution)/shard_map/filter_y/ppermute | solution.py:315
  52.4 0.0 collective-permute-done.3
  52.4 1.3 %collective-permute-done.4 = f32[72,128]{1,0:T(8,128)S(1)} collective-permute-done((f32[72,128]{1,0:T(8,128)S(1)}, f32[72,128]{1,0:T(8,128)S(1)}, u32[]{:S(2)}, u32[]{:S(2)}) %collective-permute-start.4) | collective-permute-done | bytes 36896 | tf_op jit(solution)/shard_map/filter_y/ppermute | solution.py:315
  53.7 0.0 collective-permute-done.5
  53.7 6.9 %collective-permute-start.6 = (f32[72,128]{1,0:T(8,128)S(1)}, f32[72,128]{1,0:T(8,128)S(1)}, u32[]{:S(2)}, u32[]{:S(2)}) collective-permute-start(f32[72,128]{1,0:T(8,128)S(1)} %add_add_fusion.1), channel_id=1, source_target_pairs={{0,16},{1,17},{2,18},{3,19},{4,20},{5,21},{6,22},{7,23},{8,24},{9,... | collective-permute-start | bytes 110600 | tf_op jit(solution)/shard_map/filter_z/ppermute | solution.py:315
  60.6 0.4 collective-permute-start.7
  61.0 3.2 %collective-permute-start.8 = (f32[72,128]{1,0:T(8,128)S(1)}, f32[72,128]{1,0:T(8,128)S(1)}, u32[]{:S(2)}, u32[]{:S(2)}) collective-permute-start(f32[72,128]{1,0:T(8,128)S(1)} %add_add_fusion.1), channel_id=1, source_target_pairs={{0,24},{1,25},{2,26},{3,27},{4,28},{5,29},{6,30},{7,31},{8,0},{9,1... | collective-permute-start | bytes 110600 | tf_op jit(solution)/shard_map/filter_z/ppermute | solution.py:315
  64.2 0.0 collective-permute-done.6
  64.2 1.5 %collective-permute-done.7 = f32[72,128]{1,0:T(8,128)S(1)} collective-permute-done((f32[72,128]{1,0:T(8,128)S(1)}, f32[72,128]{1,0:T(8,128)S(1)}, u32[]{:S(2)}, u32[]{:S(2)}) %collective-permute-start.7) | collective-permute-done | bytes 36896 | tf_op jit(solution)/shard_map/filter_z/ppermute | solution.py:315
  65.7 0.0 collective-permute-done.8
  65.8 3.9 %collective-permute-start.9 = (f32[72,128]{1,0:T(8,128)S(1)}, f32[72,128]{1,0:T(8,128)S(1)}, u32[]{:S(2)}, u32[]{:S(2)}) collective-permute-start(f32[72,128]{1,0:T(8,128)S(1)} %add_add_fusion.own_ref), channel_id=1, source_target_pairs={{0,1},{1,0},{2,3},{3,2},{4,5},{5,4},{6,7},{7,6},{8,9},{9,8},{10,11... | collective-permute-start | bytes 110600 | tf_op jit(solution)/shard_map/filter_out/ppermute | solution.py:347
  69.7 1.2 %input_grad.3 = bf16[512,128]{1,0:T(8,128)(2,1)} custom-call(bf16[8,64,128]{2,1,0:T(8,128)(2,1)S(1)} %slice.16.dx_ref), custom_call_target="tpu_custom_call" | custom-call | flops 67108864 | bytes 2000000 | tf_op jit(solution)/shard_map/input_grad/pallas_call | solution.py:338
  70.9 0.0 collective-permute-done.9.other_ref
  70.9 0.9 %filter_out.1 = f32[2,9,32,32]{3,2,1,0:T(8,128)} custom-call(f32[72,128]{1,0:T(8,128)S(1)} %add_add_fusion.own_ref, f32[72,128]{1,0:T(8,128)S(1)} %collective-permute-done.9.other_ref), custom_call_target="tpu_custom_call" | custom-call | flops 1000 | bytes 2000000 | tf_op jit(solution)/shard_map/filter_out/pallas_call | solution.py:348
  (5 shorter events, 0.1 us)
Async XLA Ops:
  3.1 6.8 %collective-permute-start = (bf16[2,128,128]{2,1,0:T(8,128)(2,1)}, bf16[2,128,128]{2,1,0:T(8,128)(2,1)S(1)}, u32[]{:S(2)}, u32[]{:S(2)}) collective-permute-start(bf16[2,128,128]{2,1,0:T(8,128)(2,1)} %get-tuple-element.13), channel_id=1, source_target_pairs={{1,2},{2,1},{3,4},{4,3},{5,6},{6,5},{7,8},{8,7},{9,10},{10,9},{11,... | collective-permute-start | bytes 196616 | tf_op jit(solution)/shard_map/edge_rows/ppermute | solution.py:284
  7.7 2.2 %collective-permute-start.1 = (bf16[2,128,128]{2,1,0:T(8,128)(2,1)}, bf16[2,128,128]{2,1,0:T(8,128)(2,1)S(1)}, u32[]{:S(2)}, u32[]{:S(2)}) collective-permute-start(bf16[2,128,128]{2,1,0:T(8,128)(2,1)} %get-tuple-element.14), channel_id=1, source_target_pairs={{0,1},{1,0},{2,3},{3,2},{4,5},{5,4},{6,7},{7,6},{8,9},{9,8},{10,11... | collective-permute-start | bytes 196616 | tf_op jit(solution)/shard_map/edge_rows/ppermute | solution.py:285
  9.9 0.6 copy-start.1
  9.9 0.6 copy-start.2
  13.2 15.8 %all-to-all-start = ((bf16[8,128,256]{2,1,0:T(8,128)(2,1)}), bf16[8,128,256]{2,1,0:T(8,128)(2,1)S(1)}, u32[]{:S(2)}, u32[]{:S(2)}) async-start(bf16[8,128,256]{2,1,0:T(8,128)(2,1)} %to_tiles.1), calls=%async_computation | async-start | bytes 1048576 | tf_op jit(solution)/shard_map/to_tiles/all_to_all | solution.py:294
  18.6 1.2 %slice-start = ((bf16[16,9,32,32]{3,2,1,0:T(8,128)(2,1)}), bf16[15,9,32,32]{3,2,1,0:T(8,128)(2,1)S(1)}, s32[]{:S(2)}) async-start(bf16[16,9,32,32]{3,2,1,0:T(8,128)(2,1)} %param.6), calls=%async_computation.2 | async-start | bytes 2211840 | tf_op jit(solution)/shard_map/weights/slice | solution.py:297
  18.6 1.4 %slice-start.1 = ((bf16[16,9,32,32]{3,2,1,0:T(8,128)(2,1)}), bf16[1,9,32,32]{3,2,1,0:T(8,128)(2,1)S(1)}, s32[]{:S(2)}) async-start(bf16[16,9,32,32]{3,2,1,0:T(8,128)(2,1)} %param.6), calls=%async_computation.3 | async-start | bytes 147456 | tf_op jit(solution)/shard_map/weights/slice | solution.py:297
  21.2 1.3 %copy-start = (bf16[16,9,32,32]{3,2,1,0:T(8,128)(2,1)S(1)}, bf16[16,9,32,32]{3,2,1,0:T(8,128)(2,1)}, u32[]{:S(2)}) copy-start(bf16[16,9,32,32]{3,2,1,0:T(8,128)(2,1)} %param.6) | copy-start | bytes 884740
  23.0 6.0 %copy-start.3 = (f32[32]{0:T(128)S(1)}, f32[32]{0:T(128)}, u32[]{:S(2)}) copy-start(f32[32]{0:T(128)} %param.7) | copy-start | bytes 388
  33.9 2.6 %collective-permute-start.2 = (f32[8,72,128]{2,1,0:T(8,128)S(1)}, f32[8,72,128]{2,1,0:T(8,128)S(1)}, u32[]{:S(2)}, u32[]{:S(2)}) collective-permute-start(f32[8,72,128]{2,1,0:T(8,128)S(1)} %get-tuple-element.19), channel_id=1, source_target_pairs={{0,1},{1,0},{2,3},{3,2},{4,5},{5,4},{6,7},{7,6},{8,9},{9,8},{10,11... | collective-permute-start | bytes 884744 | tf_op jit(solution)/shard_map/filter_core/ppermute | solution.py:320
  46.3 6.1 %collective-permute-start.3 = (f32[72,128]{1,0:T(8,128)S(1)}, f32[72,128]{1,0:T(8,128)S(1)}, u32[]{:S(2)}, u32[]{:S(2)}) collective-permute-start(f32[72,128]{1,0:T(8,128)S(1)} %convert_reduce_fusion), channel_id=1, source_target_pairs={{0,4},{1,5},{2,6},{3,7},{4,0},{5,1},{6,2},{7,3},{8,12},{9,13},{10,... | collective-permute-start | bytes 110600 | tf_op jit(solution)/shard_map/filter_y/ppermute | solution.py:315
  49.7 4.0 %collective-permute-start.4 = (f32[72,128]{1,0:T(8,128)S(1)}, f32[72,128]{1,0:T(8,128)S(1)}, u32[]{:S(2)}, u32[]{:S(2)}) collective-permute-start(f32[72,128]{1,0:T(8,128)S(1)} %convert_reduce_fusion), channel_id=1, source_target_pairs={{0,2},{1,3},{2,4},{3,5},{4,6},{5,7},{6,0},{7,1},{8,10},{9,11},{10,... | collective-permute-start | bytes 110600 | tf_op jit(solution)/shard_map/filter_y/ppermute | solution.py:315
  50.5 3.2 %collective-permute-start.5 = (f32[72,128]{1,0:T(8,128)S(1)}, f32[72,128]{1,0:T(8,128)S(1)}, u32[]{:S(2)}, u32[]{:S(2)}) collective-permute-start(f32[72,128]{1,0:T(8,128)S(1)} %convert_reduce_fusion), channel_id=1, source_target_pairs={{0,6},{1,7},{2,0},{3,1},{4,2},{5,3},{6,4},{7,5},{8,14},{9,15},{10,... | collective-permute-start | bytes 110600 | tf_op jit(solution)/shard_map/filter_y/ppermute | solution.py:315
  53.7 10.5 %collective-permute-start.6 = (f32[72,128]{1,0:T(8,128)S(1)}, f32[72,128]{1,0:T(8,128)S(1)}, u32[]{:S(2)}, u32[]{:S(2)}) collective-permute-start(f32[72,128]{1,0:T(8,128)S(1)} %add_add_fusion.1), channel_id=1, source_target_pairs={{0,16},{1,17},{2,18},{3,19},{4,20},{5,21},{6,22},{7,23},{8,24},{9,... | collective-permute-start | bytes 110600 | tf_op jit(solution)/shard_map/filter_z/ppermute | solution.py:315
  60.6 5.1 %collective-permute-start.7 = (f32[72,128]{1,0:T(8,128)S(1)}, f32[72,128]{1,0:T(8,128)S(1)}, u32[]{:S(2)}, u32[]{:S(2)}) collective-permute-start(f32[72,128]{1,0:T(8,128)S(1)} %add_add_fusion.1), channel_id=1, source_target_pairs={{0,8},{1,9},{2,10},{3,11},{4,12},{5,13},{6,14},{7,15},{8,16},{9,17... | collective-permute-start | bytes 110600 | tf_op jit(solution)/shard_map/filter_z/ppermute | solution.py:315
  61.0 4.7 %collective-permute-start.8 = (f32[72,128]{1,0:T(8,128)S(1)}, f32[72,128]{1,0:T(8,128)S(1)}, u32[]{:S(2)}, u32[]{:S(2)}) collective-permute-start(f32[72,128]{1,0:T(8,128)S(1)} %add_add_fusion.1), channel_id=1, source_target_pairs={{0,24},{1,25},{2,26},{3,27},{4,28},{5,29},{6,30},{7,31},{8,0},{9,1... | collective-permute-start | bytes 110600 | tf_op jit(solution)/shard_map/filter_z/ppermute | solution.py:315
  65.8 5.2 %collective-permute-start.9 = (f32[72,128]{1,0:T(8,128)S(1)}, f32[72,128]{1,0:T(8,128)S(1)}, u32[]{:S(2)}, u32[]{:S(2)}) collective-permute-start(f32[72,128]{1,0:T(8,128)S(1)} %add_add_fusion.own_ref), channel_id=1, source_target_pairs={{0,1},{1,0},{2,3},{3,2},{4,5},{5,4},{6,7},{7,6},{8,9},{9,8},{10,11... | collective-permute-start | bytes 110600 | tf_op jit(solution)/shard_map/filter_out/ppermute | solution.py:347

commit v4 on v3

--- a/solution.py
+++ b/solution.py
@@ -9,6 +9,7 @@
 
 CH = 32
 HALO = 2
+GROUP = 16
 F32 = jnp.float32
 BF16 = jnp.bfloat16
 
@@ -46,35 +47,53 @@
     return jnp.dot(one.astype(BF16), v, preferred_element_type=F32).astype(BF16)
 
 
-def turn_kernel(band, x_hbm, c_hbm, tile_ref, far_ref, near_ref, held, sems):
-    width = tile_ref.shape[2]
-    half = tile_ref.shape[1] // 2
-    copies = [pltpu.make_async_copy(src, held.at[i], sems.at[i]) for i, src in enumerate((x_hbm, c_hbm))]
-    for copy in copies:
-        copy.start()
-    upper = lax.axis_index("rows") % 2 == 1
-    for part, copy in enumerate(copies):
-        copy.wait()
-        t = exchanged(held[part], band, True).reshape(band, half, width)
-        spot = slice(part * half, (part + 1) * half)
-        tile_ref[:, spot] = t
-        first, last = t[:HALO], t[band - HALO :]
-        for ref, end in ((far_ref, upper), (near_ref, ~upper)):
-
-            @pl.when(end)
-            def _():
-                ref[:, spot] = last
-
-            @pl.when(~end)
-            def _():
-                ref[:, spot] = first
-
-
-def pack_kernel(cols, tile_ref, far_ref, near_ref, out_ref, edge_ref):
-    groups = out_ref.shape[0]
-    band, both, width = tile_ref.shape
+def place_row(parts, v, r, j, cols):
+    both, width = v.shape
     pitch = cols + 2 * HALO
     lane = lanes((both, width))
+    low = pitch * r + max(HALO - cols * j, 0)
+    high = pitch * r + min(pitch, width + HALO - cols * j)
+    moved = pltpu.roll(v, (pitch * r - cols * j + HALO) % width, 1)
+    for h in range(2):
+        if low < width * (h + 1) and high > width * h:
+            ok = (lane >= low - width * h) & (lane < high - width * h)
+            parts[h] = jnp.where(ok, moved, parts[h])
+
+
+def ends_kernel(band, x_ref, c_ref, far_ref, near_ref):
+    n, width = x_ref.shape
+    local = n // band
+    upper = (lax.axis_index("rows") % 2) * (band - HALO)
+    i = lax.broadcasted_iota(jnp.int32, (2 * HALO * local, n), 0)
+    j = lax.broadcasted_iota(jnp.int32, (2 * HALO * local, n), 1)
+    spot = i // local
+    row = spot % HALO + jnp.where(spot < HALO, upper, band - HALO - upper)
+    one = ((i % local == j // band) & (row == j % band)).astype(BF16)
+    for part, ref in enumerate((x_ref, c_ref)):
+        t = jnp.dot(one, ref[...], preferred_element_type=F32).astype(BF16)
+        t = t.reshape(2 * HALO, local, width)
+        far_ref[:, part * local : (part + 1) * local] = t[:HALO]
+        near_ref[:, part * local : (part + 1) * local] = t[HALO:]
+
+
+def own_kernel(band, cols, x_ref, c_ref, out_ref):
+    groups, both, size = out_ref.shape
+    width = size // 2
+    turned = [
+        exchanged(ref[...], band, True).reshape(band, both // 2, width) for ref in (x_ref, c_ref)
+    ]
+    rows = [jnp.concatenate([t[r] for t in turned], axis=0) for r in range(band)]
+    for j in range(groups):
+        parts = [jnp.zeros((both, width), BF16) for _ in range(2)]
+        for r in range(band):
+            place_row(parts, rows[r], r + HALO, j, cols)
+        for h in range(2):
+            out_ref[j, :, width * h : width * (h + 1)] = parts[h]
+
+
+def edge_kernel(band, cols, own_ref, far_ref, near_ref, out_ref, edge_ref):
+    groups, both, size = out_ref.shape
+    width = size // 2
     upper = lax.axis_index("rows") % 2
     for c in range(2):
 
@@ -84,21 +103,10 @@
             edge_ref[HALO:] = (far_ref if c else near_ref)[...]
 
     for j in range(groups):
-        parts = [jnp.zeros((both, width), BF16) for _ in range(2)]
-        for r in range(band + 2 * HALO):
-            if r < HALO:
-                v = edge_ref[r]
-            elif r < HALO + band:
-                v = tile_ref[r - HALO]
-            else:
-                v = edge_ref[r - band]
-            low = pitch * r + max(HALO - cols * j, 0)
-            high = pitch * r + min(pitch, width + HALO - cols * j)
-            moved = pltpu.roll(v, (pitch * r - cols * j + HALO) % width, 1)
-            for h in range(2):
-                if low < width * (h + 1) and high > width * h:
-                    ok = (lane >= low - width * h) & (lane < high - width * h)
-                    parts[h] = jnp.where(ok, moved, parts[h])
+        parts = [own_ref[j, :, width * h : width * (h + 1)] for h in range(2)]
+        for r in range(HALO):
+            place_row(parts, edge_ref[r], r, j, cols)
+            place_row(parts, edge_ref[HALO + r], r + HALO + band, j, cols)
         for h in range(2):
             out_ref[j, :, width * h : width * (h + 1)] = parts[h]
 
@@ -111,12 +119,11 @@
     return (row >= edge) & (row < band + 2 * HALO - edge) & (col >= edge) & (col < pitch - edge)
 
 
-def rows_turned(v, by):
-    by = by % v.shape[0]
-    return jnp.concatenate([v[by:], v[:by]], axis=0) if by else v
-
-
-def grad_kernel(band, cols, recv_ref, f_ref, bias_ref, g_ref, keep_ref, give_ref, x2_ref, w_ref):
+def lanes_turned(v, by):
+    return jnp.concatenate([v[:, by:], v[:, :by]], axis=1) if by else v
+
+
+def grad_kernel(band, cols, recv_ref, f_ref, bias_ref, g_ref, keep_ref, give_ref, xt_ref, w_ref):
     groups, both, size = recv_ref.shape
     half = both // 2
     n = groups * half
@@ -124,8 +131,6 @@
     pitch = cols + 2 * HALO
     x = recv_ref[:, :half, :].reshape(n, size)
     cot = recv_ref[:, half:, :].reshape(n, size)
-    x2_ref[:n] = x
-    x2_ref[n:] = x
     spread(f_ref, w_ref)
     x3 = jnp.concatenate([pltpu.roll(x, pitch, 1), x, pltpu.roll(x, size - pitch, 1)], axis=0)
     parts = [
@@ -143,41 +148,52 @@
         for a in range(3)
         for b in range(3)
     ]
-    nt = (((1,), (1,)), ((), ()))
+    turned = x.T
+    for fine in range(4):
+        v = lanes_turned(turned, CH * fine)
+        xt_ref[fine, :, :n] = v
+        xt_ref[fine, :, n:] = v
     total = None
-    for r in range(rot):
-        g8 = jnp.concatenate([t[CH * r : CH * (r + 1)] for t in moved[:8]], axis=0)
-        d = lax.dot_general(x2_ref[CH * r : CH * r + n, :], g8, nt, preferred_element_type=F32)
+    for first in range(0, rot, GROUP):
+        turns = range(first, first + GROUP)
+        g8 = [jnp.concatenate([t[CH * r : CH * (r + 1)] for t in moved[:8]], axis=0) for r in turns]
+        xs = [xt_ref[r % 4, :, 128 * (r // 4) : 128 * (r // 4) + n] for r in turns]
+        d = jnp.dot(
+            jnp.concatenate(g8, axis=1), jnp.concatenate(xs, axis=0), preferred_element_type=F32
+        )
         total = d if total is None else total + d
-    lined = [None] * 4
-    for m in range(rot // 8):
-        d = lax.dot_general(
-            x, moved[8][8 * CH * m : 8 * CH * (m + 1)], nt, preferred_element_type=F32
-        )
-        for v in range(2):
+    d = jnp.dot(moved[8], turned, preferred_element_type=F32)
+    last = jnp.zeros((CH, n), F32)
+    for fine in range(4):
+        lined = None
+        for coarse in range(rot // 4):
+            r = 4 * coarse + fine
+            e = lanes_turned(d[CH * r : CH * (r + 1)], 128 * coarse)
+            lined = e if lined is None else lined + e
+        last = last + lanes_turned(lined, CH * fine)
+    spots = lanes((2 * CH, 128)) // CH
+    spots8 = lanes((8, 128)) // CH
+    taken = []
+    for s in range(rot):
+        at = slice(128 * (s // 4), 128 * (s // 4 + 1))
+        wide = [total[2 * CH * t : 2 * CH * (t + 1), at] for t in range(4)]
+        thin = [last[8 * t : 8 * (t + 1), at] for t in range(4)]
+        for pieces, where in ((wide, spots), (thin, spots8)):
+            out = None
             for t in range(4):
-                e = rows_turned(d[:, 128 * v : 128 * (v + 1)], CH * (8 * m + 4 * v + t))
-                lined[t] = e if lined[t] is None else lined[t] + e
-    last = lined[0]
-    for t in range(1, 4):
-        last = last + pltpu.roll(lined[t], 128 - CH * t, 1)
-    split = last.reshape(groups, 2, 4, 8, 128)
-    spots = lanes((groups * 2 * 8, 128)) // CH
-    last = split[:, :, 0].reshape(-1, 128)
-    for j in range(1, 4):
-        last = jnp.where(spots == j, pltpu.roll(split[:, :, j].reshape(-1, 128), CH * j, 1), last)
-    last = last.reshape(groups, 2, 8, 128)
-    one = total[:, :128].reshape(groups, 2, CH, 128)
-    two = total[:, 128:].reshape(groups, 2, CH, 128)
+                by = CH * ((t - s) % 4)
+                v = pltpu.roll(pieces[t], by, 1) if by else pieces[t]
+                out = v if out is None else jnp.where(where == t, v, out)
+            taken.append(out)
     core = lax.axis_index("rows") % 2
     for c in range(2):
 
         @pl.when(core == c)
         def _():
             for ref, part in ((keep_ref, c), (give_ref, 1 - c)):
-                ref[:, :CH] = one[:, part]
-                ref[:, CH : 2 * CH] = two[:, part]
-                ref[:, 2 * CH :] = last[:, part]
+                for k in range(groups):
+                    ref[k, : 2 * CH] = taken[2 * (2 * k + part)]
+                    ref[k, 2 * CH :] = taken[2 * (2 * k + part) + 1]
 
 
 def input_kernel(band, cols, g_ref, f_ref, out_ref, w_ref):
@@ -235,13 +251,11 @@
         def _():
             for ref, part in ((own_ref, c), (other_ref, 1 - c)):
                 v = ref[...] * scale
-                for row in range(2):
-                    t = v[CH * row : CH * (row + 1)].T
-                    for b in range(4):
-                        out_ref[part, 4 * row + b] = t[CH * b : CH * (b + 1)]
-                e = v[2 * CH :]
-                e = jnp.concatenate([e[:, CH * j : CH * (j + 1)] for j in range(4)], axis=0)
-                out_ref[part, 8] = e.T
+                for tap in range(8):
+                    row, at = CH * (tap % 2), CH * (tap // 2)
+                    out_ref[part, tap] = v[row : row + CH, at : at + CH]
+                for t in range(4):
+                    out_ref[part, 8, 8 * t : 8 * (t + 1)] = v[2 * CH :, CH * t : CH * (t + 1)]
 
 
 def shaped(shape, dtype):
@@ -272,25 +286,22 @@
     square = pltpu.VMEM((3 * n, 3 * n), BF16)
 
     with jax.named_scope("edge_rows"):
+        x, c = inputs.reshape(n, width), cotangent.reshape(n, width)
         edge = shaped((HALO, 2 * local, width), BF16)
-        tile, far, near = call(
-            functools.partial(turn_kernel, band),
-            (shaped((band, 2 * local, width), BF16), edge, edge),
-            4 * n * n * width,
-            [pltpu.VMEM((2, n, width), BF16), pltpu.SemaphoreType.DMA((2,))],
-            in_specs=[pl.BlockSpec(memory_space=pltpu.HBM)] * 2,
-            limit=60,
-        )(inputs.reshape(n, width), cotangent.reshape(n, width))
+        far, near = call(functools.partial(ends_kernel, band), (edge, edge), 1000)(x, c)
         far = lax.ppermute(far, "rows", across)
         near = lax.ppermute(near, "rows", swap)
     with jax.named_scope("to_tiles"):
+        tiles = shaped((groups, 2 * local, size), BF16)
+        own = call(functools.partial(own_kernel, band, cols), tiles, 4 * n * n * width)(
+            x, c
+        )
         packed = call(
-            functools.partial(pack_kernel, cols),
-            shaped((groups, 2 * local, size), BF16),
+            functools.partial(edge_kernel, band, cols),
+            tiles,
             1000,
             [pltpu.VMEM((2 * HALO, 2 * local, width), BF16)],
-            limit=60,
-        )(tile, far, near)
+        )(own, far, near)
         recv = lax.all_to_all(packed, "rot", 0, 0, tiled=True)
     with jax.named_scope("weights"):
         fwd = jnp.transpose(filters, (1, 2, 0, 3)).reshape(taps, CH, n)
@@ -304,17 +315,19 @@
             functools.partial(grad_kernel, band, cols),
             (shaped((n, size), BF16), half, half),
             2 * 18 * n * n * size,
-            [pltpu.VMEM((2 * n, size), BF16), square],
+            [pltpu.VMEM((4, size, 2 * n), BF16), square],
         )(recv, fwd, bias2)
     def turn(i, step, s):
         now = i // step % 4
         return i + ((now + s) % 4 - now) * step
 
-    def add_four(v, step):
-        p1, p2, p3 = [
-            lax.ppermute(v, "rows", [(i, turn(i, step, s)) for i in range(bands)]) for s in (1, 2, 3)
+    def add_four(v, step, beside=None):
+        far, near, back = [
+            lax.ppermute(v, "rows", [(i, turn(i, step, s)) for i in range(bands)]) for s in (2, 1, 3)
         ]
-        return (v + p2) + (p1 + p3)
+        if beside is not None:
+            near, far, back, beside = lax.optimization_barrier((near, far, back, beside))
+        return (v + far) + (near + back), beside
 
     with jax.named_scope("filter_core"):
         other = lax.ppermute(give, "rows", swap)
@@ -339,9 +352,9 @@
             functools.partial(unpack_kernel, band, cols), shaped((n, width), BF16), 2 * n * n * width
         )(got[:, :local]).reshape(inputs.shape)
     with jax.named_scope("filter_y"):
-        v = add_four(v, 2)
+        v, _ = add_four(v, 2)
     with jax.named_scope("filter_z"):
-        v = add_four(v, 8)
+        v, input_grad = add_four(v, 8, input_grad)
     with jax.named_scope("filter_out"):
         scale = float(rotations * band * bands * width) ** (-0.5)
         other = lax.ppermute(v, "rows", swap)

time: 72.2 us -> 67.9 us (0.940)
  Pallas kernels: 14 us -> 10 us
  waiting for transfers between devices: 9.82 us -> 8.04 us
  local copies, waits for them, and re-layouts: 5.93 us -> 7.1 us
    pallas_call x2 -> x3, Pallas kernels: 5.18 us -> 2.35 us  [the longest x1 1.15 us: shards(): call(functools.partial(edge_kernel, band, cols), tiles, 1000, [pltpu.VMEM...]
    ppermute x6, waiting for transfers between devices: 2.88 us -> 1.35 us  [add_four(): lax.ppermute(v, 'rows', [(i, turn(i, step, s)) for i in range(bands)])]
    unnamed x8, local copies, waits for them, and re-layouts: 0.77 us -> 1.93 us
    ppermute x1, waiting for transfers between devices: 2.05 us -> 0.91 us  [shards(): far = lax.ppermute(far, 'rows', across)]
    pallas_call x1, Pallas kernels: 4.84 us -> 3.73 us  [shards(): call(functools.partial(grad_kernel, band, cols), (shaped((n, size), BF16)...]
    ppermute x1, waiting for transfers between devices: 0.01 us -> 0.87 us  [shards(): other = lax.ppermute(v, 'rows', swap)]
  transfers between devices with their start and end apart: 11 -> 11, of which waited for: 4 -> 4; matrix products, arithmetic and copies ran while one was open for 6% -> 6% of each run, Pallas kernels for 4% -> 6%
where the time goes in v4:
time: 67.9 us; the launch traced here: 67.5 us
  starting transfers between devices  31.6 us (47%)
  Pallas kernels  10 us (15%)
  blocking collectives  9.75 us (14%)
  waiting for transfers between devices  8.04 us (12%)
  local copies, waits for them, and re-layouts  7.1 us (10%)
  between operations  0.79 us (1%)
    ppermute x6, starting transfers between devices, add_four(): lax.ppermute(v, 'rows', [(i, turn(i, step, s)) for i in range(bands)])  16.5 us
    all_to_all x1, blocking collectives, shards(): got = lax.all_to_all(sent, 'rot', 0, 0, tiled=True)  9.75 us
    all_to_all x1, starting transfers between devices, shards(): recv = lax.all_to_all(packed, 'rot', 0, 0, tiled=True)  5.37 us
    all_to_all x1, waiting for transfers between devices, shards(): recv = lax.all_to_all(packed, 'rot', 0, 0, tiled=True)  4.91 us
    ppermute x1, starting transfers between devices, shards(): far = lax.ppermute(far, 'rows', across)  4.6 us
    ppermute x1, starting transfers between devices, shards(): other = lax.ppermute(v, 'rows', swap)  4.25 us
    pallas_call x1, Pallas kernels, shards(): call(functools.partial(grad_kernel, band, cols), (shaped((n, size), BF16)...  3.73 us
    unnamed x8, local copies, waits for them, and re-layouts  1.93 us
  transfers between devices with their start and end apart: 11, of which 4 were waited for; matrix products, arithmetic and copies ran while one was open for 6% of the time, Pallas kernels for 6%

profile of v4, /device:TPU:1, one launch (start us, length us, event | category | flops | bytes accessed | tf_op | source)
XLA Modules:
  0.0 67.5 jit_solution(6911536393111639211)
XLA Ops:
  0.6 0.0 copy-start
  0.6 0.9 %copy-done = bf16[64,8,128]{2,1,0:T(8,128)(2,1)S(1)} copy-done((bf16[64,8,128]{2,1,0:T(8,128)(2,1)S(1)}, bf16[64,8,128]{2,1,0:T(8,128)(2,1)}, u32[]{:S(2)}) %copy-start) | copy-done | bytes 131096
  1.5 0.0 copy-start.1
  1.5 0.9 %copy-done.1 = bf16[64,8,128]{2,1,0:T(8,128)(2,1)S(1)} copy-done((bf16[64,8,128]{2,1,0:T(8,128)(2,1)S(1)}, bf16[64,8,128]{2,1,0:T(8,128)(2,1)}, u32[]{:S(2)}) %copy-start.1) | copy-done | bytes 131096
  2.4 0.3 edge_rows.1
  2.7 4.6 %collective-permute-start = (bf16[2,128,128]{2,1,0:T(8,128)(2,1)S(1)}, bf16[2,128,128]{2,1,0:T(8,128)(2,1)S(1)}, u32[]{:S(2)}, u32[]{:S(2)}) collective-permute-start(bf16[2,128,128]{2,1,0:T(8,128)(2,1)S(1)} %get-tuple-element.15), channel_id=1, source_target_pairs={{1,2},{2,1},{3,4},{4,3},{5,6},{6,5},{7,8},{8,7},{9,10},{10,9},{11,... | collective-permute-start | bytes 196616 | tf_op jit(solution)/shard_map/edge_rows/ppermute | solution.py:292
  7.3 0.1 collective-permute-start.1
  7.4 0.9 %to_tiles.2.own_ref = bf16[8,128,256]{2,1,0:T(8,128)(2,1)S(1)} custom-call(bf16[512,128]{1,0:T(8,128)(2,1)S(1)} %bitcast.12, bf16[512,128]{1,0:T(8,128)(2,1)S(1)} %bitcast.14), custom_call_target="tpu_custom_call" | custom-call | flops 134217728 | bytes 2000000 | tf_op jit(solution)/shard_map/to_tiles/pallas_call | solution.py:296
  8.4 0.9 %collective-permute-done.far_ref = bf16[2,128,128]{2,1,0:T(8,128)(2,1)S(1)} collective-permute-done((bf16[2,128,128]{2,1,0:T(8,128)(2,1)S(1)}, bf16[2,128,128]{2,1,0:T(8,128)(2,1)S(1)}, u32[]{:S(2)}, u32[]{:S(2)}) %collective-permute-start) | collective-permute-done | bytes 65568 | tf_op jit(solution)/shard_map/edge_rows/ppermute | solution.py:292
  9.3 0.0 collective-permute-done.1.near_ref
  9.3 1.1 %to_tiles.3 = bf16[8,128,256]{2,1,0:T(8,128)(2,1)} custom-call(bf16[8,128,256]{2,1,0:T(8,128)(2,1)S(1)} %to_tiles.2.own_ref, bf16[2,128,128]{2,1,0:T(8,128)(2,1)S(1)} %collective-permute-done.far_ref, bf16[2,128,128]{2,1,0:T(8,128)(2,1)S(1)} %collective-permute-done.1.near_ref), custom_call_target="tpu_custom_call" | custom-call | flops 1000 | bytes 2000000 | tf_op jit(solution)/shard_map/to_tiles/pallas_call | solution.py:299
  10.4 5.4 %all-to-all-start = ((bf16[8,128,256]{2,1,0:T(8,128)(2,1)}), bf16[8,128,256]{2,1,0:T(8,128)(2,1)S(1)}, u32[]{:S(2)}, u32[]{:S(2)}) async-start(bf16[8,128,256]{2,1,0:T(8,128)(2,1)} %to_tiles.3), calls=%async_computation | async-start | bytes 1048576 | tf_op jit(solution)/shard_map/to_tiles/all_to_all | solution.py:305
  15.8 0.0 slice-start.1
  15.8 1.2 %slice-done = bf16[15,9,32,32]{3,2,1,0:T(8,128)(2,1)S(1)} async-done(((bf16[16,9,32,32]{3,2,1,0:T(8,128)(2,1)}), bf16[15,9,32,32]{3,2,1,0:T(8,128)(2,1)S(1)}, s32[]{:S(2)}) %slice-start) | async-done | bytes 276504 | tf_op jit(solution)/shard_map/weights/slice | solution.py:308
  17.0 0.2 rev.3
  17.2 0.0 slice-done.1
  17.2 0.2 maximum_bitcast_fusion
  17.5 0.9 %copy.7 = bf16[9,32,16,32]{3,2,1,0:T(8,128)(2,1)S(1)} copy(bf16[9,32,16,32]{1,3,0,2:T(8,128)(2,1)S(1)} %maximum_bitcast_fusion) | data formatting | bytes 589824 | tf_op jit(solution)/shard_map/weights/transpose | solution.py:309
  18.4 0.0 copy-start.2
  18.4 1.1 %reshape.26.f_ref = bf16[9,32,512]{2,1,0:T(8,128)(2,1)S(1)} reshape(bf16[9,32,16,32]{3,2,1,0:T(8,128)(2,1)S(1)} %copy.7) | data formatting | bytes 589824 | tf_op jit(solution)/shard_map/weights/reshape | solution.py:309
  19.6 0.1 copy-done.2
  19.7 0.5 copy.6
  20.2 0.0 copy-start.3
  20.2 1.1 %reshape.25.f_ref = bf16[9,32,512]{2,1,0:T(8,128)(2,1)S(1)} reshape(bf16[9,32,16,32]{3,2,1,0:T(8,128)(2,1)S(1)} %copy.6) | data formatting | bytes 589824 | tf_op jit(solution)/shard_map/weights/reshape | solution.py:307
  21.3 4.9 %all-to-all-done.recv_ref = bf16[8,128,256]{2,1,0:T(8,128)(2,1)S(1)} async-done(((bf16[8,128,256]{2,1,0:T(8,128)(2,1)}), bf16[8,128,256]{2,1,0:T(8,128)(2,1)S(1)}, u32[]{:S(2)}, u32[]{:S(2)}) %all-to-all-start) | async-done | bytes 524320 | tf_op jit(solution)/shard_map/to_tiles/all_to_all | solution.py:305
  26.2 0.0 copy-done.3
  26.2 0.1 broadcast_in_dim.2.bias_ref
  26.3 3.7 %grad.1 = (bf16[512,256]{1,0:T(8,128)(2,1)S(1)}, f32[8,72,128]{2,1,0:T(8,128)S(1)}, f32[8,72,128]{2,1,0:T(8,128)S(1)}) custom-call(bf16[8,128,256]{2,1,0:T(8,128)(2,1)S(1)} %all-to-all-done.recv_ref, bf16[9,32,512]{2,1,0:T(8,128)(2,1)S(1)} %reshape.25.f_ref, f32[32,256]{1,0:T(8,128)S(1)} %broadcast_in_dim.2.bias_ref), custom_call_target="tpu_custom_call" | custom-call | flops 2415919104 | bytes 2000000 | tf_op jit(solution)/shard_map/grad/pallas_call | solution.py:314
  30.0 0.7 %collective-permute-start.2 = (f32[8,72,128]{2,1,0:T(8,128)S(1)}, f32[8,72,128]{2,1,0:T(8,128)S(1)}, u32[]{:S(2)}, u32[]{:S(2)}) collective-permute-start(f32[8,72,128]{2,1,0:T(8,128)S(1)} %get-tuple-element.21), channel_id=1, source_target_pairs={{0,1},{1,0},{2,3},{3,2},{4,5},{5,4},{6,7},{7,6},{8,9},{9,8},{10,11... | collective-permute-start | bytes 884744 | tf_op jit(solution)/shard_map/filter_core/ppermute | solution.py:333
  30.8 1.8 %input_grad.2 = bf16[512,128]{1,0:T(8,128)(2,1)S(1)} custom-call(bf16[512,256]{1,0:T(8,128)(2,1)S(1)} %get-tuple-element.22.g_ref, bf16[9,32,512]{2,1,0:T(8,128)(2,1)S(1)} %reshape.26.f_ref), custom_call_target="tpu_custom_call" | custom-call | flops 1207959552 | bytes 2000000 | tf_op jit(solution)/shard_map/input_grad/pallas_call | solution.py:335
  32.6 0.0 collective-permute-done.2.other_ref
  32.6 9.8 %all_to_all.10 = bf16[8,144,128]{2,1,0:T(8,128)(2,1)S(1)} all-to-all(bf16[8,144,128]{2,1,0:T(8,128)(2,1)S(1)} %to_channels.1), channel_id=1, replica_groups=mesh['rot'=8,'rows'=32] {'rot'}, dimensions={0} | all-to-all | bytes 589824 | tf_op jit(solution)/shard_map/to_channels/all_to_all | solution.py:347
  42.4 3.4 %collective-permute-start.3 = (f32[72,128]{1,0:T(8,128)S(1)}, f32[72,128]{1,0:T(8,128)S(1)}, u32[]{:S(2)}, u32[]{:S(2)}) collective-permute-start(f32[72,128]{1,0:T(8,128)S(1)} %convert_reduce_fusion), channel_id=1, source_target_pairs={{0,4},{1,5},{2,6},{3,7},{4,0},{5,1},{6,2},{7,3},{8,12},{9,13},{10,... | collective-permute-start | bytes 110600 | tf_op jit(solution)/shard_map/filter_y/ppermute | solution.py:326
  45.8 1.1 %collective-permute-start.4 = (f32[72,128]{1,0:T(8,128)S(1)}, f32[72,128]{1,0:T(8,128)S(1)}, u32[]{:S(2)}, u32[]{:S(2)}) collective-permute-start(f32[72,128]{1,0:T(8,128)S(1)} %convert_reduce_fusion), channel_id=1, source_target_pairs={{0,2},{1,3},{2,4},{3,5},{4,6},{5,7},{6,0},{7,1},{8,10},{9,11},{10,... | collective-permute-start | bytes 110600 | tf_op jit(solution)/shard_map/filter_y/ppermute | solution.py:326
  46.9 1.6 %collective-permute-start.5 = (f32[72,128]{1,0:T(8,128)S(1)}, f32[72,128]{1,0:T(8,128)S(1)}, u32[]{:S(2)}, u32[]{:S(2)}) collective-permute-start(f32[72,128]{1,0:T(8,128)S(1)} %convert_reduce_fusion), channel_id=1, source_target_pairs={{0,6},{1,7},{2,0},{3,1},{4,2},{5,3},{6,4},{7,5},{8,14},{9,15},{10,... | collective-permute-start | bytes 110600 | tf_op jit(solution)/shard_map/filter_y/ppermute | solution.py:326
  48.5 0.0 collective-permute-done.3
  48.5 1.3 %collective-permute-done.4 = f32[72,128]{1,0:T(8,128)S(1)} collective-permute-done((f32[72,128]{1,0:T(8,128)S(1)}, f32[72,128]{1,0:T(8,128)S(1)}, u32[]{:S(2)}, u32[]{:S(2)}) %collective-permute-start.4) | collective-permute-done | bytes 36896 | tf_op jit(solution)/shard_map/filter_y/ppermute | solution.py:326
  49.8 0.0 collective-permute-done.5
  49.8 3.5 %collective-permute-start.6 = (f32[72,128]{1,0:T(8,128)S(1)}, f32[72,128]{1,0:T(8,128)S(1)}, u32[]{:S(2)}, u32[]{:S(2)}) collective-permute-start(f32[72,128]{1,0:T(8,128)S(1)} %add_add_fusion.1), channel_id=1, source_target_pairs={{0,8},{1,9},{2,10},{3,11},{4,12},{5,13},{6,14},{7,15},{8,16},{9,17... | collective-permute-start | bytes 110600 | tf_op jit(solution)/shard_map/filter_z/ppermute | solution.py:326
  53.3 3.8 %collective-permute-start.7 = (f32[72,128]{1,0:T(8,128)S(1)}, f32[72,128]{1,0:T(8,128)S(1)}, u32[]{:S(2)}, u32[]{:S(2)}) collective-permute-start(f32[72,128]{1,0:T(8,128)S(1)} %add_add_fusion.1), channel_id=1, source_target_pairs={{0,16},{1,17},{2,18},{3,19},{4,20},{5,21},{6,22},{7,23},{8,24},{9,... | collective-permute-start | bytes 110600 | tf_op jit(solution)/shard_map/filter_z/ppermute | solution.py:326
  57.1 3.2 %collective-permute-start.8 = (f32[72,128]{1,0:T(8,128)S(1)}, f32[72,128]{1,0:T(8,128)S(1)}, u32[]{:S(2)}, u32[]{:S(2)}) collective-permute-start(f32[72,128]{1,0:T(8,128)S(1)} %add_add_fusion.1), channel_id=1, source_target_pairs={{0,24},{1,25},{2,26},{3,27},{4,28},{5,29},{6,30},{7,31},{8,0},{9,1... | collective-permute-start | bytes 110600 | tf_op jit(solution)/shard_map/filter_z/ppermute | solution.py:326
  60.3 1.2 %input_grad.3 = bf16[512,128]{1,0:T(8,128)(2,1)} custom-call(bf16[8,64,128]{2,1,0:T(8,128)(2,1)S(1)} %slice.17.dx_ref), custom_call_target="tpu_custom_call" | custom-call | flops 67108864 | bytes 2000000 | tf_op jit(solution)/shard_map/input_grad/pallas_call | solution.py:351
  61.6 0.0 collective-permute-done.6
  61.6 0.0 collective-permute-done.7
  61.6 0.0 collective-permute-done.8
  61.6 4.2 %collective-permute-start.9 = (f32[72,128]{1,0:T(8,128)S(1)}, f32[72,128]{1,0:T(8,128)S(1)}, u32[]{:S(2)}, u32[]{:S(2)}) collective-permute-start(f32[72,128]{1,0:T(8,128)S(1)} %add_add_fusion.own_ref), channel_id=1, source_target_pairs={{0,1},{1,0},{2,3},{3,2},{4,5},{5,4},{6,7},{7,6},{8,9},{9,8},{10,11... | collective-permute-start | bytes 110600 | tf_op jit(solution)/shard_map/filter_out/ppermute | solution.py:360
  65.8 0.9 %collective-permute-done.9.other_ref = f32[72,128]{1,0:T(8,128)S(1)} collective-permute-done((f32[72,128]{1,0:T(8,128)S(1)}, f32[72,128]{1,0:T(8,128)S(1)}, u32[]{:S(2)}, u32[]{:S(2)}) %collective-permute-start.9) | collective-permute-done | bytes 36896 | tf_op jit(solution)/shard_map/filter_out/ppermute | solution.py:360
  66.7 0.8 %filter_out.1 = f32[2,9,32,32]{3,2,1,0:T(8,128)} custom-call(f32[72,128]{1,0:T(8,128)S(1)} %add_add_fusion.own_ref, f32[72,128]{1,0:T(8,128)S(1)} %collective-permute-done.9.other_ref), custom_call_target="tpu_custom_call" | custom-call | flops 1000 | bytes 2000000 | tf_op jit(solution)/shard_map/filter_out/pallas_call | solution.py:361
  (6 shorter events, 0.1 us)
Async XLA Ops:
  0.6 0.9 %copy-start = (bf16[64,8,128]{2,1,0:T(8,128)(2,1)S(1)}, bf16[64,8,128]{2,1,0:T(8,128)(2,1)}, u32[]{:S(2)}) copy-start(bf16[64,8,128]{2,1,0:T(8,128)(2,1)} %param.4) | copy-start | bytes 393220
  1.5 0.9 %copy-start.1 = (bf16[64,8,128]{2,1,0:T(8,128)(2,1)S(1)}, bf16[64,8,128]{2,1,0:T(8,128)(2,1)}, u32[]{:S(2)}) copy-start(bf16[64,8,128]{2,1,0:T(8,128)(2,1)} %param.5) | copy-start | bytes 393220
  2.7 6.5 %collective-permute-start = (bf16[2,128,128]{2,1,0:T(8,128)(2,1)S(1)}, bf16[2,128,128]{2,1,0:T(8,128)(2,1)S(1)}, u32[]{:S(2)}, u32[]{:S(2)}) collective-permute-start(bf16[2,128,128]{2,1,0:T(8,128)(2,1)S(1)} %get-tuple-element.15), channel_id=1, source_target_pairs={{1,2},{2,1},{3,4},{4,3},{5,6},{6,5},{7,8},{8,7},{9,10},{10,9},{11,... | collective-permute-start | bytes 196616 | tf_op jit(solution)/shard_map/edge_rows/ppermute | solution.py:292
  7.3 1.9 %collective-permute-start.1 = (bf16[2,128,128]{2,1,0:T(8,128)(2,1)S(1)}, bf16[2,128,128]{2,1,0:T(8,128)(2,1)S(1)}, u32[]{:S(2)}, u32[]{:S(2)}) collective-permute-start(bf16[2,128,128]{2,1,0:T(8,128)(2,1)S(1)} %get-tuple-element.16), channel_id=1, source_target_pairs={{0,1},{1,0},{2,3},{3,2},{4,5},{5,4},{6,7},{7,6},{8,9},{9,8},{10,11... | collective-permute-start | bytes 196616 | tf_op jit(solution)/shard_map/edge_rows/ppermute | solution.py:293
  10.4 15.8 %all-to-all-start = ((bf16[8,128,256]{2,1,0:T(8,128)(2,1)}), bf16[8,128,256]{2,1,0:T(8,128)(2,1)S(1)}, u32[]{:S(2)}, u32[]{:S(2)}) async-start(bf16[8,128,256]{2,1,0:T(8,128)(2,1)} %to_tiles.3), calls=%async_computation | async-start | bytes 1048576 | tf_op jit(solution)/shard_map/to_tiles/all_to_all | solution.py:305
  15.8 1.2 %slice-start = ((bf16[16,9,32,32]{3,2,1,0:T(8,128)(2,1)}), bf16[15,9,32,32]{3,2,1,0:T(8,128)(2,1)S(1)}, s32[]{:S(2)}) async-start(bf16[16,9,32,32]{3,2,1,0:T(8,128)(2,1)} %param.6), calls=%async_computation.2 | async-start | bytes 2211840 | tf_op jit(solution)/shard_map/weights/slice | solution.py:308
  15.8 1.4 %slice-start.1 = ((bf16[16,9,32,32]{3,2,1,0:T(8,128)(2,1)}), bf16[1,9,32,32]{3,2,1,0:T(8,128)(2,1)S(1)}, s32[]{:S(2)}) async-start(bf16[16,9,32,32]{3,2,1,0:T(8,128)(2,1)} %param.6), calls=%async_computation.3 | async-start | bytes 147456 | tf_op jit(solution)/shard_map/weights/slice | solution.py:308
  18.4 1.3 %copy-start.2 = (bf16[16,9,32,32]{3,2,1,0:T(8,128)(2,1)S(1)}, bf16[16,9,32,32]{3,2,1,0:T(8,128)(2,1)}, u32[]{:S(2)}) copy-start(bf16[16,9,32,32]{3,2,1,0:T(8,128)(2,1)} %param.6) | copy-start | bytes 884740
  20.2 6.1 %copy-start.3 = (f32[32]{0:T(128)S(1)}, f32[32]{0:T(128)}, u32[]{:S(2)}) copy-start(f32[32]{0:T(128)} %param.7) | copy-start | bytes 388
  30.0 2.6 %collective-permute-start.2 = (f32[8,72,128]{2,1,0:T(8,128)S(1)}, f32[8,72,128]{2,1,0:T(8,128)S(1)}, u32[]{:S(2)}, u32[]{:S(2)}) collective-permute-start(f32[8,72,128]{2,1,0:T(8,128)S(1)} %get-tuple-element.21), channel_id=1, source_target_pairs={{0,1},{1,0},{2,3},{3,2},{4,5},{5,4},{6,7},{7,6},{8,9},{9,8},{10,11... | collective-permute-start | bytes 884744 | tf_op jit(solution)/shard_map/filter_core/ppermute | solution.py:333
  42.4 6.0 %collective-permute-start.3 = (f32[72,128]{1,0:T(8,128)S(1)}, f32[72,128]{1,0:T(8,128)S(1)}, u32[]{:S(2)}, u32[]{:S(2)}) collective-permute-start(f32[72,128]{1,0:T(8,128)S(1)} %convert_reduce_fusion), channel_id=1, source_target_pairs={{0,4},{1,5},{2,6},{3,7},{4,0},{5,1},{6,2},{7,3},{8,12},{9,13},{10,... | collective-permute-start | bytes 110600 | tf_op jit(solution)/shard_map/filter_y/ppermute | solution.py:326
  45.8 4.0 %collective-permute-start.4 = (f32[72,128]{1,0:T(8,128)S(1)}, f32[72,128]{1,0:T(8,128)S(1)}, u32[]{:S(2)}, u32[]{:S(2)}) collective-permute-start(f32[72,128]{1,0:T(8,128)S(1)} %convert_reduce_fusion), channel_id=1, source_target_pairs={{0,2},{1,3},{2,4},{3,5},{4,6},{5,7},{6,0},{7,1},{8,10},{9,11},{10,... | collective-permute-start | bytes 110600 | tf_op jit(solution)/shard_map/filter_y/ppermute | solution.py:326
  46.9 2.9 %collective-permute-start.5 = (f32[72,128]{1,0:T(8,128)S(1)}, f32[72,128]{1,0:T(8,128)S(1)}, u32[]{:S(2)}, u32[]{:S(2)}) collective-permute-start(f32[72,128]{1,0:T(8,128)S(1)} %convert_reduce_fusion), channel_id=1, source_target_pairs={{0,6},{1,7},{2,0},{3,1},{4,2},{5,3},{6,4},{7,5},{8,14},{9,15},{10,... | collective-permute-start | bytes 110600 | tf_op jit(solution)/shard_map/filter_y/ppermute | solution.py:326
  49.8 11.7 %collective-permute-start.6 = (f32[72,128]{1,0:T(8,128)S(1)}, f32[72,128]{1,0:T(8,128)S(1)}, u32[]{:S(2)}, u32[]{:S(2)}) collective-permute-start(f32[72,128]{1,0:T(8,128)S(1)} %add_add_fusion.1), channel_id=1, source_target_pairs={{0,8},{1,9},{2,10},{3,11},{4,12},{5,13},{6,14},{7,15},{8,16},{9,17... | collective-permute-start | bytes 110600 | tf_op jit(solution)/shard_map/filter_z/ppermute | solution.py:326
  53.3 8.3 %collective-permute-start.7 = (f32[72,128]{1,0:T(8,128)S(1)}, f32[72,128]{1,0:T(8,128)S(1)}, u32[]{:S(2)}, u32[]{:S(2)}) collective-permute-start(f32[72,128]{1,0:T(8,128)S(1)} %add_add_fusion.1), channel_id=1, source_target_pairs={{0,16},{1,17},{2,18},{3,19},{4,20},{5,21},{6,22},{7,23},{8,24},{9,... | collective-permute-start | bytes 110600 | tf_op jit(solution)/shard_map/filter_z/ppermute | solution.py:326
  57.1 4.5 %collective-permute-start.8 = (f32[72,128]{1,0:T(8,128)S(1)}, f32[72,128]{1,0:T(8,128)S(1)}, u32[]{:S(2)}, u32[]{:S(2)}) collective-permute-start(f32[72,128]{1,0:T(8,128)S(1)} %add_add_fusion.1), channel_id=1, source_target_pairs={{0,24},{1,25},{2,26},{3,27},{4,28},{5,29},{6,30},{7,31},{8,0},{9,1... | collective-permute-start | bytes 110600 | tf_op jit(solution)/shard_map/filter_z/ppermute | solution.py:326
  61.6 5.1 %collective-permute-start.9 = (f32[72,128]{1,0:T(8,128)S(1)}, f32[72,128]{1,0:T(8,128)S(1)}, u32[]{:S(2)}, u32[]{:S(2)}) collective-permute-start(f32[72,128]{1,0:T(8,128)S(1)} %add_add_fusion.own_ref), channel_id=1, source_target_pairs={{0,1},{1,0},{2,3},{3,2},{4,5},{5,4},{6,7},{7,6},{8,9},{9,8},{10,11... | collective-permute-start | bytes 110600 | tf_op jit(solution)/shard_map/filter_out/ppermute | solution.py:360

commit v5 on v4

--- a/solution.py
+++ b/solution.py
@@ -288,7 +288,7 @@
     with jax.named_scope("edge_rows"):
         x, c = inputs.reshape(n, width), cotangent.reshape(n, width)
         edge = shaped((HALO, 2 * local, width), BF16)
-        far, near = call(functools.partial(ends_kernel, band), (edge, edge), 1000)(x, c)
+        far, near = call(functools.partial(ends_kernel, band), (edge, edge), 1000, limit=60)(x, c)
         far = lax.ppermute(far, "rows", across)
         near = lax.ppermute(near, "rows", swap)
     with jax.named_scope("to_tiles"):
@@ -317,17 +317,20 @@
             2 * 18 * n * n * size,
             [pltpu.VMEM((4, size, 2 * n), BF16), square],
         )(recv, fwd, bias2)
-    def turn(i, step, s):
-        now = i // step % 4
-        return i + ((now + s) % 4 - now) * step
-
-    def add_four(v, step, beside=None):
-        far, near, back = [
-            lax.ppermute(v, "rows", [(i, turn(i, step, s)) for i in range(bands)]) for s in (2, 1, 3)
-        ]
+    def met(i, along, pair):
+        now = i // along % 4
+        return i + (pair(now) - now) * along
+
+    def add_four(v, pair, beside=None):
+        def swapped(to):
+            return lax.ppermute(v, "rows", [(i, to(i)) for i in range(bands)])
+
+        both = swapped(lambda i: met(met(i, 2, pair), 8, pair))
+        deep = swapped(lambda i: met(i, 8, pair))
+        wide = swapped(lambda i: met(i, 2, pair))
         if beside is not None:
-            near, far, back, beside = lax.optimization_barrier((near, far, back, beside))
-        return (v + far) + (near + back), beside
+            both, deep, wide, beside = lax.optimization_barrier((both, deep, wide, beside))
+        return (v + both) + (deep + wide), beside
 
     with jax.named_scope("filter_core"):
         other = lax.ppermute(give, "rows", swap)
@@ -351,10 +354,10 @@
         input_grad = call(
             functools.partial(unpack_kernel, band, cols), shaped((n, width), BF16), 2 * n * n * width
         )(got[:, :local]).reshape(inputs.shape)
-    with jax.named_scope("filter_y"):
-        v, _ = add_four(v, 2)
-    with jax.named_scope("filter_z"):
-        v, input_grad = add_four(v, 8, input_grad)
+    with jax.named_scope("filter_blocks"):
+        v, _ = add_four(v, lambda k: k ^ 1)
+    with jax.named_scope("filter_rows"):
+        v, input_grad = add_four(v, lambda k: 3 - k, input_grad)
     with jax.named_scope("filter_out"):
         scale = float(rotations * band * bands * width) ** (-0.5)
         other = lax.ppermute(v, "rows", swap)

time: 67.9 us -> 68.8 us (1.013)
  starting transfers between devices: 31.6 us -> 28.8 us
  waiting for transfers between devices: 8.04 us -> 10 us
  Pallas kernels: 10 us -> 11.6 us
    ppermute x6, waiting for transfers between devices: 1.35 us -> 5.29 us  [swapped(): return lax.ppermute(v, 'rows', [(i, to(i)) for i in range(bands)])]
    ppermute x6, starting transfers between devices: 16.5 us -> 12.9 us  [swapped(): return lax.ppermute(v, 'rows', [(i, to(i)) for i in range(bands)])]
    pallas_call x1, Pallas kernels: 0.29 us -> 1.89 us  [shards(): call(functools.partial(ends_kernel, band), (edge, edge), 1000, limit=60)]
    all_to_all x1, waiting for transfers between devices: 4.91 us -> 3.86 us  [shards(): recv = lax.all_to_all(packed, 'rot', 0, 0, tiled=True)]
    ppermute x1, starting transfers between devices: 0.73 us -> 1.73 us  [shards(): other = lax.ppermute(give, 'rows', swap)]
    ppermute x1, waiting for transfers between devices: 0.91 us -> 0.01 us  [shards(): far = lax.ppermute(far, 'rows', across)]
  transfers between devices with their start and end apart: 11 -> 11, of which waited for: 4 -> 6; matrix products, arithmetic and copies ran while one was open for 6% -> 6% of each run, Pallas kernels for 6% -> 6%
where the time goes in v5:
time: 68.8 us; the launch traced here: 68.5 us
  starting transfers between devices  28.8 us (42%)
  Pallas kernels  11.6 us (17%)
  waiting for transfers between devices  10 us (15%)
  blocking collectives  9.82 us (14%)
  local copies, waits for them, and re-layouts  7.1 us (10%)
  between operations  0.8 us (1%)
    ppermute x6, starting transfers between devices, swapped(): return lax.ppermute(v, 'rows', [(i, to(i)) for i in range(bands)])  12.9 us
    all_to_all x1, blocking collectives, shards(): got = lax.all_to_all(sent, 'rot', 0, 0, tiled=True)  9.82 us
    all_to_all x1, starting transfers between devices, shards(): recv = lax.all_to_all(packed, 'rot', 0, 0, tiled=True)  5.37 us
    ppermute x6, waiting for transfers between devices, swapped(): return lax.ppermute(v, 'rows', [(i, to(i)) for i in range(bands)])  5.29 us
    ppermute x1, starting transfers between devices, shards(): far = lax.ppermute(far, 'rows', across)  4.58 us
    ppermute x1, starting transfers between devices, shards(): other = lax.ppermute(v, 'rows', swap)  4.1 us
    all_to_all x1, waiting for transfers between devices, shards(): recv = lax.all_to_all(packed, 'rot', 0, 0, tiled=True)  3.86 us
    pallas_call x1, Pallas kernels, shards(): call(functools.partial(grad_kernel, band, cols), (shaped((n, size), BF16)...  3.73 us
  transfers between devices with their start and end apart: 11, of which 6 were waited for; matrix products, arithmetic and copies ran while one was open for 6% of the time, Pallas kernels for 6%

profile of v5, /device:TPU:1, one launch (start us, length us, event | category | flops | bytes accessed | tf_op | source)
XLA Modules:
  0.0 68.5 jit_solution(18418784657281216463)
XLA Ops:
  0.6 1.9 %edge_rows.1 = (bf16[2,128,128]{2,1,0:T(8,128)(2,1)}, bf16[2,128,128]{2,1,0:T(8,128)(2,1)}) custom-call(bf16[512,128]{1,0:T(8,128)(2,1)} %bitcast.11, bf16[512,128]{1,0:T(8,128)(2,1)} %bitcast.13), custom_call_target="tpu_custom_call" | custom-call | flops 1000 | bytes 2000000 | tf_op jit(solution)/shard_map/edge_rows/pallas_call | solution.py:291
  2.5 4.6 %collective-permute-start = (bf16[2,128,128]{2,1,0:T(8,128)(2,1)}, bf16[2,128,128]{2,1,0:T(8,128)(2,1)S(1)}, u32[]{:S(2)}, u32[]{:S(2)}) collective-permute-start(bf16[2,128,128]{2,1,0:T(8,128)(2,1)} %get-tuple-element.15), channel_id=1, source_target_pairs={{1,2},{2,1},{3,4},{4,3},{5,6},{6,5},{7,8},{8,7},{9,10},{10,9},{11,... | collective-permute-start | bytes 196616 | tf_op jit(solution)/shard_map/edge_rows/ppermute | solution.py:292
  7.1 0.1 collective-permute-start.1
  7.2 0.0 copy-start
  7.2 0.9 %copy-done = bf16[64,8,128]{2,1,0:T(8,128)(2,1)S(1)} copy-done((bf16[64,8,128]{2,1,0:T(8,128)(2,1)S(1)}, bf16[64,8,128]{2,1,0:T(8,128)(2,1)}, u32[]{:S(2)}) %copy-start) | copy-done | bytes 131096
  8.1 0.0 copy-start.1
  8.1 0.9 %copy-done.1 = bf16[64,8,128]{2,1,0:T(8,128)(2,1)S(1)} copy-done((bf16[64,8,128]{2,1,0:T(8,128)(2,1)S(1)}, bf16[64,8,128]{2,1,0:T(8,128)(2,1)}, u32[]{:S(2)}) %copy-start.1) | copy-done | bytes 131096
  9.0 0.9 %to_tiles.2.own_ref = bf16[8,128,256]{2,1,0:T(8,128)(2,1)S(1)} custom-call(bf16[512,128]{1,0:T(8,128)(2,1)S(1)} %bitcast.12, bf16[512,128]{1,0:T(8,128)(2,1)S(1)} %bitcast.14), custom_call_target="tpu_custom_call" | custom-call | flops 134217728 | bytes 2000000 | tf_op jit(solution)/shard_map/to_tiles/pallas_call | solution.py:296
  9.9 0.0 collective-permute-done.far_ref
  10.0 0.0 collective-permute-done.1.near_ref
  10.0 1.2 %to_tiles.3 = bf16[8,128,256]{2,1,0:T(8,128)(2,1)} custom-call(bf16[8,128,256]{2,1,0:T(8,128)(2,1)S(1)} %to_tiles.2.own_ref, bf16[2,128,128]{2,1,0:T(8,128)(2,1)S(1)} %collective-permute-done.far_ref, bf16[2,128,128]{2,1,0:T(8,128)(2,1)S(1)} %collective-permute-done.1.near_ref), custom_call_target="tpu_custom_call" | custom-call | flops 1000 | bytes 2000000 | tf_op jit(solution)/shard_map/to_tiles/pallas_call | solution.py:299
  11.1 5.4 %all-to-all-start = ((bf16[8,128,256]{2,1,0:T(8,128)(2,1)}), bf16[8,128,256]{2,1,0:T(8,128)(2,1)S(1)}, u32[]{:S(2)}, u32[]{:S(2)}) async-start(bf16[8,128,256]{2,1,0:T(8,128)(2,1)} %to_tiles.3), calls=%async_computation | async-start | bytes 1048576 | tf_op jit(solution)/shard_map/to_tiles/all_to_all | solution.py:305
  16.5 0.0 slice-start.1
  16.5 1.2 %slice-done = bf16[15,9,32,32]{3,2,1,0:T(8,128)(2,1)S(1)} async-done(((bf16[16,9,32,32]{3,2,1,0:T(8,128)(2,1)}), bf16[15,9,32,32]{3,2,1,0:T(8,128)(2,1)S(1)}, s32[]{:S(2)}) %slice-start) | async-done | bytes 276504 | tf_op jit(solution)/shard_map/weights/slice | solution.py:308
  17.8 0.2 rev.3
  17.9 0.0 slice-done.1
  18.0 0.2 maximum_bitcast_fusion
  18.2 0.9 %copy.7 = bf16[9,32,16,32]{3,2,1,0:T(8,128)(2,1)S(1)} copy(bf16[9,32,16,32]{1,3,0,2:T(8,128)(2,1)S(1)} %maximum_bitcast_fusion) | data formatting | bytes 589824 | tf_op jit(solution)/shard_map/weights/transpose | solution.py:309
  19.1 0.0 copy-start.2
  19.2 1.1 %reshape.26.f_ref = bf16[9,32,512]{2,1,0:T(8,128)(2,1)S(1)} reshape(bf16[9,32,16,32]{3,2,1,0:T(8,128)(2,1)S(1)} %copy.7) | data formatting | bytes 589824 | tf_op jit(solution)/shard_map/weights/reshape | solution.py:309
  20.3 0.1 copy-done.2
  20.4 0.5 copy.6
  20.9 0.0 copy-start.3
  20.9 1.1 %reshape.25.f_ref = bf16[9,32,512]{2,1,0:T(8,128)(2,1)S(1)} reshape(bf16[9,32,16,32]{3,2,1,0:T(8,128)(2,1)S(1)} %copy.6) | data formatting | bytes 589824 | tf_op jit(solution)/shard_map/weights/reshape | solution.py:307
  22.0 3.9 %all-to-all-done.recv_ref = bf16[8,128,256]{2,1,0:T(8,128)(2,1)S(1)} async-done(((bf16[8,128,256]{2,1,0:T(8,128)(2,1)}), bf16[8,128,256]{2,1,0:T(8,128)(2,1)S(1)}, u32[]{:S(2)}, u32[]{:S(2)}) %all-to-all-start) | async-done | bytes 524320 | tf_op jit(solution)/shard_map/to_tiles/all_to_all | solution.py:305
  25.9 0.0 copy-done.3
  25.9 0.1 broadcast_in_dim.2.bias_ref
  26.0 3.7 %grad.1 = (bf16[512,256]{1,0:T(8,128)(2,1)S(1)}, f32[8,72,128]{2,1,0:T(8,128)S(1)}, f32[8,72,128]{2,1,0:T(8,128)S(1)}) custom-call(bf16[8,128,256]{2,1,0:T(8,128)(2,1)S(1)} %all-to-all-done.recv_ref, bf16[9,32,512]{2,1,0:T(8,128)(2,1)S(1)} %reshape.25.f_ref, f32[32,256]{1,0:T(8,128)S(1)} %broadcast_in_dim.2.bias_ref), custom_call_target="tpu_custom_call" | custom-call | flops 2415919104 | bytes 2000000 | tf_op jit(solution)/shard_map/grad/pallas_call | solution.py:314
  29.7 1.7 %collective-permute-start.2 = (f32[8,72,128]{2,1,0:T(8,128)S(1)}, f32[8,72,128]{2,1,0:T(8,128)S(1)}, u32[]{:S(2)}, u32[]{:S(2)}) collective-permute-start(f32[8,72,128]{2,1,0:T(8,128)S(1)} %get-tuple-element.21), channel_id=1, source_target_pairs={{0,1},{1,0},{2,3},{3,2},{4,5},{5,4},{6,7},{7,6},{8,9},{9,8},{10,11... | collective-permute-start | bytes 884744 | tf_op jit(solution)/shard_map/filter_core/ppermute | solution.py:336
  31.4 1.8 %input_grad.2 = bf16[512,128]{1,0:T(8,128)(2,1)S(1)} custom-call(bf16[512,256]{1,0:T(8,128)(2,1)S(1)} %get-tuple-element.22.g_ref, bf16[9,32,512]{2,1,0:T(8,128)(2,1)S(1)} %reshape.26.f_ref), custom_call_target="tpu_custom_call" | custom-call | flops 1207959552 | bytes 2000000 | tf_op jit(solution)/shard_map/input_grad/pallas_call | solution.py:338
  33.2 0.0 collective-permute-done.2.other_ref
  33.3 9.8 %all_to_all.10 = bf16[8,144,128]{2,1,0:T(8,128)(2,1)S(1)} all-to-all(bf16[8,144,128]{2,1,0:T(8,128)(2,1)S(1)} %to_channels.1), channel_id=1, replica_groups=mesh['rot'=8,'rows'=32] {'rot'}, dimensions={0} | all-to-all | bytes 589824 | tf_op jit(solution)/shard_map/to_channels/all_to_all | solution.py:350
  43.2 4.3 %collective-permute-start.3 = (f32[72,128]{1,0:T(8,128)S(1)}, f32[72,128]{1,0:T(8,128)S(1)}, u32[]{:S(2)}, u32[]{:S(2)}) collective-permute-start(f32[72,128]{1,0:T(8,128)S(1)} %convert_reduce_fusion), channel_id=1, source_target_pairs={{0,10},{1,11},{2,8},{3,9},{4,14},{5,15},{6,12},{7,13},{8,2},{9,3},... | collective-permute-start | bytes 110600 | tf_op jit(solution)/shard_map/filter_blocks/ppermute | solution.py:326
  47.4 0.1 collective-permute-start.4
  47.5 1.1 %collective-permute-start.5 = (f32[72,128]{1,0:T(8,128)S(1)}, f32[72,128]{1,0:T(8,128)S(1)}, u32[]{:S(2)}, u32[]{:S(2)}) collective-permute-start(f32[72,128]{1,0:T(8,128)S(1)} %convert_reduce_fusion), channel_id=1, source_target_pairs={{0,2},{1,3},{2,0},{3,1},{4,6},{5,7},{6,4},{7,5},{8,10},{9,11},{10,... | collective-permute-start | bytes 110600 | tf_op jit(solution)/shard_map/filter_blocks/ppermute | solution.py:326
  48.6 0.2 collective-permute-done.3
  48.8 2.4 %collective-permute-done.4 = f32[72,128]{1,0:T(8,128)S(1)} collective-permute-done((f32[72,128]{1,0:T(8,128)S(1)}, f32[72,128]{1,0:T(8,128)S(1)}, u32[]{:S(2)}, u32[]{:S(2)}) %collective-permute-start.4) | collective-permute-done | bytes 36896 | tf_op jit(solution)/shard_map/filter_blocks/ppermute | solution.py:326
  51.1 0.0 collective-permute-done.5
  51.1 5.3 %collective-permute-start.6 = (f32[72,128]{1,0:T(8,128)S(1)}, f32[72,128]{1,0:T(8,128)S(1)}, u32[]{:S(2)}, u32[]{:S(2)}) collective-permute-start(f32[72,128]{1,0:T(8,128)S(1)} %add_add_fusion.1), channel_id=1, source_target_pairs={{0,30},{1,31},{2,28},{3,29},{4,26},{5,27},{6,24},{7,25},{8,22},{9,... | collective-permute-start | bytes 110600 | tf_op jit(solution)/shard_map/filter_rows/ppermute | solution.py:326
  56.5 2.2 %collective-permute-start.7 = (f32[72,128]{1,0:T(8,128)S(1)}, f32[72,128]{1,0:T(8,128)S(1)}, u32[]{:S(2)}, u32[]{:S(2)}) collective-permute-start(f32[72,128]{1,0:T(8,128)S(1)} %add_add_fusion.1), channel_id=1, source_target_pairs={{0,24},{1,25},{2,26},{3,27},{4,28},{5,29},{6,30},{7,31},{8,16},{9,... | collective-permute-start | bytes 110600 | tf_op jit(solution)/shard_map/filter_rows/ppermute | solution.py:326
  58.6 0.0 collective-permute-start.8
  58.7 1.2 %input_grad.3 = bf16[512,128]{1,0:T(8,128)(2,1)} custom-call(bf16[8,64,128]{2,1,0:T(8,128)(2,1)S(1)} %slice.17.dx_ref), custom_call_target="tpu_custom_call" | custom-call | flops 67108864 | bytes 2000000 | tf_op jit(solution)/shard_map/input_grad/pallas_call | solution.py:354
  59.9 0.0 collective-permute-done.6
  59.9 1.8 %collective-permute-done.7 = f32[72,128]{1,0:T(8,128)S(1)} collective-permute-done((f32[72,128]{1,0:T(8,128)S(1)}, f32[72,128]{1,0:T(8,128)S(1)}, u32[]{:S(2)}, u32[]{:S(2)}) %collective-permute-start.7) | collective-permute-done | bytes 36896 | tf_op jit(solution)/shard_map/filter_rows/ppermute | solution.py:326
  61.7 1.0 %collective-permute-done.8 = f32[72,128]{1,0:T(8,128)S(1)} collective-permute-done((f32[72,128]{1,0:T(8,128)S(1)}, f32[72,128]{1,0:T(8,128)S(1)}, u32[]{:S(2)}, u32[]{:S(2)}) %collective-permute-start.8) | collective-permute-done | bytes 36896 | tf_op jit(solution)/shard_map/filter_rows/ppermute | solution.py:326
  62.7 4.1 %collective-permute-start.9 = (f32[72,128]{1,0:T(8,128)S(1)}, f32[72,128]{1,0:T(8,128)S(1)}, u32[]{:S(2)}, u32[]{:S(2)}) collective-permute-start(f32[72,128]{1,0:T(8,128)S(1)} %add_add_fusion.own_ref), channel_id=1, source_target_pairs={{0,1},{1,0},{2,3},{3,2},{4,5},{5,4},{6,7},{7,6},{8,9},{9,8},{10,11... | collective-permute-start | bytes 110600 | tf_op jit(solution)/shard_map/filter_out/ppermute | solution.py:363
  66.8 0.9 %collective-permute-done.9.other_ref = f32[72,128]{1,0:T(8,128)S(1)} collective-permute-done((f32[72,128]{1,0:T(8,128)S(1)}, f32[72,128]{1,0:T(8,128)S(1)}, u32[]{:S(2)}, u32[]{:S(2)}) %collective-permute-start.9) | collective-permute-done | bytes 36896 | tf_op jit(solution)/shard_map/filter_out/ppermute | solution.py:363
  67.6 0.8 %filter_out.1 = f32[2,9,32,32]{3,2,1,0:T(8,128)} custom-call(f32[72,128]{1,0:T(8,128)S(1)} %add_add_fusion.own_ref, f32[72,128]{1,0:T(8,128)S(1)} %collective-permute-done.9.other_ref), custom_call_target="tpu_custom_call" | custom-call | flops 1000 | bytes 2000000 | tf_op jit(solution)/shard_map/filter_out/pallas_call | solution.py:364
  (6 shorter events, 0.1 us)
Async XLA Ops:
  2.5 7.4 %collective-permute-start = (bf16[2,128,128]{2,1,0:T(8,128)(2,1)}, bf16[2,128,128]{2,1,0:T(8,128)(2,1)S(1)}, u32[]{:S(2)}, u32[]{:S(2)}) collective-permute-start(bf16[2,128,128]{2,1,0:T(8,128)(2,1)} %get-tuple-element.15), channel_id=1, source_target_pairs={{1,2},{2,1},{3,4},{4,3},{5,6},{6,5},{7,8},{8,7},{9,10},{10,9},{11,... | collective-permute-start | bytes 196616 | tf_op jit(solution)/shard_map/edge_rows/ppermute | solution.py:292
  7.1 2.8 %collective-permute-start.1 = (bf16[2,128,128]{2,1,0:T(8,128)(2,1)}, bf16[2,128,128]{2,1,0:T(8,128)(2,1)S(1)}, u32[]{:S(2)}, u32[]{:S(2)}) collective-permute-start(bf16[2,128,128]{2,1,0:T(8,128)(2,1)} %get-tuple-element.16), channel_id=1, source_target_pairs={{0,1},{1,0},{2,3},{3,2},{4,5},{5,4},{6,7},{7,6},{8,9},{9,8},{10,11... | collective-permute-start | bytes 196616 | tf_op jit(solution)/shard_map/edge_rows/ppermute | solution.py:293
  7.2 0.9 %copy-start = (bf16[64,8,128]{2,1,0:T(8,128)(2,1)S(1)}, bf16[64,8,128]{2,1,0:T(8,128)(2,1)}, u32[]{:S(2)}) copy-start(bf16[64,8,128]{2,1,0:T(8,128)(2,1)} %param.4) | copy-start | bytes 393220
  8.1 0.9 %copy-start.1 = (bf16[64,8,128]{2,1,0:T(8,128)(2,1)S(1)}, bf16[64,8,128]{2,1,0:T(8,128)(2,1)}, u32[]{:S(2)}) copy-start(bf16[64,8,128]{2,1,0:T(8,128)(2,1)} %param.5) | copy-start | bytes 393220
  11.1 14.7 %all-to-all-start = ((bf16[8,128,256]{2,1,0:T(8,128)(2,1)}), bf16[8,128,256]{2,1,0:T(8,128)(2,1)S(1)}, u32[]{:S(2)}, u32[]{:S(2)}) async-start(bf16[8,128,256]{2,1,0:T(8,128)(2,1)} %to_tiles.3), calls=%async_computation | async-start | bytes 1048576 | tf_op jit(solution)/shard_map/to_tiles/all_to_all | solution.py:305
  16.5 1.2 %slice-start = ((bf16[16,9,32,32]{3,2,1,0:T(8,128)(2,1)}), bf16[15,9,32,32]{3,2,1,0:T(8,128)(2,1)S(1)}, s32[]{:S(2)}) async-start(bf16[16,9,32,32]{3,2,1,0:T(8,128)(2,1)} %param.6), calls=%async_computation.2 | async-start | bytes 2211840 | tf_op jit(solution)/shard_map/weights/slice | solution.py:308
  16.5 1.4 %slice-start.1 = ((bf16[16,9,32,32]{3,2,1,0:T(8,128)(2,1)}), bf16[1,9,32,32]{3,2,1,0:T(8,128)(2,1)S(1)}, s32[]{:S(2)}) async-start(bf16[16,9,32,32]{3,2,1,0:T(8,128)(2,1)} %param.6), calls=%async_computation.3 | async-start | bytes 147456 | tf_op jit(solution)/shard_map/weights/slice | solution.py:308
  19.1 1.3 %copy-start.2 = (bf16[16,9,32,32]{3,2,1,0:T(8,128)(2,1)S(1)}, bf16[16,9,32,32]{3,2,1,0:T(8,128)(2,1)}, u32[]{:S(2)}) copy-start(bf16[16,9,32,32]{3,2,1,0:T(8,128)(2,1)} %param.6) | copy-start | bytes 884740
  20.9 5.0 %copy-start.3 = (f32[32]{0:T(128)S(1)}, f32[32]{0:T(128)}, u32[]{:S(2)}) copy-start(f32[32]{0:T(128)} %param.7) | copy-start | bytes 388
  29.7 3.6 %collective-permute-start.2 = (f32[8,72,128]{2,1,0:T(8,128)S(1)}, f32[8,72,128]{2,1,0:T(8,128)S(1)}, u32[]{:S(2)}, u32[]{:S(2)}) collective-permute-start(f32[8,72,128]{2,1,0:T(8,128)S(1)} %get-tuple-element.21), channel_id=1, source_target_pairs={{0,1},{1,0},{2,3},{3,2},{4,5},{5,4},{6,7},{7,6},{8,9},{9,8},{10,11... | collective-permute-start | bytes 884744 | tf_op jit(solution)/shard_map/filter_core/ppermute | solution.py:336
  43.2 5.6 %collective-permute-start.3 = (f32[72,128]{1,0:T(8,128)S(1)}, f32[72,128]{1,0:T(8,128)S(1)}, u32[]{:S(2)}, u32[]{:S(2)}) collective-permute-start(f32[72,128]{1,0:T(8,128)S(1)} %convert_reduce_fusion), channel_id=1, source_target_pairs={{0,10},{1,11},{2,8},{3,9},{4,14},{5,15},{6,12},{7,13},{8,2},{9,3},... | collective-permute-start | bytes 110600 | tf_op jit(solution)/shard_map/filter_blocks/ppermute | solution.py:326
  47.4 3.7 %collective-permute-start.4 = (f32[72,128]{1,0:T(8,128)S(1)}, f32[72,128]{1,0:T(8,128)S(1)}, u32[]{:S(2)}, u32[]{:S(2)}) collective-permute-start(f32[72,128]{1,0:T(8,128)S(1)} %convert_reduce_fusion), channel_id=1, source_target_pairs={{0,8},{1,9},{2,10},{3,11},{4,12},{5,13},{6,14},{7,15},{8,0},{9,1},... | collective-permute-start | bytes 110600 | tf_op jit(solution)/shard_map/filter_blocks/ppermute | solution.py:326
  47.5 3.6 %collective-permute-start.5 = (f32[72,128]{1,0:T(8,128)S(1)}, f32[72,128]{1,0:T(8,128)S(1)}, u32[]{:S(2)}, u32[]{:S(2)}) collective-permute-start(f32[72,128]{1,0:T(8,128)S(1)} %convert_reduce_fusion), channel_id=1, source_target_pairs={{0,2},{1,3},{2,0},{3,1},{4,6},{5,7},{6,4},{7,5},{8,10},{9,11},{10,... | collective-permute-start | bytes 110600 | tf_op jit(solution)/shard_map/filter_blocks/ppermute | solution.py:326
  51.1 8.7 %collective-permute-start.6 = (f32[72,128]{1,0:T(8,128)S(1)}, f32[72,128]{1,0:T(8,128)S(1)}, u32[]{:S(2)}, u32[]{:S(2)}) collective-permute-start(f32[72,128]{1,0:T(8,128)S(1)} %add_add_fusion.1), channel_id=1, source_target_pairs={{0,30},{1,31},{2,28},{3,29},{4,26},{5,27},{6,24},{7,25},{8,22},{9,... | collective-permute-start | bytes 110600 | tf_op jit(solution)/shard_map/filter_rows/ppermute | solution.py:326
  56.5 5.2 %collective-permute-start.7 = (f32[72,128]{1,0:T(8,128)S(1)}, f32[72,128]{1,0:T(8,128)S(1)}, u32[]{:S(2)}, u32[]{:S(2)}) collective-permute-start(f32[72,128]{1,0:T(8,128)S(1)} %add_add_fusion.1), channel_id=1, source_target_pairs={{0,24},{1,25},{2,26},{3,27},{4,28},{5,29},{6,30},{7,31},{8,16},{9,... | collective-permute-start | bytes 110600 | tf_op jit(solution)/shard_map/filter_rows/ppermute | solution.py:326
  58.6 4.0 %collective-permute-start.8 = (f32[72,128]{1,0:T(8,128)S(1)}, f32[72,128]{1,0:T(8,128)S(1)}, u32[]{:S(2)}, u32[]{:S(2)}) collective-permute-start(f32[72,128]{1,0:T(8,128)S(1)} %add_add_fusion.1), channel_id=1, source_target_pairs={{0,6},{1,7},{2,4},{3,5},{4,2},{5,3},{6,0},{7,1},{8,14},{9,15},{10,... | collective-permute-start | bytes 110600 | tf_op jit(solution)/shard_map/filter_rows/ppermute | solution.py:326
  62.7 5.0 %collective-permute-start.9 = (f32[72,128]{1,0:T(8,128)S(1)}, f32[72,128]{1,0:T(8,128)S(1)}, u32[]{:S(2)}, u32[]{:S(2)}) collective-permute-start(f32[72,128]{1,0:T(8,128)S(1)} %add_add_fusion.own_ref), channel_id=1, source_target_pairs={{0,1},{1,0},{2,3},{3,2},{4,5},{5,4},{6,7},{7,6},{8,9},{9,8},{10,11... | collective-permute-start | bytes 110600 | tf_op jit(solution)/shard_map/filter_out/ppermute | solution.py:363

commit v6 on v5

--- a/solution.py
+++ b/solution.py
@@ -288,7 +288,7 @@
     with jax.named_scope("edge_rows"):
         x, c = inputs.reshape(n, width), cotangent.reshape(n, width)
         edge = shaped((HALO, 2 * local, width), BF16)
-        far, near = call(functools.partial(ends_kernel, band), (edge, edge), 1000, limit=60)(x, c)
+        far, near = call(functools.partial(ends_kernel, band), (edge, edge), 1000)(x, c)
         far = lax.ppermute(far, "rows", across)
         near = lax.ppermute(near, "rows", swap)
     with jax.named_scope("to_tiles"):
@@ -322,6 +322,8 @@
         return i + (pair(now) - now) * along
 
     def add_four(v, pair, beside=None):
+        v = v.astype(BF16)
+
         def swapped(to):
             return lax.ppermute(v, "rows", [(i, to(i)) for i in range(bands)])
 
@@ -330,6 +332,7 @@
         wide = swapped(lambda i: met(i, 2, pair))
         if beside is not None:
             both, deep, wide, beside = lax.optimization_barrier((both, deep, wide, beside))
+        v, both, deep, wide = [t.astype(F32) for t in (v, both, deep, wide)]
         return (v + both) + (deep + wide), beside
 
     with jax.named_scope("filter_core"):

time: 68.8 us -> 67 us (0.974)
  Pallas kernels: 11.6 us -> 10 us
    pallas_call x1, Pallas kernels: 1.89 us -> 0.29 us  [shards(): call(functools.partial(ends_kernel, band), (edge, edge), 1000)(x, c)]
    ppermute x6, waiting for transfers between devices: 5.29 us -> 3.76 us  [swapped(): return lax.ppermute(v, 'rows', [(i, to(i)) for i in range(bands)])]
    all_to_all x1, waiting for transfers between devices: 3.86 us -> 4.91 us  [shards(): recv = lax.all_to_all(packed, 'rot', 0, 0, tiled=True)]
    ppermute x1, starting transfers between devices: 1.73 us -> 0.73 us  [shards(): other = lax.ppermute(give, 'rows', swap)]
    ppermute x1, waiting for transfers between devices: 0.01 us -> 0.91 us  [shards(): far = lax.ppermute(far, 'rows', across)]
  transfers between devices with their start and end apart: 11 -> 11, of which waited for: 6 -> 5; matrix products, arithmetic and copies ran while one was open for 6% -> 6% of each run, Pallas kernels for 6% -> 6%
where the time goes in v6:
time: 67 us; the launch traced here: 66.7 us
  starting transfers between devices  28.3 us (42%)
  waiting for transfers between devices  10.5 us (16%)
  Pallas kernels  10 us (15%)
  blocking collectives  9.75 us (15%)
  local copies, waits for them, and re-layouts  7.1 us (11%)
  between operations  0.79 us (1%)
    ppermute x6, starting transfers between devices, swapped(): return lax.ppermute(v, 'rows', [(i, to(i)) for i in range(bands)])  13.3 us
    all_to_all x1, blocking collectives, shards(): got = lax.all_to_all(sent, 'rot', 0, 0, tiled=True)  9.75 us
    all_to_all x1, starting transfers between devices, shards(): recv = lax.all_to_all(packed, 'rot', 0, 0, tiled=True)  5.37 us
    all_to_all x1, waiting for transfers between devices, shards(): recv = lax.all_to_all(packed, 'rot', 0, 0, tiled=True)  4.91 us
    ppermute x1, starting transfers between devices, shards(): far = lax.ppermute(far, 'rows', across)  4.6 us
    ppermute x1, starting transfers between devices, shards(): other = lax.ppermute(v, 'rows', swap)  4.22 us
    ppermute x6, waiting for transfers between devices, swapped(): return lax.ppermute(v, 'rows', [(i, to(i)) for i in range(bands)])  3.76 us
    pallas_call x1, Pallas kernels, shards(): call(functools.partial(grad_kernel, band, cols), (shaped((n, size), BF16)...  3.73 us
  transfers between devices with their start and end apart: 11, of which 5 were waited for; matrix products, arithmetic and copies ran while one was open for 6% of the time, Pallas kernels for 6%

profile of v6, /device:TPU:1, one launch (start us, length us, event | category | flops | bytes accessed | tf_op | source)
XLA Modules:
  0.0 66.7 jit_solution(11180952038524035220)
XLA Ops:
  0.6 0.0 copy-start
  0.6 0.9 %copy-done = bf16[64,8,128]{2,1,0:T(8,128)(2,1)S(1)} copy-done((bf16[64,8,128]{2,1,0:T(8,128)(2,1)S(1)}, bf16[64,8,128]{2,1,0:T(8,128)(2,1)}, u32[]{:S(2)}) %copy-start) | copy-done | bytes 131096
  1.5 0.0 copy-start.1
  1.5 0.9 %copy-done.1 = bf16[64,8,128]{2,1,0:T(8,128)(2,1)S(1)} copy-done((bf16[64,8,128]{2,1,0:T(8,128)(2,1)S(1)}, bf16[64,8,128]{2,1,0:T(8,128)(2,1)}, u32[]{:S(2)}) %copy-start.1) | copy-done | bytes 131096
  2.4 0.3 edge_rows.1
  2.7 4.6 %collective-permute-start = (bf16[2,128,128]{2,1,0:T(8,128)(2,1)S(1)}, bf16[2,128,128]{2,1,0:T(8,128)(2,1)S(1)}, u32[]{:S(2)}, u32[]{:S(2)}) collective-permute-start(bf16[2,128,128]{2,1,0:T(8,128)(2,1)S(1)} %get-tuple-element.15), channel_id=1, source_target_pairs={{1,2},{2,1},{3,4},{4,3},{5,6},{6,5},{7,8},{8,7},{9,10},{10,9},{11,... | collective-permute-start | bytes 196616 | tf_op jit(solution)/shard_map/edge_rows/ppermute | solution.py:292
  7.3 0.1 collective-permute-start.1
  7.4 0.9 %to_tiles.2.own_ref = bf16[8,128,256]{2,1,0:T(8,128)(2,1)S(1)} custom-call(bf16[512,128]{1,0:T(8,128)(2,1)S(1)} %bitcast.12, bf16[512,128]{1,0:T(8,128)(2,1)S(1)} %bitcast.14), custom_call_target="tpu_custom_call" | custom-call | flops 134217728 | bytes 2000000 | tf_op jit(solution)/shard_map/to_tiles/pallas_call | solution.py:296
  8.4 0.9 %collective-permute-done.far_ref = bf16[2,128,128]{2,1,0:T(8,128)(2,1)S(1)} collective-permute-done((bf16[2,128,128]{2,1,0:T(8,128)(2,1)S(1)}, bf16[2,128,128]{2,1,0:T(8,128)(2,1)S(1)}, u32[]{:S(2)}, u32[]{:S(2)}) %collective-permute-start) | collective-permute-done | bytes 65568 | tf_op jit(solution)/shard_map/edge_rows/ppermute | solution.py:292
  9.3 0.0 collective-permute-done.1.near_ref
  9.3 1.1 %to_tiles.3 = bf16[8,128,256]{2,1,0:T(8,128)(2,1)} custom-call(bf16[8,128,256]{2,1,0:T(8,128)(2,1)S(1)} %to_tiles.2.own_ref, bf16[2,128,128]{2,1,0:T(8,128)(2,1)S(1)} %collective-permute-done.far_ref, bf16[2,128,128]{2,1,0:T(8,128)(2,1)S(1)} %collective-permute-done.1.near_ref), custom_call_target="tpu_custom_call" | custom-call | flops 1000 | bytes 2000000 | tf_op jit(solution)/shard_map/to_tiles/pallas_call | solution.py:299
  10.4 5.4 %all-to-all-start = ((bf16[8,128,256]{2,1,0:T(8,128)(2,1)}), bf16[8,128,256]{2,1,0:T(8,128)(2,1)S(1)}, u32[]{:S(2)}, u32[]{:S(2)}) async-start(bf16[8,128,256]{2,1,0:T(8,128)(2,1)} %to_tiles.3), calls=%async_computation | async-start | bytes 1048576 | tf_op jit(solution)/shard_map/to_tiles/all_to_all | solution.py:305
  15.8 0.0 slice-start.1
  15.8 1.2 %slice-done = bf16[15,9,32,32]{3,2,1,0:T(8,128)(2,1)S(1)} async-done(((bf16[16,9,32,32]{3,2,1,0:T(8,128)(2,1)}), bf16[15,9,32,32]{3,2,1,0:T(8,128)(2,1)S(1)}, s32[]{:S(2)}) %slice-start) | async-done | bytes 276504 | tf_op jit(solution)/shard_map/weights/slice | solution.py:308
  17.0 0.2 rev.3
  17.2 0.0 slice-done.1
  17.2 0.2 maximum_bitcast_fusion
  17.5 0.9 %copy.7 = bf16[9,32,16,32]{3,2,1,0:T(8,128)(2,1)S(1)} copy(bf16[9,32,16,32]{1,3,0,2:T(8,128)(2,1)S(1)} %maximum_bitcast_fusion) | data formatting | bytes 589824 | tf_op jit(solution)/shard_map/weights/transpose | solution.py:309
  18.4 0.0 copy-start.2
  18.4 1.1 %reshape.26.f_ref = bf16[9,32,512]{2,1,0:T(8,128)(2,1)S(1)} reshape(bf16[9,32,16,32]{3,2,1,0:T(8,128)(2,1)S(1)} %copy.7) | data formatting | bytes 589824 | tf_op jit(solution)/shard_map/weights/reshape | solution.py:309
  19.6 0.1 copy-done.2
  19.7 0.5 copy.6
  20.2 0.0 copy-start.3
  20.2 1.1 %reshape.25.f_ref = bf16[9,32,512]{2,1,0:T(8,128)(2,1)S(1)} reshape(bf16[9,32,16,32]{3,2,1,0:T(8,128)(2,1)S(1)} %copy.6) | data formatting | bytes 589824 | tf_op jit(solution)/shard_map/weights/reshape | solution.py:307
  21.3 4.9 %all-to-all-done.recv_ref = bf16[8,128,256]{2,1,0:T(8,128)(2,1)S(1)} async-done(((bf16[8,128,256]{2,1,0:T(8,128)(2,1)}), bf16[8,128,256]{2,1,0:T(8,128)(2,1)S(1)}, u32[]{:S(2)}, u32[]{:S(2)}) %all-to-all-start) | async-done | bytes 524320 | tf_op jit(solution)/shard_map/to_tiles/all_to_all | solution.py:305
  26.2 0.0 copy-done.3
  26.2 0.1 broadcast_in_dim.2.bias_ref
  26.3 3.7 %grad.1 = (bf16[512,256]{1,0:T(8,128)(2,1)S(1)}, f32[8,72,128]{2,1,0:T(8,128)S(1)}, f32[8,72,128]{2,1,0:T(8,128)S(1)}) custom-call(bf16[8,128,256]{2,1,0:T(8,128)(2,1)S(1)} %all-to-all-done.recv_ref, bf16[9,32,512]{2,1,0:T(8,128)(2,1)S(1)} %reshape.25.f_ref, f32[32,256]{1,0:T(8,128)S(1)} %broadcast_in_dim.2.bias_ref), custom_call_target="tpu_custom_call" | custom-call | flops 2415919104 | bytes 2000000 | tf_op jit(solution)/shard_map/grad/pallas_call | solution.py:314
  30.0 0.7 %collective-permute-start.2 = (f32[8,72,128]{2,1,0:T(8,128)S(1)}, f32[8,72,128]{2,1,0:T(8,128)S(1)}, u32[]{:S(2)}, u32[]{:S(2)}) collective-permute-start(f32[8,72,128]{2,1,0:T(8,128)S(1)} %get-tuple-element.21), channel_id=1, source_target_pairs={{0,1},{1,0},{2,3},{3,2},{4,5},{5,4},{6,7},{7,6},{8,9},{9,8},{10,11... | collective-permute-start | bytes 884744 | tf_op jit(solution)/shard_map/filter_core/ppermute | solution.py:339
  30.8 1.8 %input_grad.2 = bf16[512,128]{1,0:T(8,128)(2,1)S(1)} custom-call(bf16[512,256]{1,0:T(8,128)(2,1)S(1)} %get-tuple-element.22.g_ref, bf16[9,32,512]{2,1,0:T(8,128)(2,1)S(1)} %reshape.26.f_ref), custom_call_target="tpu_custom_call" | custom-call | flops 1207959552 | bytes 2000000 | tf_op jit(solution)/shard_map/input_grad/pallas_call | solution.py:341
  32.6 0.0 collective-permute-done.2.other_ref
  32.6 9.8 %all_to_all.10 = bf16[8,144,128]{2,1,0:T(8,128)(2,1)S(1)} all-to-all(bf16[8,144,128]{2,1,0:T(8,128)(2,1)S(1)} %to_channels.1), channel_id=1, replica_groups=mesh['rot'=8,'rows'=32] {'rot'}, dimensions={0} | all-to-all | bytes 589824 | tf_op jit(solution)/shard_map/to_channels/all_to_all | solution.py:353
  42.4 4.5 %collective-permute-start.3 = (bf16[72,128]{1,0:T(8,128)(2,1)S(1)}, bf16[72,128]{1,0:T(8,128)(2,1)S(1)}, u32[]{:S(2)}, u32[]{:S(2)}) collective-permute-start(bf16[72,128]{1,0:T(8,128)(2,1)S(1)} %slice_reduce_fusion), channel_id=1, source_target_pairs={{0,10},{1,11},{2,8},{3,9},{4,14},{5,15},{6,12},{7,13},{8,2},{9,3},... | collective-permute-start | bytes 55304 | tf_op jit(solution)/shard_map/filter_blocks/ppermute | solution.py:328
  46.9 0.7 %collective-permute-start.4 = (bf16[72,128]{1,0:T(8,128)(2,1)S(1)}, bf16[72,128]{1,0:T(8,128)(2,1)S(1)}, u32[]{:S(2)}, u32[]{:S(2)}) collective-permute-start(bf16[72,128]{1,0:T(8,128)(2,1)S(1)} %slice_reduce_fusion), channel_id=1, source_target_pairs={{0,8},{1,9},{2,10},{3,11},{4,12},{5,13},{6,14},{7,15},{8,0},{9,1},... | collective-permute-start | bytes 55304 | tf_op jit(solution)/shard_map/filter_blocks/ppermute | solution.py:328
  47.5 1.1 %collective-permute-start.5 = (bf16[72,128]{1,0:T(8,128)(2,1)S(1)}, bf16[72,128]{1,0:T(8,128)(2,1)S(1)}, u32[]{:S(2)}, u32[]{:S(2)}) collective-permute-start(bf16[72,128]{1,0:T(8,128)(2,1)S(1)} %slice_reduce_fusion), channel_id=1, source_target_pairs={{0,2},{1,3},{2,0},{3,1},{4,6},{5,7},{6,4},{7,5},{8,10},{9,11},{10,... | collective-permute-start | bytes 55304 | tf_op jit(solution)/shard_map/filter_blocks/ppermute | solution.py:328
  48.6 0.0 collective-permute-done.3
  48.6 1.9 %collective-permute-done.4 = bf16[72,128]{1,0:T(8,128)(2,1)S(1)} collective-permute-done((bf16[72,128]{1,0:T(8,128)(2,1)S(1)}, bf16[72,128]{1,0:T(8,128)(2,1)S(1)}, u32[]{:S(2)}, u32[]{:S(2)}) %collective-permute-start.4) | collective-permute-done | bytes 18464 | tf_op jit(solution)/shard_map/filter_blocks/ppermute | solution.py:328
  50.5 0.0 collective-permute-done.5
  50.5 5.2 %collective-permute-start.6 = (bf16[72,128]{1,0:T(8,128)(2,1)S(1)}, bf16[72,128]{1,0:T(8,128)(2,1)S(1)}, u32[]{:S(2)}, u32[]{:S(2)}) collective-permute-start(bf16[72,128]{1,0:T(8,128)(2,1)S(1)} %add_convert_fusion), channel_id=1, source_target_pairs={{0,30},{1,31},{2,28},{3,29},{4,26},{5,27},{6,24},{7,25},{8,22},{9,... | collective-permute-start | bytes 55304 | tf_op jit(solution)/shard_map/filter_rows/ppermute | solution.py:328
  55.7 0.2 collective-permute-start.7
  55.9 1.7 %collective-permute-start.8 = (bf16[72,128]{1,0:T(8,128)(2,1)S(1)}, bf16[72,128]{1,0:T(8,128)(2,1)S(1)}, u32[]{:S(2)}, u32[]{:S(2)}) collective-permute-start(bf16[72,128]{1,0:T(8,128)(2,1)S(1)} %add_convert_fusion), channel_id=1, source_target_pairs={{0,6},{1,7},{2,4},{3,5},{4,2},{5,3},{6,0},{7,1},{8,14},{9,15},{10,... | collective-permute-start | bytes 55304 | tf_op jit(solution)/shard_map/filter_rows/ppermute | solution.py:328
  57.6 1.2 %input_grad.3 = bf16[512,128]{1,0:T(8,128)(2,1)} custom-call(bf16[8,64,128]{2,1,0:T(8,128)(2,1)S(1)} %slice.17.dx_ref), custom_call_target="tpu_custom_call" | custom-call | flops 67108864 | bytes 2000000 | tf_op jit(solution)/shard_map/input_grad/pallas_call | solution.py:357
  58.9 0.0 collective-permute-done.6
  58.9 1.9 %collective-permute-done.7 = bf16[72,128]{1,0:T(8,128)(2,1)S(1)} collective-permute-done((bf16[72,128]{1,0:T(8,128)(2,1)S(1)}, bf16[72,128]{1,0:T(8,128)(2,1)S(1)}, u32[]{:S(2)}, u32[]{:S(2)}) %collective-permute-start.7) | collective-permute-done | bytes 18464 | tf_op jit(solution)/shard_map/filter_rows/ppermute | solution.py:328
  60.8 0.0 collective-permute-done.8
  60.8 4.2 %collective-permute-start.9 = (f32[72,128]{1,0:T(8,128)S(1)}, f32[72,128]{1,0:T(8,128)S(1)}, u32[]{:S(2)}, u32[]{:S(2)}) collective-permute-start(f32[72,128]{1,0:T(8,128)S(1)} %add_add_fusion.own_ref), channel_id=1, source_target_pairs={{0,1},{1,0},{2,3},{3,2},{4,5},{5,4},{6,7},{7,6},{8,9},{9,8},{10,11... | collective-permute-start | bytes 110600 | tf_op jit(solution)/shard_map/filter_out/ppermute | solution.py:366
  65.0 0.9 %collective-permute-done.9.other_ref = f32[72,128]{1,0:T(8,128)S(1)} collective-permute-done((f32[72,128]{1,0:T(8,128)S(1)}, f32[72,128]{1,0:T(8,128)S(1)}, u32[]{:S(2)}, u32[]{:S(2)}) %collective-permute-start.9) | collective-permute-done | bytes 36896 | tf_op jit(solution)/shard_map/filter_out/ppermute | solution.py:366
  65.9 0.8 %filter_out.1 = f32[2,9,32,32]{3,2,1,0:T(8,128)} custom-call(f32[72,128]{1,0:T(8,128)S(1)} %add_add_fusion.own_ref, f32[72,128]{1,0:T(8,128)S(1)} %collective-permute-done.9.other_ref), custom_call_target="tpu_custom_call" | custom-call | flops 1000 | bytes 2000000 | tf_op jit(solution)/shard_map/filter_out/pallas_call | solution.py:367
  (6 shorter events, 0.1 us)
Async XLA Ops:
  0.6 0.9 %copy-start = (bf16[64,8,128]{2,1,0:T(8,128)(2,1)S(1)}, bf16[64,8,128]{2,1,0:T(8,128)(2,1)}, u32[]{:S(2)}) copy-start(bf16[64,8,128]{2,1,0:T(8,128)(2,1)} %param.4) | copy-start | bytes 393220
  1.5 0.9 %copy-start.1 = (bf16[64,8,128]{2,1,0:T(8,128)(2,1)S(1)}, bf16[64,8,128]{2,1,0:T(8,128)(2,1)}, u32[]{:S(2)}) copy-start(bf16[64,8,128]{2,1,0:T(8,128)(2,1)} %param.5) | copy-start | bytes 393220
  2.7 6.5 %collective-permute-start = (bf16[2,128,128]{2,1,0:T(8,128)(2,1)S(1)}, bf16[2,128,128]{2,1,0:T(8,128)(2,1)S(1)}, u32[]{:S(2)}, u32[]{:S(2)}) collective-permute-start(bf16[2,128,128]{2,1,0:T(8,128)(2,1)S(1)} %get-tuple-element.15), channel_id=1, source_target_pairs={{1,2},{2,1},{3,4},{4,3},{5,6},{6,5},{7,8},{8,7},{9,10},{10,9},{11,... | collective-permute-start | bytes 196616 | tf_op jit(solution)/shard_map/edge_rows/ppermute | solution.py:292
  7.3 1.9 %collective-permute-start.1 = (bf16[2,128,128]{2,1,0:T(8,128)(2,1)S(1)}, bf16[2,128,128]{2,1,0:T(8,128)(2,1)S(1)}, u32[]{:S(2)}, u32[]{:S(2)}) collective-permute-start(bf16[2,128,128]{2,1,0:T(8,128)(2,1)S(1)} %get-tuple-element.16), channel_id=1, source_target_pairs={{0,1},{1,0},{2,3},{3,2},{4,5},{5,4},{6,7},{7,6},{8,9},{9,8},{10,11... | collective-permute-start | bytes 196616 | tf_op jit(solution)/shard_map/edge_rows/ppermute | solution.py:293
  10.4 15.8 %all-to-all-start = ((bf16[8,128,256]{2,1,0:T(8,128)(2,1)}), bf16[8,128,256]{2,1,0:T(8,128)(2,1)S(1)}, u32[]{:S(2)}, u32[]{:S(2)}) async-start(bf16[8,128,256]{2,1,0:T(8,128)(2,1)} %to_tiles.3), calls=%async_computation | async-start | bytes 1048576 | tf_op jit(solution)/shard_map/to_tiles/all_to_all | solution.py:305
  15.8 1.2 %slice-start = ((bf16[16,9,32,32]{3,2,1,0:T(8,128)(2,1)}), bf16[15,9,32,32]{3,2,1,0:T(8,128)(2,1)S(1)}, s32[]{:S(2)}) async-start(bf16[16,9,32,32]{3,2,1,0:T(8,128)(2,1)} %param.6), calls=%async_computation.2 | async-start | bytes 2211840 | tf_op jit(solution)/shard_map/weights/slice | solution.py:308
  15.8 1.4 %slice-start.1 = ((bf16[16,9,32,32]{3,2,1,0:T(8,128)(2,1)}), bf16[1,9,32,32]{3,2,1,0:T(8,128)(2,1)S(1)}, s32[]{:S(2)}) async-start(bf16[16,9,32,32]{3,2,1,0:T(8,128)(2,1)} %param.6), calls=%async_computation.3 | async-start | bytes 147456 | tf_op jit(solution)/shard_map/weights/slice | solution.py:308
  18.4 1.3 %copy-start.2 = (bf16[16,9,32,32]{3,2,1,0:T(8,128)(2,1)S(1)}, bf16[16,9,32,32]{3,2,1,0:T(8,128)(2,1)}, u32[]{:S(2)}) copy-start(bf16[16,9,32,32]{3,2,1,0:T(8,128)(2,1)} %param.6) | copy-start | bytes 884740
  20.2 6.1 %copy-start.3 = (f32[32]{0:T(128)S(1)}, f32[32]{0:T(128)}, u32[]{:S(2)}) copy-start(f32[32]{0:T(128)} %param.7) | copy-start | bytes 388
  30.0 2.6 %collective-permute-start.2 = (f32[8,72,128]{2,1,0:T(8,128)S(1)}, f32[8,72,128]{2,1,0:T(8,128)S(1)}, u32[]{:S(2)}, u32[]{:S(2)}) collective-permute-start(f32[8,72,128]{2,1,0:T(8,128)S(1)} %get-tuple-element.21), channel_id=1, source_target_pairs={{0,1},{1,0},{2,3},{3,2},{4,5},{5,4},{6,7},{7,6},{8,9},{9,8},{10,11... | collective-permute-start | bytes 884744 | tf_op jit(solution)/shard_map/filter_core/ppermute | solution.py:339
  42.4 6.2 %collective-permute-start.3 = (bf16[72,128]{1,0:T(8,128)(2,1)S(1)}, bf16[72,128]{1,0:T(8,128)(2,1)S(1)}, u32[]{:S(2)}, u32[]{:S(2)}) collective-permute-start(bf16[72,128]{1,0:T(8,128)(2,1)S(1)} %slice_reduce_fusion), channel_id=1, source_target_pairs={{0,10},{1,11},{2,8},{3,9},{4,14},{5,15},{6,12},{7,13},{8,2},{9,3},... | collective-permute-start | bytes 55304 | tf_op jit(solution)/shard_map/filter_blocks/ppermute | solution.py:328
  46.9 3.6 %collective-permute-start.4 = (bf16[72,128]{1,0:T(8,128)(2,1)S(1)}, bf16[72,128]{1,0:T(8,128)(2,1)S(1)}, u32[]{:S(2)}, u32[]{:S(2)}) collective-permute-start(bf16[72,128]{1,0:T(8,128)(2,1)S(1)} %slice_reduce_fusion), channel_id=1, source_target_pairs={{0,8},{1,9},{2,10},{3,11},{4,12},{5,13},{6,14},{7,15},{8,0},{9,1},... | collective-permute-start | bytes 55304 | tf_op jit(solution)/shard_map/filter_blocks/ppermute | solution.py:328
  47.5 3.0 %collective-permute-start.5 = (bf16[72,128]{1,0:T(8,128)(2,1)S(1)}, bf16[72,128]{1,0:T(8,128)(2,1)S(1)}, u32[]{:S(2)}, u32[]{:S(2)}) collective-permute-start(bf16[72,128]{1,0:T(8,128)(2,1)S(1)} %slice_reduce_fusion), channel_id=1, source_target_pairs={{0,2},{1,3},{2,0},{3,1},{4,6},{5,7},{6,4},{7,5},{8,10},{9,11},{10,... | collective-permute-start | bytes 55304 | tf_op jit(solution)/shard_map/filter_blocks/ppermute | solution.py:328
  50.5 8.4 %collective-permute-start.6 = (bf16[72,128]{1,0:T(8,128)(2,1)S(1)}, bf16[72,128]{1,0:T(8,128)(2,1)S(1)}, u32[]{:S(2)}, u32[]{:S(2)}) collective-permute-start(bf16[72,128]{1,0:T(8,128)(2,1)S(1)} %add_convert_fusion), channel_id=1, source_target_pairs={{0,30},{1,31},{2,28},{3,29},{4,26},{5,27},{6,24},{7,25},{8,22},{9,... | collective-permute-start | bytes 55304 | tf_op jit(solution)/shard_map/filter_rows/ppermute | solution.py:328
  55.7 5.1 %collective-permute-start.7 = (bf16[72,128]{1,0:T(8,128)(2,1)S(1)}, bf16[72,128]{1,0:T(8,128)(2,1)S(1)}, u32[]{:S(2)}, u32[]{:S(2)}) collective-permute-start(bf16[72,128]{1,0:T(8,128)(2,1)S(1)} %add_convert_fusion), channel_id=1, source_target_pairs={{0,24},{1,25},{2,26},{3,27},{4,28},{5,29},{6,30},{7,31},{8,16},{9,... | collective-permute-start | bytes 55304 | tf_op jit(solution)/shard_map/filter_rows/ppermute | solution.py:328
  55.9 4.9 %collective-permute-start.8 = (bf16[72,128]{1,0:T(8,128)(2,1)S(1)}, bf16[72,128]{1,0:T(8,128)(2,1)S(1)}, u32[]{:S(2)}, u32[]{:S(2)}) collective-permute-start(bf16[72,128]{1,0:T(8,128)(2,1)S(1)} %add_convert_fusion), channel_id=1, source_target_pairs={{0,6},{1,7},{2,4},{3,5},{4,2},{5,3},{6,0},{7,1},{8,14},{9,15},{10,... | collective-permute-start | bytes 55304 | tf_op jit(solution)/shard_map/filter_rows/ppermute | solution.py:328
  60.8 5.1 %collective-permute-start.9 = (f32[72,128]{1,0:T(8,128)S(1)}, f32[72,128]{1,0:T(8,128)S(1)}, u32[]{:S(2)}, u32[]{:S(2)}) collective-permute-start(f32[72,128]{1,0:T(8,128)S(1)} %add_add_fusion.own_ref), channel_id=1, source_target_pairs={{0,1},{1,0},{2,3},{3,2},{4,5},{5,4},{6,7},{7,6},{8,9},{9,8},{10,11... | collective-permute-start | bytes 110600 | tf_op jit(solution)/shard_map/filter_out/ppermute | solution.py:366

commit v7 on v6

--- a/solution.py
+++ b/solution.py
@@ -123,7 +123,7 @@
     return jnp.concatenate([v[:, by:], v[:, :by]], axis=1) if by else v
 
 
-def grad_kernel(band, cols, recv_ref, f_ref, bias_ref, g_ref, keep_ref, give_ref, xt_ref, w_ref):
+def grad_kernel(band, cols, recv_ref, f_ref, bias_ref, g_ref, part_ref, xt_ref, w_ref):
     groups, both, size = recv_ref.shape
     half = both // 2
     n = groups * half
@@ -185,15 +185,9 @@
                 v = pltpu.roll(pieces[t], by, 1) if by else pieces[t]
                 out = v if out is None else jnp.where(where == t, v, out)
             taken.append(out)
-    core = lax.axis_index("rows") % 2
-    for c in range(2):
-
-        @pl.when(core == c)
-        def _():
-            for ref, part in ((keep_ref, c), (give_ref, 1 - c)):
-                for k in range(groups):
-                    ref[k, : 2 * CH] = taken[2 * (2 * k + part)]
-                    ref[k, 2 * CH :] = taken[2 * (2 * k + part) + 1]
+    for at, v in enumerate(taken):
+        start = at // 2 % 2 * 9 * 8 + at % 2 * 2 * CH
+        part_ref[at // 4, start : start + v.shape[0]] = v
 
 
 def input_kernel(band, cols, g_ref, f_ref, out_ref, w_ref):
@@ -221,13 +215,11 @@
     out_ref[...] = out
 
 
-def join_kernel(keep_ref, other_ref, dx_ref, out_ref):
-    groups, terms, width = keep_ref.shape
+def join_kernel(part_ref, other_ref, dx_ref, out_ref):
+    groups, terms, width = part_ref.shape
     local = dx_ref.shape[1]
     out_ref[:, :local] = dx_ref[...]
-    sums = keep_ref[...] + other_ref[...]
-    pad = jnp.zeros((groups, out_ref.shape[1] - local - terms, width), F32)
-    out_ref[:, local:] = jnp.concatenate([sums, pad], axis=1).astype(BF16)
+    out_ref[:, local:] = (part_ref[...] + other_ref[...]).astype(BF16)
 
 
 def unpack_kernel(band, cols, dx_ref, out_ref):
@@ -243,19 +235,14 @@
     out_ref[...] = exchanged(jnp.concatenate(rows, axis=0), band, False)
 
 
-def out_kernel(scale, own_ref, other_ref, out_ref):
-    core = lax.axis_index("rows") % 2
-    for c in range(2):
-
-        @pl.when(core == c)
-        def _():
-            for ref, part in ((own_ref, c), (other_ref, 1 - c)):
-                v = ref[...] * scale
-                for tap in range(8):
-                    row, at = CH * (tap % 2), CH * (tap // 2)
-                    out_ref[part, tap] = v[row : row + CH, at : at + CH]
-                for t in range(4):
-                    out_ref[part, 8, 8 * t : 8 * (t + 1)] = v[2 * CH :, CH * t : CH * (t + 1)]
+def out_kernel(scale, v_ref, out_ref):
+    for part in range(2):
+        v = v_ref[9 * 8 * part : 9 * 8 * (part + 1)] * scale
+        for tap in range(8):
+            row, at = CH * (tap % 2), CH * (tap // 2)
+            out_ref[part, tap] = v[row : row + CH, at : at + CH]
+        for t in range(4):
+            out_ref[part, 8, 8 * t : 8 * (t + 1)] = v[2 * CH :, CH * t : CH * (t + 1)]
 
 
 def shaped(shape, dtype):
@@ -310,10 +297,9 @@
         bias2 = jnp.broadcast_to(bias[:, None], (CH, size))
         recv, fwd, bwd, bias2 = lax.optimization_barrier((recv, fwd, bwd, bias2))
     with jax.named_scope("grad"):
-        half = shaped((groups, 9 * 8, 4 * CH), F32)
-        g, keep, give = call(
+        g, part = call(
             functools.partial(grad_kernel, band, cols),
-            (shaped((n, size), BF16), half, half),
+            (shaped((n, size), BF16), shaped((groups, 2 * 9 * 8, 4 * CH), F32)),
             2 * 18 * n * n * size,
             [pltpu.VMEM((4, size, 2 * n), BF16), square],
         )(recv, fwd, bias2)
@@ -336,7 +322,7 @@
         return (v + both) + (deep + wide), beside
 
     with jax.named_scope("filter_core"):
-        other = lax.ppermute(give, "rows", swap)
+        other = lax.ppermute(part, "rows", swap)
     with jax.named_scope("input_grad"):
         dx = call(
             functools.partial(input_kernel, band, cols),
@@ -345,10 +331,10 @@
             [square],
         )(g, bwd)
     with jax.named_scope("to_channels"):
-        terms = keep.shape[1]
-        block = local + -(-terms // 16) * 16
+        terms = part.shape[1]
+        block = local + terms
         sent = call(join_kernel, shaped((groups, block, width), BF16), 1000)(
-            keep, other, dx.reshape(groups, local, width)
+            part, other, dx.reshape(groups, local, width)
         )
         got = lax.all_to_all(sent, "rot", 0, 0, tiled=True)
     with jax.named_scope("filter_rot"):
@@ -363,10 +349,9 @@
         v, input_grad = add_four(v, lambda k: 3 - k, input_grad)
     with jax.named_scope("filter_out"):
         scale = float(rotations * band * bands * width) ** (-0.5)
-        other = lax.ppermute(v, "rows", swap)
         filter_grad = call(
             functools.partial(out_kernel, scale), shaped((2, taps, CH, CH), F32), 1000
-        )(v, other)
+        )(v)
     return input_grad, filter_grad
 
 

time: 67 us -> 66.1 us (0.987)
  the two profiles are of different devices: /device:TPU:1 before, /device:TPU:16 now
where the time goes in v7:
time: 66.1 us; the launch traced here: 65.8 us
  starting transfers between devices  21.1 us (32%)
  waiting for transfers between devices  14.2 us (21%)
  blocking collectives  12.3 us (19%)
  Pallas kernels  9.99 us (15%)
  local copies, waits for them, and re-layouts  7.1 us (11%)
  between operations  0.78 us (1%)
    all_to_all x1, blocking collectives, shards(): got = lax.all_to_all(sent, 'rot', 0, 0, tiled=True)  12.3 us
    ppermute x6, starting transfers between devices, swapped(): return lax.ppermute(v, 'rows', [(i, to(i)) for i in range(bands)])  12 us
    ppermute x6, waiting for transfers between devices, swapped(): return lax.ppermute(v, 'rows', [(i, to(i)) for i in range(bands)])  7.96 us
    all_to_all x1, starting transfers between devices, shards(): recv = lax.all_to_all(packed, 'rot', 0, 0, tiled=True)  5.65 us
    all_to_all x1, waiting for transfers between devices, shards(): recv = lax.all_to_all(packed, 'rot', 0, 0, tiled=True)  4.85 us
    pallas_call x1, Pallas kernels, shards(): call(functools.partial(grad_kernel, band, cols), (shaped((n, size), BF16)...  3.69 us
    unnamed x8, local copies, waits for them, and re-layouts  1.93 us
    ppermute x1, starting transfers between devices, shards(): far = lax.ppermute(far, 'rows', across)  1.92 us
  transfers between devices with their start and end apart: 10, of which 7 were waited for; matrix products, arithmetic and copies ran while one was open for 6% of the time, Pallas kernels for 6%

profile of v7, /device:TPU:16, one launch (start us, length us, event | category | flops | bytes accessed | tf_op | source)
XLA Modules:
  0.0 65.8 jit_solution(12609884838954590454)
XLA Ops:
  0.6 0.0 copy-start
  0.6 0.9 %copy-done = bf16[64,8,128]{2,1,0:T(8,128)(2,1)S(1)} copy-done((bf16[64,8,128]{2,1,0:T(8,128)(2,1)S(1)}, bf16[64,8,128]{2,1,0:T(8,128)(2,1)}, u32[]{:S(2)}) %copy-start) | copy-done | bytes 131096
  1.5 0.0 copy-start.1
  1.5 0.9 %copy-done.1 = bf16[64,8,128]{2,1,0:T(8,128)(2,1)S(1)} copy-done((bf16[64,8,128]{2,1,0:T(8,128)(2,1)S(1)}, bf16[64,8,128]{2,1,0:T(8,128)(2,1)}, u32[]{:S(2)}) %copy-start.1) | copy-done | bytes 131096
  2.4 0.3 edge_rows.1
  2.7 1.9 %collective-permute-start = (bf16[2,128,128]{2,1,0:T(8,128)(2,1)S(1)}, bf16[2,128,128]{2,1,0:T(8,128)(2,1)S(1)}, u32[]{:S(2)}, u32[]{:S(2)}) collective-permute-start(bf16[2,128,128]{2,1,0:T(8,128)(2,1)S(1)} %get-tuple-element.14), channel_id=1, source_target_pairs={{1,2},{2,1},{3,4},{4,3},{5,6},{6,5},{7,8},{8,7},{9,10},{10,9},{11,... | collective-permute-start | bytes 196616 | tf_op jit(solution)/shard_map/edge_rows/ppermute | solution.py:279
  4.7 1.5 %collective-permute-start.1 = (bf16[2,128,128]{2,1,0:T(8,128)(2,1)S(1)}, bf16[2,128,128]{2,1,0:T(8,128)(2,1)S(1)}, u32[]{:S(2)}, u32[]{:S(2)}) collective-permute-start(bf16[2,128,128]{2,1,0:T(8,128)(2,1)S(1)} %get-tuple-element.15), channel_id=1, source_target_pairs={{0,1},{1,0},{2,3},{3,2},{4,5},{5,4},{6,7},{7,6},{8,9},{9,8},{10,11... | collective-permute-start | bytes 196616 | tf_op jit(solution)/shard_map/edge_rows/ppermute | solution.py:280
  6.1 0.9 %to_tiles.2.own_ref = bf16[8,128,256]{2,1,0:T(8,128)(2,1)S(1)} custom-call(bf16[512,128]{1,0:T(8,128)(2,1)S(1)} %bitcast.12, bf16[512,128]{1,0:T(8,128)(2,1)S(1)} %bitcast.14), custom_call_target="tpu_custom_call" | custom-call | flops 134217728 | bytes 2000000 | tf_op jit(solution)/shard_map/to_tiles/pallas_call | solution.py:283
  7.1 1.3 %collective-permute-done.far_ref = bf16[2,128,128]{2,1,0:T(8,128)(2,1)S(1)} collective-permute-done((bf16[2,128,128]{2,1,0:T(8,128)(2,1)S(1)}, bf16[2,128,128]{2,1,0:T(8,128)(2,1)S(1)}, u32[]{:S(2)}, u32[]{:S(2)}) %collective-permute-start) | collective-permute-done | bytes 65568 | tf_op jit(solution)/shard_map/edge_rows/ppermute | solution.py:279
  8.3 0.0 collective-permute-done.1.near_ref
  8.3 1.2 %to_tiles.3 = bf16[8,128,256]{2,1,0:T(8,128)(2,1)} custom-call(bf16[8,128,256]{2,1,0:T(8,128)(2,1)S(1)} %to_tiles.2.own_ref, bf16[2,128,128]{2,1,0:T(8,128)(2,1)S(1)} %collective-permute-done.far_ref, bf16[2,128,128]{2,1,0:T(8,128)(2,1)S(1)} %collective-permute-done.1.near_ref), custom_call_target="tpu_custom_call" | custom-call | flops 1000 | bytes 2000000 | tf_op jit(solution)/shard_map/to_tiles/pallas_call | solution.py:286
  9.5 5.7 %all-to-all-start = ((bf16[8,128,256]{2,1,0:T(8,128)(2,1)}), bf16[8,128,256]{2,1,0:T(8,128)(2,1)S(1)}, u32[]{:S(2)}, u32[]{:S(2)}) async-start(bf16[8,128,256]{2,1,0:T(8,128)(2,1)} %to_tiles.3), calls=%async_computation | async-start | bytes 1048576 | tf_op jit(solution)/shard_map/to_tiles/all_to_all | solution.py:292
  15.1 0.0 slice-start
  15.1 0.0 slice-start.1
  15.1 1.2 %slice-done = bf16[15,9,32,32]{3,2,1,0:T(8,128)(2,1)S(1)} async-done(((bf16[16,9,32,32]{3,2,1,0:T(8,128)(2,1)}), bf16[15,9,32,32]{3,2,1,0:T(8,128)(2,1)S(1)}, s32[]{:S(2)}) %slice-start) | async-done | bytes 276504 | tf_op jit(solution)/shard_map/weights/slice | solution.py:295
  16.4 0.2 rev.3
  16.6 0.0 slice-done.1
  16.6 0.2 maximum_bitcast_fusion
  16.8 0.9 %copy.7 = bf16[9,32,16,32]{3,2,1,0:T(8,128)(2,1)S(1)} copy(bf16[9,32,16,32]{1,3,0,2:T(8,128)(2,1)S(1)} %maximum_bitcast_fusion) | data formatting | bytes 589824 | tf_op jit(solution)/shard_map/weights/transpose | solution.py:296
  17.8 0.0 copy-start.2
  17.8 1.1 %reshape.26.f_ref = bf16[9,32,512]{2,1,0:T(8,128)(2,1)S(1)} reshape(bf16[9,32,16,32]{3,2,1,0:T(8,128)(2,1)S(1)} %copy.7) | data formatting | bytes 589824 | tf_op jit(solution)/shard_map/weights/reshape | solution.py:296
  18.9 0.1 copy-done.2
  19.0 0.5 copy.6
  19.5 0.0 copy-start.3
  19.5 1.1 %reshape.25.f_ref = bf16[9,32,512]{2,1,0:T(8,128)(2,1)S(1)} reshape(bf16[9,32,16,32]{3,2,1,0:T(8,128)(2,1)S(1)} %copy.6) | data formatting | bytes 589824 | tf_op jit(solution)/shard_map/weights/reshape | solution.py:294
  20.6 4.8 %all-to-all-done.recv_ref = bf16[8,128,256]{2,1,0:T(8,128)(2,1)S(1)} async-done(((bf16[8,128,256]{2,1,0:T(8,128)(2,1)}), bf16[8,128,256]{2,1,0:T(8,128)(2,1)S(1)}, u32[]{:S(2)}, u32[]{:S(2)}) %all-to-all-start) | async-done | bytes 524320 | tf_op jit(solution)/shard_map/to_tiles/all_to_all | solution.py:292
  25.5 0.0 copy-done.3
  25.5 0.1 broadcast_in_dim.2.bias_ref
  25.6 3.7 %grad.1 = (bf16[512,256]{1,0:T(8,128)(2,1)S(1)}, f32[8,144,128]{2,1,0:T(8,128)S(1)}) custom-call(bf16[8,128,256]{2,1,0:T(8,128)(2,1)S(1)} %all-to-all-done.recv_ref, bf16[9,32,512]{2,1,0:T(8,128)(2,1)S(1)} %reshape.25.f_ref, f32[32,256]{1,0:T(8,128)S(1)} %broadcast_in_dim.2.bias_ref), custom_call_target="tpu_custom_call" | custom-call | flops 2415919104 | bytes 2000000 | tf_op jit(solution)/shard_map/grad/pallas_call | solution.py:300
  29.3 0.1 collective-permute-start.2
  29.4 1.8 %input_grad.2 = bf16[512,128]{1,0:T(8,128)(2,1)S(1)} custom-call(bf16[512,256]{1,0:T(8,128)(2,1)S(1)} %get-tuple-element.20.g_ref, bf16[9,32,512]{2,1,0:T(8,128)(2,1)S(1)} %reshape.26.f_ref), custom_call_target="tpu_custom_call" | custom-call | flops 1207959552 | bytes 2000000 | tf_op jit(solution)/shard_map/input_grad/pallas_call | solution.py:327
  31.2 0.2 collective-permute-done.2.other_ref
  31.4 0.1 to_channels.1
  31.4 12.3 %all_to_all.10 = bf16[8,208,128]{2,1,0:T(8,128)(2,1)S(1)} all-to-all(bf16[8,208,128]{2,1,0:T(8,128)(2,1)S(1)} %to_channels.1), channel_id=1, replica_groups=mesh['rot'=8,'rows'=32] {'rot'}, dimensions={0} | all-to-all | bytes 851968 | tf_op jit(solution)/shard_map/to_channels/all_to_all | solution.py:339
  43.7 5.6 %collective-permute-start.3 = (bf16[144,128]{1,0:T(8,128)(2,1)S(1)}, bf16[144,128]{1,0:T(8,128)(2,1)S(1)}, u32[]{:S(2)}, u32[]{:S(2)}) collective-permute-start(bf16[144,128]{1,0:T(8,128)(2,1)S(1)} %slice_reduce_fusion), channel_id=1, source_target_pairs={{0,10},{1,11},{2,8},{3,9},{4,14},{5,15},{6,12},{7,13},{8,2},{9,3},... | collective-permute-start | bytes 110600 | tf_op jit(solution)/shard_map/filter_blocks/ppermute | solution.py:314
  49.3 0.0 collective-permute-start.4
  49.4 0.7 %collective-permute-start.5 = (bf16[144,128]{1,0:T(8,128)(2,1)S(1)}, bf16[144,128]{1,0:T(8,128)(2,1)S(1)}, u32[]{:S(2)}, u32[]{:S(2)}) collective-permute-start(bf16[144,128]{1,0:T(8,128)(2,1)S(1)} %slice_reduce_fusion), channel_id=1, source_target_pairs={{0,2},{1,3},{2,0},{3,1},{4,6},{5,7},{6,4},{7,5},{8,10},{9,11},{10,... | collective-permute-start | bytes 110600 | tf_op jit(solution)/shard_map/filter_blocks/ppermute | solution.py:314
  50.0 2.0 %collective-permute-done.3 = bf16[144,128]{1,0:T(8,128)(2,1)S(1)} collective-permute-done((bf16[144,128]{1,0:T(8,128)(2,1)S(1)}, bf16[144,128]{1,0:T(8,128)(2,1)S(1)}, u32[]{:S(2)}, u32[]{:S(2)}) %collective-permute-start.3) | collective-permute-done | bytes 36896 | tf_op jit(solution)/shard_map/filter_blocks/ppermute | solution.py:314
  52.1 2.5 %collective-permute-done.4 = bf16[144,128]{1,0:T(8,128)(2,1)S(1)} collective-permute-done((bf16[144,128]{1,0:T(8,128)(2,1)S(1)}, bf16[144,128]{1,0:T(8,128)(2,1)S(1)}, u32[]{:S(2)}, u32[]{:S(2)}) %collective-permute-start.4) | collective-permute-done | bytes 36896 | tf_op jit(solution)/shard_map/filter_blocks/ppermute | solution.py:314
  54.6 0.0 collective-permute-done.5
  54.6 4.2 %collective-permute-start.6 = (bf16[144,128]{1,0:T(8,128)(2,1)S(1)}, bf16[144,128]{1,0:T(8,128)(2,1)S(1)}, u32[]{:S(2)}, u32[]{:S(2)}) collective-permute-start(bf16[144,128]{1,0:T(8,128)(2,1)S(1)} %add_convert_fusion), channel_id=1, source_target_pairs={{0,30},{1,31},{2,28},{3,29},{4,26},{5,27},{6,24},{7,25},{8,22},{9,... | collective-permute-start | bytes 110600 | tf_op jit(solution)/shard_map/filter_rows/ppermute | solution.py:314
  58.9 0.0 collective-permute-start.7
  58.9 1.4 %collective-permute-start.8 = (bf16[144,128]{1,0:T(8,128)(2,1)S(1)}, bf16[144,128]{1,0:T(8,128)(2,1)S(1)}, u32[]{:S(2)}, u32[]{:S(2)}) collective-permute-start(bf16[144,128]{1,0:T(8,128)(2,1)S(1)} %add_convert_fusion), channel_id=1, source_target_pairs={{0,6},{1,7},{2,4},{3,5},{4,2},{5,3},{6,0},{7,1},{8,14},{9,15},{10,... | collective-permute-start | bytes 110600 | tf_op jit(solution)/shard_map/filter_rows/ppermute | solution.py:314
  60.3 1.2 %input_grad.3 = bf16[512,128]{1,0:T(8,128)(2,1)} custom-call(bf16[8,64,128]{2,1,0:T(8,128)(2,1)S(1)} %slice.17.dx_ref), custom_call_target="tpu_custom_call" | custom-call | flops 67108864 | bytes 2000000 | tf_op jit(solution)/shard_map/input_grad/pallas_call | solution.py:343
  61.6 0.1 collective-permute-done.6
  61.7 3.2 %collective-permute-done.7 = bf16[144,128]{1,0:T(8,128)(2,1)S(1)} collective-permute-done((bf16[144,128]{1,0:T(8,128)(2,1)S(1)}, bf16[144,128]{1,0:T(8,128)(2,1)S(1)}, u32[]{:S(2)}, u32[]{:S(2)}) %collective-permute-start.7) | collective-permute-done | bytes 36896 | tf_op jit(solution)/shard_map/filter_rows/ppermute | solution.py:314
  64.9 0.0 collective-permute-done.8
  65.0 0.8 %filter_out.1 = f32[2,9,32,32]{3,2,1,0:T(8,128)} custom-call(f32[144,128]{1,0:T(8,128)S(1)} %add_add_fusion.v_ref), custom_call_target="tpu_custom_call" | custom-call | flops 1000 | bytes 2000000 | tf_op jit(solution)/shard_map/filter_out/pallas_call | solution.py:352
  (4 shorter events, 0.1 us)
Async XLA Ops:
  0.6 0.9 %copy-start = (bf16[64,8,128]{2,1,0:T(8,128)(2,1)S(1)}, bf16[64,8,128]{2,1,0:T(8,128)(2,1)}, u32[]{:S(2)}) copy-start(bf16[64,8,128]{2,1,0:T(8,128)(2,1)} %param.4) | copy-start | bytes 393220
  1.5 0.9 %copy-start.1 = (bf16[64,8,128]{2,1,0:T(8,128)(2,1)S(1)}, bf16[64,8,128]{2,1,0:T(8,128)(2,1)}, u32[]{:S(2)}) copy-start(bf16[64,8,128]{2,1,0:T(8,128)(2,1)} %param.5) | copy-start | bytes 393220
  2.7 5.6 %collective-permute-start = (bf16[2,128,128]{2,1,0:T(8,128)(2,1)S(1)}, bf16[2,128,128]{2,1,0:T(8,128)(2,1)S(1)}, u32[]{:S(2)}, u32[]{:S(2)}) collective-permute-start(bf16[2,128,128]{2,1,0:T(8,128)(2,1)S(1)} %get-tuple-element.14), channel_id=1, source_target_pairs={{1,2},{2,1},{3,4},{4,3},{5,6},{6,5},{7,8},{8,7},{9,10},{10,9},{11,... | collective-permute-start | bytes 196616 | tf_op jit(solution)/shard_map/edge_rows/ppermute | solution.py:279
  4.7 3.7 %collective-permute-start.1 = (bf16[2,128,128]{2,1,0:T(8,128)(2,1)S(1)}, bf16[2,128,128]{2,1,0:T(8,128)(2,1)S(1)}, u32[]{:S(2)}, u32[]{:S(2)}) collective-permute-start(bf16[2,128,128]{2,1,0:T(8,128)(2,1)S(1)} %get-tuple-element.15), channel_id=1, source_target_pairs={{0,1},{1,0},{2,3},{3,2},{4,5},{5,4},{6,7},{7,6},{8,9},{9,8},{10,11... | collective-permute-start | bytes 196616 | tf_op jit(solution)/shard_map/edge_rows/ppermute | solution.py:280
  9.5 16.0 %all-to-all-start = ((bf16[8,128,256]{2,1,0:T(8,128)(2,1)}), bf16[8,128,256]{2,1,0:T(8,128)(2,1)S(1)}, u32[]{:S(2)}, u32[]{:S(2)}) async-start(bf16[8,128,256]{2,1,0:T(8,128)(2,1)} %to_tiles.3), calls=%async_computation | async-start | bytes 1048576 | tf_op jit(solution)/shard_map/to_tiles/all_to_all | solution.py:292
  15.1 1.2 %slice-start = ((bf16[16,9,32,32]{3,2,1,0:T(8,128)(2,1)}), bf16[15,9,32,32]{3,2,1,0:T(8,128)(2,1)S(1)}, s32[]{:S(2)}) async-start(bf16[16,9,32,32]{3,2,1,0:T(8,128)(2,1)} %param.6), calls=%async_computation.2 | async-start | bytes 2211840 | tf_op jit(solution)/shard_map/weights/slice | solution.py:295
  15.1 1.4 %slice-start.1 = ((bf16[16,9,32,32]{3,2,1,0:T(8,128)(2,1)}), bf16[1,9,32,32]{3,2,1,0:T(8,128)(2,1)S(1)}, s32[]{:S(2)}) async-start(bf16[16,9,32,32]{3,2,1,0:T(8,128)(2,1)} %param.6), calls=%async_computation.3 | async-start | bytes 147456 | tf_op jit(solution)/shard_map/weights/slice | solution.py:295
  17.8 1.3 %copy-start.2 = (bf16[16,9,32,32]{3,2,1,0:T(8,128)(2,1)S(1)}, bf16[16,9,32,32]{3,2,1,0:T(8,128)(2,1)}, u32[]{:S(2)}) copy-start(bf16[16,9,32,32]{3,2,1,0:T(8,128)(2,1)} %param.6) | copy-start | bytes 884740
  19.5 6.0 %copy-start.3 = (f32[32]{0:T(128)S(1)}, f32[32]{0:T(128)}, u32[]{:S(2)}) copy-start(f32[32]{0:T(128)} %param.7) | copy-start | bytes 388
  29.3 2.1 %collective-permute-start.2 = (f32[8,144,128]{2,1,0:T(8,128)S(1)}, f32[8,144,128]{2,1,0:T(8,128)S(1)}, u32[]{:S(2)}, u32[]{:S(2)}) collective-permute-start(f32[8,144,128]{2,1,0:T(8,128)S(1)} %get-tuple-element.19.part_ref), channel_id=1, source_target_pairs={{0,1},{1,0},{2,3},{3,2},{4,5},{5,4},{6,7},{7,6},{8,9},{9,8},{10,11... | collective-permute-start | bytes 1769480 | tf_op jit(solution)/shard_map/filter_core/ppermute | solution.py:325
  43.7 8.3 %collective-permute-start.3 = (bf16[144,128]{1,0:T(8,128)(2,1)S(1)}, bf16[144,128]{1,0:T(8,128)(2,1)S(1)}, u32[]{:S(2)}, u32[]{:S(2)}) collective-permute-start(bf16[144,128]{1,0:T(8,128)(2,1)S(1)} %slice_reduce_fusion), channel_id=1, source_target_pairs={{0,10},{1,11},{2,8},{3,9},{4,14},{5,15},{6,12},{7,13},{8,2},{9,3},... | collective-permute-start | bytes 110600 | tf_op jit(solution)/shard_map/filter_blocks/ppermute | solution.py:314
  49.3 5.3 %collective-permute-start.4 = (bf16[144,128]{1,0:T(8,128)(2,1)S(1)}, bf16[144,128]{1,0:T(8,128)(2,1)S(1)}, u32[]{:S(2)}, u32[]{:S(2)}) collective-permute-start(bf16[144,128]{1,0:T(8,128)(2,1)S(1)} %slice_reduce_fusion), channel_id=1, source_target_pairs={{0,8},{1,9},{2,10},{3,11},{4,12},{5,13},{6,14},{7,15},{8,0},{9,1},... | collective-permute-start | bytes 110600 | tf_op jit(solution)/shard_map/filter_blocks/ppermute | solution.py:314
  49.4 5.3 %collective-permute-start.5 = (bf16[144,128]{1,0:T(8,128)(2,1)S(1)}, bf16[144,128]{1,0:T(8,128)(2,1)S(1)}, u32[]{:S(2)}, u32[]{:S(2)}) collective-permute-start(bf16[144,128]{1,0:T(8,128)(2,1)S(1)} %slice_reduce_fusion), channel_id=1, source_target_pairs={{0,2},{1,3},{2,0},{3,1},{4,6},{5,7},{6,4},{7,5},{8,10},{9,11},{10,... | collective-permute-start | bytes 110600 | tf_op jit(solution)/shard_map/filter_blocks/ppermute | solution.py:314
  54.6 7.1 %collective-permute-start.6 = (bf16[144,128]{1,0:T(8,128)(2,1)S(1)}, bf16[144,128]{1,0:T(8,128)(2,1)S(1)}, u32[]{:S(2)}, u32[]{:S(2)}) collective-permute-start(bf16[144,128]{1,0:T(8,128)(2,1)S(1)} %add_convert_fusion), channel_id=1, source_target_pairs={{0,30},{1,31},{2,28},{3,29},{4,26},{5,27},{6,24},{7,25},{8,22},{9,... | collective-permute-start | bytes 110600 | tf_op jit(solution)/shard_map/filter_rows/ppermute | solution.py:314
  58.9 6.1 %collective-permute-start.7 = (bf16[144,128]{1,0:T(8,128)(2,1)S(1)}, bf16[144,128]{1,0:T(8,128)(2,1)S(1)}, u32[]{:S(2)}, u32[]{:S(2)}) collective-permute-start(bf16[144,128]{1,0:T(8,128)(2,1)S(1)} %add_convert_fusion), channel_id=1, source_target_pairs={{0,24},{1,25},{2,26},{3,27},{4,28},{5,29},{6,30},{7,31},{8,16},{9,... | collective-permute-start | bytes 110600 | tf_op jit(solution)/shard_map/filter_rows/ppermute | solution.py:314
  58.9 6.1 %collective-permute-start.8 = (bf16[144,128]{1,0:T(8,128)(2,1)S(1)}, bf16[144,128]{1,0:T(8,128)(2,1)S(1)}, u32[]{:S(2)}, u32[]{:S(2)}) collective-permute-start(bf16[144,128]{1,0:T(8,128)(2,1)S(1)} %add_convert_fusion), channel_id=1, source_target_pairs={{0,6},{1,7},{2,4},{3,5},{4,2},{5,3},{6,0},{7,1},{8,14},{9,15},{10,... | collective-permute-start | bytes 110600 | tf_op jit(solution)/shard_map/filter_rows/ppermute | solution.py:314

commit v8 on v7

--- a/solution.py
+++ b/solution.py
@@ -303,23 +303,19 @@
             2 * 18 * n * n * size,
             [pltpu.VMEM((4, size, 2 * n), BF16), square],
         )(recv, fwd, bias2)
-    def met(i, along, pair):
-        now = i // along % 4
-        return i + (pair(now) - now) * along
-
-    def add_four(v, pair, beside=None):
+    def turn(i, step, by):
+        now = i // step % 4
+        return i + ((now + by) % 4 - now) * step
+
+    def add_four(v, step, beside=None):
         v = v.astype(BF16)
-
-        def swapped(to):
-            return lax.ppermute(v, "rows", [(i, to(i)) for i in range(bands)])
-
-        both = swapped(lambda i: met(met(i, 2, pair), 8, pair))
-        deep = swapped(lambda i: met(i, 8, pair))
-        wide = swapped(lambda i: met(i, 2, pair))
+        far, near, back = [
+            lax.ppermute(v, "rows", [(i, turn(i, step, by)) for i in range(bands)]) for by in (2, 1, 3)
+        ]
         if beside is not None:
-            both, deep, wide, beside = lax.optimization_barrier((both, deep, wide, beside))
-        v, both, deep, wide = [t.astype(F32) for t in (v, both, deep, wide)]
-        return (v + both) + (deep + wide), beside
+            far, near, back, beside = lax.optimization_barrier((far, near, back, beside))
+        v, far, near, back = [t.astype(F32) for t in (v, far, near, back)]
+        return (v + far) + (near + back), beside
 
     with jax.named_scope("filter_core"):
         other = lax.ppermute(part, "rows", swap)
@@ -343,10 +339,10 @@
         input_grad = call(
             functools.partial(unpack_kernel, band, cols), shaped((n, width), BF16), 2 * n * n * width
         )(got[:, :local]).reshape(inputs.shape)
-    with jax.named_scope("filter_blocks"):
-        v, _ = add_four(v, lambda k: k ^ 1)
-    with jax.named_scope("filter_rows"):
-        v, input_grad = add_four(v, lambda k: 3 - k, input_grad)
+    with jax.named_scope("filter_y"):
+        v, _ = add_four(v, 2)
+    with jax.named_scope("filter_z"):
+        v, input_grad = add_four(v, 8, input_grad)
     with jax.named_scope("filter_out"):
         scale = float(rotations * band * bands * width) ** (-0.5)
         filter_grad = call(

time: 66.1 us -> 67 us (1.014)
  the two profiles are of different devices: /device:TPU:16 before, /device:TPU:24 now
where the time goes in v8:
time: 67 us; the launch traced here: 66.7 us
  starting transfers between devices  25.1 us (37%)
  blocking collectives  12.1 us (18%)
  waiting for transfers between devices  11.2 us (17%)
  Pallas kernels  10 us (15%)
  local copies, waits for them, and re-layouts  7.1 us (11%)
  between operations  0.79 us (1%)
    ppermute x6, starting transfers between devices, add_four(): lax.ppermute(v, 'rows', [(i, turn(i, step, by)) for i in range(bands)])  13.3 us
    all_to_all x1, blocking collectives, shards(): got = lax.all_to_all(sent, 'rot', 0, 0, tiled=True)  12.1 us
    ppermute x6, waiting for transfers between devices, add_four(): lax.ppermute(v, 'rows', [(i, turn(i, step, by)) for i in range(bands)])  6.45 us
    all_to_all x1, starting transfers between devices, shards(): recv = lax.all_to_all(packed, 'rot', 0, 0, tiled=True)  5.65 us
    all_to_all x1, waiting for transfers between devices, shards(): recv = lax.all_to_all(packed, 'rot', 0, 0, tiled=True)  4.78 us
    pallas_call x1, Pallas kernels, shards(): call(functools.partial(grad_kernel, band, cols), (shaped((n, size), BF16)...  3.69 us
    ppermute x1, starting transfers between devices, shards(): near = lax.ppermute(near, 'rows', swap)  2.95 us
    ppermute x1, starting transfers between devices, shards(): far = lax.ppermute(far, 'rows', across)  2.09 us
  transfers between devices with their start and end apart: 10, of which 5 were waited for; matrix products, arithmetic and copies ran while one was open for 6% of the time, Pallas kernels for 6%

profile of v8, /device:TPU:24, one launch (start us, length us, event | category | flops | bytes accessed | tf_op | source)
XLA Modules:
  0.0 66.7 jit_solution(14848037406046966985)
XLA Ops:
  0.6 0.0 copy-start
  0.6 0.9 %copy-done = bf16[64,8,128]{2,1,0:T(8,128)(2,1)S(1)} copy-done((bf16[64,8,128]{2,1,0:T(8,128)(2,1)S(1)}, bf16[64,8,128]{2,1,0:T(8,128)(2,1)}, u32[]{:S(2)}) %copy-start) | copy-done | bytes 131096
  1.5 0.0 copy-start.1
  1.5 0.9 %copy-done.1 = bf16[64,8,128]{2,1,0:T(8,128)(2,1)S(1)} copy-done((bf16[64,8,128]{2,1,0:T(8,128)(2,1)S(1)}, bf16[64,8,128]{2,1,0:T(8,128)(2,1)}, u32[]{:S(2)}) %copy-start.1) | copy-done | bytes 131096
  2.4 0.3 edge_rows.1
  2.7 2.1 %collective-permute-start = (bf16[2,128,128]{2,1,0:T(8,128)(2,1)S(1)}, bf16[2,128,128]{2,1,0:T(8,128)(2,1)S(1)}, u32[]{:S(2)}, u32[]{:S(2)}) collective-permute-start(bf16[2,128,128]{2,1,0:T(8,128)(2,1)S(1)} %get-tuple-element.14), channel_id=1, source_target_pairs={{1,2},{2,1},{3,4},{4,3},{5,6},{6,5},{7,8},{8,7},{9,10},{10,9},{11,... | collective-permute-start | bytes 196616 | tf_op jit(solution)/shard_map/edge_rows/ppermute | solution.py:279
  4.8 3.0 %collective-permute-start.1 = (bf16[2,128,128]{2,1,0:T(8,128)(2,1)S(1)}, bf16[2,128,128]{2,1,0:T(8,128)(2,1)S(1)}, u32[]{:S(2)}, u32[]{:S(2)}) collective-permute-start(bf16[2,128,128]{2,1,0:T(8,128)(2,1)S(1)} %get-tuple-element.15), channel_id=1, source_target_pairs={{0,1},{1,0},{2,3},{3,2},{4,5},{5,4},{6,7},{7,6},{8,9},{9,8},{10,11... | collective-permute-start | bytes 196616 | tf_op jit(solution)/shard_map/edge_rows/ppermute | solution.py:280
  7.8 0.9 %to_tiles.2.own_ref = bf16[8,128,256]{2,1,0:T(8,128)(2,1)S(1)} custom-call(bf16[512,128]{1,0:T(8,128)(2,1)S(1)} %bitcast.12, bf16[512,128]{1,0:T(8,128)(2,1)S(1)} %bitcast.14), custom_call_target="tpu_custom_call" | custom-call | flops 134217728 | bytes 2000000 | tf_op jit(solution)/shard_map/to_tiles/pallas_call | solution.py:283
  8.7 0.0 collective-permute-done.far_ref
  8.7 0.0 collective-permute-done.1.near_ref
  8.7 1.2 %to_tiles.3 = bf16[8,128,256]{2,1,0:T(8,128)(2,1)} custom-call(bf16[8,128,256]{2,1,0:T(8,128)(2,1)S(1)} %to_tiles.2.own_ref, bf16[2,128,128]{2,1,0:T(8,128)(2,1)S(1)} %collective-permute-done.far_ref, bf16[2,128,128]{2,1,0:T(8,128)(2,1)S(1)} %collective-permute-done.1.near_ref), custom_call_target="tpu_custom_call" | custom-call | flops 1000 | bytes 2000000 | tf_op jit(solution)/shard_map/to_tiles/pallas_call | solution.py:286
  9.9 5.7 %all-to-all-start = ((bf16[8,128,256]{2,1,0:T(8,128)(2,1)}), bf16[8,128,256]{2,1,0:T(8,128)(2,1)S(1)}, u32[]{:S(2)}, u32[]{:S(2)}) async-start(bf16[8,128,256]{2,1,0:T(8,128)(2,1)} %to_tiles.3), calls=%async_computation | async-start | bytes 1048576 | tf_op jit(solution)/shard_map/to_tiles/all_to_all | solution.py:292
  15.5 0.0 slice-start
  15.6 0.0 slice-start.1
  15.6 1.2 %slice-done = bf16[15,9,32,32]{3,2,1,0:T(8,128)(2,1)S(1)} async-done(((bf16[16,9,32,32]{3,2,1,0:T(8,128)(2,1)}), bf16[15,9,32,32]{3,2,1,0:T(8,128)(2,1)S(1)}, s32[]{:S(2)}) %slice-start) | async-done | bytes 276504 | tf_op jit(solution)/shard_map/weights/slice | solution.py:295
  16.8 0.2 rev.3
  17.0 0.0 slice-done.1
  17.0 0.2 maximum_bitcast_fusion
  17.2 0.9 %copy.7 = bf16[9,32,16,32]{3,2,1,0:T(8,128)(2,1)S(1)} copy(bf16[9,32,16,32]{1,3,0,2:T(8,128)(2,1)S(1)} %maximum_bitcast_fusion) | data formatting | bytes 589824 | tf_op jit(solution)/shard_map/weights/transpose | solution.py:296
  18.2 0.0 copy-start.2
  18.2 1.1 %reshape.26.f_ref = bf16[9,32,512]{2,1,0:T(8,128)(2,1)S(1)} reshape(bf16[9,32,16,32]{3,2,1,0:T(8,128)(2,1)S(1)} %copy.7) | data formatting | bytes 589824 | tf_op jit(solution)/shard_map/weights/reshape | solution.py:296
  19.3 0.1 copy-done.2
  19.5 0.5 copy.6
  19.9 0.0 copy-start.3
  19.9 1.1 %reshape.25.f_ref = bf16[9,32,512]{2,1,0:T(8,128)(2,1)S(1)} reshape(bf16[9,32,16,32]{3,2,1,0:T(8,128)(2,1)S(1)} %copy.6) | data formatting | bytes 589824 | tf_op jit(solution)/shard_map/weights/reshape | solution.py:294
  21.1 4.8 %all-to-all-done.recv_ref = bf16[8,128,256]{2,1,0:T(8,128)(2,1)S(1)} async-done(((bf16[8,128,256]{2,1,0:T(8,128)(2,1)}), bf16[8,128,256]{2,1,0:T(8,128)(2,1)S(1)}, u32[]{:S(2)}, u32[]{:S(2)}) %all-to-all-start) | async-done | bytes 524320 | tf_op jit(solution)/shard_map/to_tiles/all_to_all | solution.py:292
  25.8 0.0 copy-done.3
  25.8 0.1 broadcast_in_dim.2.bias_ref
  25.9 3.7 %grad.1 = (bf16[512,256]{1,0:T(8,128)(2,1)S(1)}, f32[8,144,128]{2,1,0:T(8,128)S(1)}) custom-call(bf16[8,128,256]{2,1,0:T(8,128)(2,1)S(1)} %all-to-all-done.recv_ref, bf16[9,32,512]{2,1,0:T(8,128)(2,1)S(1)} %reshape.25.f_ref, f32[32,256]{1,0:T(8,128)S(1)} %broadcast_in_dim.2.bias_ref), custom_call_target="tpu_custom_call" | custom-call | flops 2415919104 | bytes 2000000 | tf_op jit(solution)/shard_map/grad/pallas_call | solution.py:300
  29.6 1.1 %collective-permute-start.2 = (f32[8,144,128]{2,1,0:T(8,128)S(1)}, f32[8,144,128]{2,1,0:T(8,128)S(1)}, u32[]{:S(2)}, u32[]{:S(2)}) collective-permute-start(f32[8,144,128]{2,1,0:T(8,128)S(1)} %get-tuple-element.19.part_ref), channel_id=1, source_target_pairs={{0,1},{1,0},{2,3},{3,2},{4,5},{5,4},{6,7},{7,6},{8,9},{9,8},{10,11... | collective-permute-start | bytes 1769480 | tf_op jit(solution)/shard_map/filter_core/ppermute | solution.py:321
  30.7 1.8 %input_grad.2 = bf16[512,128]{1,0:T(8,128)(2,1)S(1)} custom-call(bf16[512,256]{1,0:T(8,128)(2,1)S(1)} %get-tuple-element.20.g_ref, bf16[9,32,512]{2,1,0:T(8,128)(2,1)S(1)} %reshape.26.f_ref), custom_call_target="tpu_custom_call" | custom-call | flops 1207959552 | bytes 2000000 | tf_op jit(solution)/shard_map/input_grad/pallas_call | solution.py:323
  32.5 0.0 collective-permute-done.2.other_ref
  32.6 0.1 to_channels.1
  32.6 12.1 %all_to_all.10 = bf16[8,208,128]{2,1,0:T(8,128)(2,1)S(1)} all-to-all(bf16[8,208,128]{2,1,0:T(8,128)(2,1)S(1)} %to_channels.1), channel_id=1, replica_groups=mesh['rot'=8,'rows'=32] {'rot'}, dimensions={0} | all-to-all | bytes 851968 | tf_op jit(solution)/shard_map/to_channels/all_to_all | solution.py:335
  44.8 0.5 collective-permute-start.3
  45.3 2.2 %collective-permute-start.4 = (bf16[144,128]{1,0:T(8,128)(2,1)S(1)}, bf16[144,128]{1,0:T(8,128)(2,1)S(1)}, u32[]{:S(2)}, u32[]{:S(2)}) collective-permute-start(bf16[144,128]{1,0:T(8,128)(2,1)S(1)} %slice_reduce_fusion), channel_id=1, source_target_pairs={{0,2},{1,3},{2,4},{3,5},{4,6},{5,7},{6,0},{7,1},{8,10},{9,11},{10,... | collective-permute-start | bytes 110600 | tf_op jit(solution)/shard_map/filter_y/ppermute | solution.py:313
  47.4 0.0 collective-permute-start.5
  47.4 3.1 %collective-permute-done.3 = bf16[144,128]{1,0:T(8,128)(2,1)S(1)} collective-permute-done((bf16[144,128]{1,0:T(8,128)(2,1)S(1)}, bf16[144,128]{1,0:T(8,128)(2,1)S(1)}, u32[]{:S(2)}, u32[]{:S(2)}) %collective-permute-start.3) | collective-permute-done | bytes 36896 | tf_op jit(solution)/shard_map/filter_y/ppermute | solution.py:313
  50.5 0.0 collective-permute-done.4
  50.5 2.1 %collective-permute-done.5 = bf16[144,128]{1,0:T(8,128)(2,1)S(1)} collective-permute-done((bf16[144,128]{1,0:T(8,128)(2,1)S(1)}, bf16[144,128]{1,0:T(8,128)(2,1)S(1)}, u32[]{:S(2)}, u32[]{:S(2)}) %collective-permute-start.5) | collective-permute-done | bytes 36896 | tf_op jit(solution)/shard_map/filter_y/ppermute | solution.py:313
  52.6 6.5 %collective-permute-start.6 = (bf16[144,128]{1,0:T(8,128)(2,1)S(1)}, bf16[144,128]{1,0:T(8,128)(2,1)S(1)}, u32[]{:S(2)}, u32[]{:S(2)}) collective-permute-start(bf16[144,128]{1,0:T(8,128)(2,1)S(1)} %add_convert_fusion), channel_id=1, source_target_pairs={{0,16},{1,17},{2,18},{3,19},{4,20},{5,21},{6,22},{7,23},{8,24},{9,... | collective-permute-start | bytes 110600 | tf_op jit(solution)/shard_map/filter_z/ppermute | solution.py:313
  59.2 1.3 %collective-permute-start.7 = (bf16[144,128]{1,0:T(8,128)(2,1)S(1)}, bf16[144,128]{1,0:T(8,128)(2,1)S(1)}, u32[]{:S(2)}, u32[]{:S(2)}) collective-permute-start(bf16[144,128]{1,0:T(8,128)(2,1)S(1)} %add_convert_fusion), channel_id=1, source_target_pairs={{0,8},{1,9},{2,10},{3,11},{4,12},{5,13},{6,14},{7,15},{8,16},{9,17... | collective-permute-start | bytes 110600 | tf_op jit(solution)/shard_map/filter_z/ppermute | solution.py:313
  60.5 2.8 %collective-permute-start.8 = (bf16[144,128]{1,0:T(8,128)(2,1)S(1)}, bf16[144,128]{1,0:T(8,128)(2,1)S(1)}, u32[]{:S(2)}, u32[]{:S(2)}) collective-permute-start(bf16[144,128]{1,0:T(8,128)(2,1)S(1)} %add_convert_fusion), channel_id=1, source_target_pairs={{0,24},{1,25},{2,26},{3,27},{4,28},{5,29},{6,30},{7,31},{8,0},{9,1... | collective-permute-start | bytes 110600 | tf_op jit(solution)/shard_map/filter_z/ppermute | solution.py:313
  63.3 1.2 %input_grad.3 = bf16[512,128]{1,0:T(8,128)(2,1)} custom-call(bf16[8,64,128]{2,1,0:T(8,128)(2,1)S(1)} %slice.17.dx_ref), custom_call_target="tpu_custom_call" | custom-call | flops 67108864 | bytes 2000000 | tf_op jit(solution)/shard_map/input_grad/pallas_call | solution.py:339
  64.5 0.0 collective-permute-done.6
  64.5 0.7 %collective-permute-done.7 = bf16[144,128]{1,0:T(8,128)(2,1)S(1)} collective-permute-done((bf16[144,128]{1,0:T(8,128)(2,1)S(1)}, bf16[144,128]{1,0:T(8,128)(2,1)S(1)}, u32[]{:S(2)}, u32[]{:S(2)}) %collective-permute-start.7) | collective-permute-done | bytes 36896 | tf_op jit(solution)/shard_map/filter_z/ppermute | solution.py:313
  65.2 0.6 collective-permute-done.8
  65.9 0.8 %filter_out.1 = f32[2,9,32,32]{3,2,1,0:T(8,128)} custom-call(f32[144,128]{1,0:T(8,128)S(1)} %add_add_fusion.v_ref), custom_call_target="tpu_custom_call" | custom-call | flops 1000 | bytes 2000000 | tf_op jit(solution)/shard_map/filter_out/pallas_call | solution.py:348
  (4 shorter events, 0.1 us)
Async XLA Ops:
  0.6 0.9 %copy-start = (bf16[64,8,128]{2,1,0:T(8,128)(2,1)S(1)}, bf16[64,8,128]{2,1,0:T(8,128)(2,1)}, u32[]{:S(2)}) copy-start(bf16[64,8,128]{2,1,0:T(8,128)(2,1)} %param.4) | copy-start | bytes 393220
  1.5 0.9 %copy-start.1 = (bf16[64,8,128]{2,1,0:T(8,128)(2,1)S(1)}, bf16[64,8,128]{2,1,0:T(8,128)(2,1)}, u32[]{:S(2)}) copy-start(bf16[64,8,128]{2,1,0:T(8,128)(2,1)} %param.5) | copy-start | bytes 393220
  2.7 6.0 %collective-permute-start = (bf16[2,128,128]{2,1,0:T(8,128)(2,1)S(1)}, bf16[2,128,128]{2,1,0:T(8,128)(2,1)S(1)}, u32[]{:S(2)}, u32[]{:S(2)}) collective-permute-start(bf16[2,128,128]{2,1,0:T(8,128)(2,1)S(1)} %get-tuple-element.14), channel_id=1, source_target_pairs={{1,2},{2,1},{3,4},{4,3},{5,6},{6,5},{7,8},{8,7},{9,10},{10,9},{11,... | collective-permute-start | bytes 196616 | tf_op jit(solution)/shard_map/edge_rows/ppermute | solution.py:279
  4.8 3.9 %collective-permute-start.1 = (bf16[2,128,128]{2,1,0:T(8,128)(2,1)S(1)}, bf16[2,128,128]{2,1,0:T(8,128)(2,1)S(1)}, u32[]{:S(2)}, u32[]{:S(2)}) collective-permute-start(bf16[2,128,128]{2,1,0:T(8,128)(2,1)S(1)} %get-tuple-element.15), channel_id=1, source_target_pairs={{0,1},{1,0},{2,3},{3,2},{4,5},{5,4},{6,7},{7,6},{8,9},{9,8},{10,11... | collective-permute-start | bytes 196616 | tf_op jit(solution)/shard_map/edge_rows/ppermute | solution.py:280
  9.9 15.9 %all-to-all-start = ((bf16[8,128,256]{2,1,0:T(8,128)(2,1)}), bf16[8,128,256]{2,1,0:T(8,128)(2,1)S(1)}, u32[]{:S(2)}, u32[]{:S(2)}) async-start(bf16[8,128,256]{2,1,0:T(8,128)(2,1)} %to_tiles.3), calls=%async_computation | async-start | bytes 1048576 | tf_op jit(solution)/shard_map/to_tiles/all_to_all | solution.py:292
  15.5 1.2 %slice-start = ((bf16[16,9,32,32]{3,2,1,0:T(8,128)(2,1)}), bf16[15,9,32,32]{3,2,1,0:T(8,128)(2,1)S(1)}, s32[]{:S(2)}) async-start(bf16[16,9,32,32]{3,2,1,0:T(8,128)(2,1)} %param.6), calls=%async_computation.2 | async-start | bytes 2211840 | tf_op jit(solution)/shard_map/weights/slice | solution.py:295
  15.6 1.4 %slice-start.1 = ((bf16[16,9,32,32]{3,2,1,0:T(8,128)(2,1)}), bf16[1,9,32,32]{3,2,1,0:T(8,128)(2,1)S(1)}, s32[]{:S(2)}) async-start(bf16[16,9,32,32]{3,2,1,0:T(8,128)(2,1)} %param.6), calls=%async_computation.3 | async-start | bytes 147456 | tf_op jit(solution)/shard_map/weights/slice | solution.py:295
  18.2 1.3 %copy-start.2 = (bf16[16,9,32,32]{3,2,1,0:T(8,128)(2,1)S(1)}, bf16[16,9,32,32]{3,2,1,0:T(8,128)(2,1)}, u32[]{:S(2)}) copy-start(bf16[16,9,32,32]{3,2,1,0:T(8,128)(2,1)} %param.6) | copy-start | bytes 884740
  19.9 5.9 %copy-start.3 = (f32[32]{0:T(128)S(1)}, f32[32]{0:T(128)}, u32[]{:S(2)}) copy-start(f32[32]{0:T(128)} %param.7) | copy-start | bytes 388
  29.6 2.9 %collective-permute-start.2 = (f32[8,144,128]{2,1,0:T(8,128)S(1)}, f32[8,144,128]{2,1,0:T(8,128)S(1)}, u32[]{:S(2)}, u32[]{:S(2)}) collective-permute-start(f32[8,144,128]{2,1,0:T(8,128)S(1)} %get-tuple-element.19.part_ref), channel_id=1, source_target_pairs={{0,1},{1,0},{2,3},{3,2},{4,5},{5,4},{6,7},{7,6},{8,9},{9,8},{10,11... | collective-permute-start | bytes 1769480 | tf_op jit(solution)/shard_map/filter_core/ppermute | solution.py:321
  44.8 5.7 %collective-permute-start.3 = (bf16[144,128]{1,0:T(8,128)(2,1)S(1)}, bf16[144,128]{1,0:T(8,128)(2,1)S(1)}, u32[]{:S(2)}, u32[]{:S(2)}) collective-permute-start(bf16[144,128]{1,0:T(8,128)(2,1)S(1)} %slice_reduce_fusion), channel_id=1, source_target_pairs={{0,4},{1,5},{2,6},{3,7},{4,0},{5,1},{6,2},{7,3},{8,12},{9,13},{10,... | collective-permute-start | bytes 110600 | tf_op jit(solution)/shard_map/filter_y/ppermute | solution.py:313
  45.3 5.3 %collective-permute-start.4 = (bf16[144,128]{1,0:T(8,128)(2,1)S(1)}, bf16[144,128]{1,0:T(8,128)(2,1)S(1)}, u32[]{:S(2)}, u32[]{:S(2)}) collective-permute-start(bf16[144,128]{1,0:T(8,128)(2,1)S(1)} %slice_reduce_fusion), channel_id=1, source_target_pairs={{0,2},{1,3},{2,4},{3,5},{4,6},{5,7},{6,0},{7,1},{8,10},{9,11},{10,... | collective-permute-start | bytes 110600 | tf_op jit(solution)/shard_map/filter_y/ppermute | solution.py:313
  47.4 5.2 %collective-permute-start.5 = (bf16[144,128]{1,0:T(8,128)(2,1)S(1)}, bf16[144,128]{1,0:T(8,128)(2,1)S(1)}, u32[]{:S(2)}, u32[]{:S(2)}) collective-permute-start(bf16[144,128]{1,0:T(8,128)(2,1)S(1)} %slice_reduce_fusion), channel_id=1, source_target_pairs={{0,6},{1,7},{2,0},{3,1},{4,2},{5,3},{6,4},{7,5},{8,14},{9,15},{10,... | collective-permute-start | bytes 110600 | tf_op jit(solution)/shard_map/filter_y/ppermute | solution.py:313
  52.6 11.9 %collective-permute-start.6 = (bf16[144,128]{1,0:T(8,128)(2,1)S(1)}, bf16[144,128]{1,0:T(8,128)(2,1)S(1)}, u32[]{:S(2)}, u32[]{:S(2)}) collective-permute-start(bf16[144,128]{1,0:T(8,128)(2,1)S(1)} %add_convert_fusion), channel_id=1, source_target_pairs={{0,16},{1,17},{2,18},{3,19},{4,20},{5,21},{6,22},{7,23},{8,24},{9,... | collective-permute-start | bytes 110600 | tf_op jit(solution)/shard_map/filter_z/ppermute | solution.py:313
  59.2 6.1 %collective-permute-start.7 = (bf16[144,128]{1,0:T(8,128)(2,1)S(1)}, bf16[144,128]{1,0:T(8,128)(2,1)S(1)}, u32[]{:S(2)}, u32[]{:S(2)}) collective-permute-start(bf16[144,128]{1,0:T(8,128)(2,1)S(1)} %add_convert_fusion), channel_id=1, source_target_pairs={{0,8},{1,9},{2,10},{3,11},{4,12},{5,13},{6,14},{7,15},{8,16},{9,17... | collective-permute-start | bytes 110600 | tf_op jit(solution)/shard_map/filter_z/ppermute | solution.py:313
  60.5 5.4 %collective-permute-start.8 = (bf16[144,128]{1,0:T(8,128)(2,1)S(1)}, bf16[144,128]{1,0:T(8,128)(2,1)S(1)}, u32[]{:S(2)}, u32[]{:S(2)}) collective-permute-start(bf16[144,128]{1,0:T(8,128)(2,1)S(1)} %add_convert_fusion), channel_id=1, source_target_pairs={{0,24},{1,25},{2,26},{3,27},{4,28},{5,29},{6,30},{7,31},{8,0},{9,1... | collective-permute-start | bytes 110600 | tf_op jit(solution)/shard_map/filter_z/ppermute | solution.py:313
